TPU v7x, 32 devices: a whole 2x2x4 slice. The times are simulated.
32 devices in a mesh: ctx: 8 (over z, y), fsdp: 4 (over x, core).
Axes of the slice: x: 2, y: 2, z: 4, core: 2. Of those that a mesh axis runs over, the one named last changes fastest.
Arguments:
- tokens: float32 [8, 2048, 768], P('fsdp', 'ctx'), may hold values from -6 to 6
- lengths: int32 [8], P('fsdp'), may hold values from 1 to 2048, as said below
- attend_weight: bfloat16 [768, 2304], P('fsdp'), may hold values from -0.21875 to 0.21875
- query_bias: bfloat16 [768], P('fsdp'), may hold values from -3 to 3
- value_bias: bfloat16 [768], P('fsdp'), may hold values from -3 to 3
- mixing_weight: bfloat16 [768, 768], P('fsdp'), may hold values from -6 to 6
- mixing_bias: bfloat16 [768], P('fsdp'), may hold values from -3 to 3
- first_gain: bfloat16 [768], P('fsdp'), may hold values from 0.25 to 1.75
- first_shift: bfloat16 [768], P('fsdp'), may hold values from -3 to 3
- up_weight: bfloat16 [768, 3072], P('fsdp'), may hold values from -0.21875 to 0.21875
- up_bias: bfloat16 [3072], P('fsdp'), may hold values from -3 to 3
- down_weight: bfloat16 [3072, 768], P('fsdp'), may hold values from -0.109375 to 0.109375
- down_bias: bfloat16 [768], P('fsdp'), may hold values from -3 to 3
- second_gain: bfloat16 [768], P('fsdp'), may hold values from 0.25 to 1.75
- second_shift: bfloat16 [768], P('fsdp'), may hold values from -3 to 3
- cotangent: float32 [8, 2048, 768], P('fsdp', 'ctx'), may hold values from -6 to 6
Outputs:
- result: float32 [8, 2048, 768], P('fsdp', 'ctx')
- tokens_grad: float32 [8, 2048, 768], P('fsdp', 'ctx')
- attend_grad: float32 [768, 2304], P('fsdp')
- querybias_grad: float32 [768], P('fsdp')
- valuebias_grad: float32 [768], P('fsdp')
- mixing_grad: float32 [768, 768], P('fsdp')
- mixingbias_grad: float32 [768], P('fsdp')
- firstgain_grad: float32 [768], P('fsdp')
- firstshift_grad: float32 [768], P('fsdp')
- upweight_grad: float32 [768, 3072], P('fsdp')
- upbias_grad: float32 [3072], P('fsdp')
- downweight_grad: float32 [3072, 768], P('fsdp')
- downbias_grad: float32 [768], P('fsdp')
- secondgain_grad: float32 [768], P('fsdp')
- secondshift_grad: float32 [768], P('fsdp')
Inputs may be any that keep to these rules, and one draw needn't show every extreme that they name: `lengths`: each entry counts the real tokens of a sequence; positions at or past it are padding. Among the 2 sequences held by each index of fsdp, one chosen by the seed has exactly 2048.
All inputs are finite; a program needn't handle non-finite values.
Results may differ from a plain program's by a relative error of at most 0.022.
Values may be sent and summed in bfloat16 or wider, within the bound.
No kernel may reach another device: no remote copies, remote signals or barrier semaphores. Data moves between devices by JAX's collectives and lax.ppermute only.
A program may use at most 128 MiB of HBM per device.

v0:
```python
import math

import jax
import jax.numpy as jnp
from jax import lax
from jax.sharding import PartitionSpec as P

HEAD_DIM = 64


LN_TWO = math.log(2.0)
EPS = 1e-12
SCALE = 0.125
MASKED = -1e30
FLOOR_LEVEL = -30000.0


def shifted(value, axis, steps):
    count = lax.axis_size(axis)
    pairs = [(source, (source + steps) % count) for source in range(count)]
    return lax.ppermute(value, axis, pairs)


def layer_norm(value, gain, shift):
    mean = jnp.mean(value, axis=-1, keepdims=True)
    centred = value - mean
    spread = jnp.mean(centred * centred, axis=-1, keepdims=True)
    return centred * lax.rsqrt(spread + EPS) * gain + shift


def gelu_exact(value):
    return jax.nn.gelu(value, approximate=False)


def block_scores(query4, keys3, start, lengths):
    seqs, count, width = keys3.shape
    heads = query4.shape[2]
    keys4 = keys3.reshape(seqs, count, heads, HEAD_DIM)
    raw = jnp.einsum("sqhd,skhd->shqk", query4, keys4, preferred_element_type=jnp.float32) * SCALE
    spots = start + lax.iota(jnp.int32, count)
    live = spots[None, :] < lengths[:, None]
    return jnp.where(live[:, None, None, :], raw, MASKED)


def pair_terms(query4, dnumer, level, corr, keys3, values3, start, lengths):
    seqs, block, width = keys3.shape
    heads = query4.shape[2]
    scores = block_scores(query4, keys3, start, lengths)
    weights = jnp.exp(scores - (level * LN_TWO)[..., None])
    keys4 = keys3.reshape(seqs, block, heads, HEAD_DIM)
    values4 = values3.reshape(seqs, block, heads, HEAD_DIM)
    dprob = jnp.einsum("sqhd,skhd->shqk", dnumer, values4, preferred_element_type=jnp.float32)
    dscores = (weights * (dprob - corr[..., None])).astype(jnp.bfloat16)
    query_term = (
        jnp.einsum("shqk,skhd->sqhd", dscores, keys4, preferred_element_type=jnp.float32) * SCALE
    )
    key_term = (
        jnp.einsum("shqk,sqhd->skhd", dscores, query4, preferred_element_type=jnp.float32) * SCALE
    ).reshape(seqs, block, width)
    value_term = jnp.einsum(
        "shqk,sqhd->skhd", weights.astype(jnp.bfloat16), dnumer, preferred_element_type=jnp.float32
    ).reshape(seqs, block, width)
    return (query_term, key_term, value_term)


def per_device(
    tokens,
    lengths,
    attend_weight,
    query_bias,
    value_bias,
    mixing_weight,
    mixing_bias,
    first_gain,
    first_shift,
    up_weight,
    up_bias,
    down_weight,
    down_bias,
    second_gain,
    second_shift,
    cotangent,
):
    seqs, block, width = tokens.shape
    heads = width // HEAD_DIM
    rows = seqs * block
    cycle = lax.axis_size("ctx")
    place = lax.axis_index("ctx")
    f32 = jnp.float32
    b16 = jnp.bfloat16
    attend_full, qbias_full, vbias_full, mixing_full, mixbias_full = (
        lax.all_gather(attend_weight, "fsdp", axis=0, tiled=True),
        lax.all_gather(query_bias, "fsdp", axis=0, tiled=True),
        lax.all_gather(value_bias, "fsdp", axis=0, tiled=True),
        lax.all_gather(mixing_weight, "fsdp", axis=0, tiled=True),
        lax.all_gather(mixing_bias, "fsdp", axis=0, tiled=True),
    )
    up_full, upbias_full, down_full, downbias_full, fgain, fshift, sgain, sshift = (
        lax.all_gather(up_weight, "fsdp", axis=0, tiled=True),
        lax.all_gather(up_bias, "fsdp", axis=0, tiled=True),
        lax.all_gather(down_weight, "fsdp", axis=0, tiled=True),
        lax.all_gather(down_bias, "fsdp", axis=0, tiled=True),
        lax.all_gather(first_gain, "fsdp", axis=0, tiled=True),
        lax.all_gather(first_shift, "fsdp", axis=0, tiled=True),
        lax.all_gather(second_gain, "fsdp", axis=0, tiled=True),
        lax.all_gather(second_shift, "fsdp", axis=0, tiled=True),
    )
    fgain = fgain.astype(f32)
    fshift = fshift.astype(f32)
    sgain = sgain.astype(f32)
    sshift = sshift.astype(f32)
    flat = tokens.reshape(rows, width)
    flat_low = flat.astype(b16)
    projected = jnp.dot(flat_low, attend_full, preferred_element_type=f32)
    query = (projected[:, :width] + qbias_full.astype(f32)).astype(b16)
    keys = projected[:, width : 2 * width].astype(b16)
    values = (projected[:, 2 * width :] + vbias_full.astype(f32)).astype(b16)
    query4 = query.reshape(seqs, block, heads, HEAD_DIM)
    keys3 = keys.reshape(seqs, block, width)
    values3 = values.reshape(seqs, block, width)
    start_state = (
        jnp.full((seqs, heads, block), FLOOR_LEVEL, f32),
        jnp.zeros((seqs, heads, block), f32),
        jnp.zeros((seqs, block, heads, HEAD_DIM), f32),
    )
    carry = start_state
    piece_keys = lax.all_gather(keys3, "ctx", axis=1, tiled=True)
    piece_values = lax.all_gather(values3, "ctx", axis=1, tiled=True)
    count = piece_keys.shape[1]
    size = math.gcd(count, 512)

    def one_step(state, offset):
        level, total, accum = state
        key_part = lax.dynamic_slice_in_dim(piece_keys, offset, size, 1)
        value_part = lax.dynamic_slice_in_dim(piece_values, offset, size, 1)
        scores = block_scores(query4, key_part, offset, lengths)
        top = jnp.ceil(jnp.max(scores, axis=-1) / LN_TWO)
        new_level = jnp.maximum(level, top)
        factor = jnp.exp2(level - new_level)
        weights = jnp.exp(scores - (new_level * LN_TWO)[..., None])
        total = total * factor + jnp.sum(weights, axis=-1)
        value4 = value_part.reshape(seqs, size, heads, HEAD_DIM)
        update = jnp.einsum(
            "shqk,skhd->sqhd", weights.astype(b16), value4, preferred_element_type=f32
        )
        accum = accum * jnp.transpose(factor, (0, 2, 1))[..., None] + update
        return ((new_level, total, accum), None)

    offsets = jnp.arange(count // size, dtype=jnp.int32) * size
    carry, _ = lax.scan(one_step, carry, offsets)
    level, total, accum = carry
    total_t = jnp.transpose(total, (0, 2, 1))
    attended4 = accum / total_t[..., None]
    attended = attended4.reshape(rows, width)
    attended_low = attended.astype(b16)
    mixed = jnp.dot(attended_low, mixing_full, preferred_element_type=f32) + mixbias_full.astype(
        f32
    )
    hidden = flat + mixed
    first = layer_norm(hidden, fgain, fshift)
    first_low = first.astype(b16)
    pre = jnp.dot(first_low, up_full, preferred_element_type=f32) + upbias_full.astype(f32)
    act = gelu_exact(pre)
    act_low = act.astype(b16)
    branch = jnp.dot(act_low, down_full, preferred_element_type=f32) + downbias_full.astype(f32)
    summed = first + branch
    result = layer_norm(summed, sgain, sshift)
    grad_out = cotangent.reshape(rows, width)
    _, second_back = jax.vjp(layer_norm, summed, sgain, sshift)
    dsummed, grad_sgain, grad_sshift = second_back(grad_out)
    dbranch = dsummed.astype(b16)
    grad_down = jnp.einsum("rf,rd->fd", act_low, dbranch, preferred_element_type=f32)
    grad_downbias = jnp.sum(dbranch.astype(f32), axis=0)
    dact = jnp.einsum("rd,fd->rf", dbranch, down_full, preferred_element_type=f32)
    _, gelu_back = jax.vjp(gelu_exact, pre)
    dpre = gelu_back(dact)[0].astype(b16)
    grad_up = jnp.einsum("rd,rf->df", first_low, dpre, preferred_element_type=f32)
    grad_upbias = jnp.sum(dpre.astype(f32), axis=0)
    dfirst = dsummed + jnp.einsum("rf,df->rd", dpre, up_full, preferred_element_type=f32)
    _, first_back = jax.vjp(layer_norm, hidden, fgain, fshift)
    dhidden, grad_fgain, grad_fshift = first_back(dfirst)
    dmixed = dhidden.astype(b16)
    grad_mixing = jnp.einsum("rd,re->de", attended_low, dmixed, preferred_element_type=f32)
    grad_mixbias = jnp.sum(dmixed.astype(f32), axis=0)
    dattended = jnp.einsum("re,de->rd", dmixed, mixing_full, preferred_element_type=f32)
    dattended4 = dattended.reshape(seqs, block, heads, HEAD_DIM)
    dnumer = (dattended4 / total_t[..., None]).astype(b16)
    corr = jnp.transpose(jnp.sum(dattended4 * attended4, axis=-1) / total_t, (0, 2, 1))
    empty_kv = jnp.zeros((seqs, block, width), f32)
    empty_q = jnp.zeros((seqs, block, heads, HEAD_DIM), f32)

    def cycle_step(step, state):
        held_keys, held_values, dkeys, dvalues, dquery = state
        source = (place - step) % cycle
        query_term, key_term, value_term = pair_terms(
            query4, dnumer, level, corr, held_keys, held_values, source * block, lengths
        )
        dquery = dquery + query_term
        dkeys = dkeys + key_term
        dvalues = dvalues + value_term
        held_keys, held_values = shifted((held_keys, held_values), "ctx", 1)
        dkeys, dvalues = (
            shifted(dkeys.astype(jnp.bfloat16), "ctx", 1).astype(dkeys.dtype),
            shifted(dvalues.astype(jnp.bfloat16), "ctx", 1).astype(dvalues.dtype),
        )
        return (held_keys, held_values, dkeys, dvalues, dquery)

    cycle_start = (keys3, values3, empty_kv, empty_kv, empty_q)
    _, _, dkeys, dvalues, dquery = lax.fori_loop(0, cycle, cycle_step, cycle_start)
    dprojected = jnp.concatenate(
        [dquery.reshape(rows, width), dkeys.reshape(rows, width), dvalues.reshape(rows, width)],
        axis=1,
    ).astype(b16)
    grad_attend = jnp.einsum("rd,re->de", flat_low, dprojected, preferred_element_type=f32)
    grad_qbias = jnp.sum(dprojected[:, :width].astype(f32), axis=0)
    grad_vbias = jnp.sum(dprojected[:, 2 * width :].astype(f32), axis=0)
    tokens_grad = dhidden + jnp.einsum(
        "re,de->rd", dprojected, attend_full, preferred_element_type=f32
    )
    terms = (
        grad_attend,
        grad_qbias,
        grad_vbias,
        grad_mixing,
        grad_mixbias,
        grad_fgain,
        grad_fshift,
        grad_up,
        grad_upbias,
        grad_down,
        grad_downbias,
        grad_sgain,
        grad_sshift,
    )
    owned = (
        lax.psum_scatter(
            terms[0].astype(jnp.bfloat16), "fsdp", scatter_dimension=0, tiled=True
        ).astype(jnp.float32),
        lax.psum_scatter(
            terms[1].astype(jnp.bfloat16), "fsdp", scatter_dimension=0, tiled=True
        ).astype(jnp.float32),
        lax.psum_scatter(
            terms[2].astype(jnp.bfloat16), "fsdp", scatter_dimension=0, tiled=True
        ).astype(jnp.float32),
        lax.psum_scatter(
            terms[3].astype(jnp.bfloat16), "fsdp", scatter_dimension=0, tiled=True
        ).astype(jnp.float32),
        lax.psum_scatter(
            terms[4].astype(jnp.bfloat16), "fsdp", scatter_dimension=0, tiled=True
        ).astype(jnp.float32),
        lax.psum_scatter(
            terms[5].astype(jnp.bfloat16), "fsdp", scatter_dimension=0, tiled=True
        ).astype(jnp.float32),
        lax.psum_scatter(
            terms[6].astype(jnp.bfloat16), "fsdp", scatter_dimension=0, tiled=True
        ).astype(jnp.float32),
        lax.psum_scatter(
            terms[7].astype(jnp.bfloat16), "fsdp", scatter_dimension=0, tiled=True
        ).astype(jnp.float32),
        lax.psum_scatter(
            terms[8].astype(jnp.bfloat16), "fsdp", scatter_dimension=0, tiled=True
        ).astype(jnp.float32),
        lax.psum_scatter(
            terms[9].astype(jnp.bfloat16), "fsdp", scatter_dimension=0, tiled=True
        ).astype(jnp.float32),
        lax.psum_scatter(
            terms[10].astype(jnp.bfloat16), "fsdp", scatter_dimension=0, tiled=True
        ).astype(jnp.float32),
        lax.psum_scatter(
            terms[11].astype(jnp.bfloat16), "fsdp", scatter_dimension=0, tiled=True
        ).astype(jnp.float32),
        lax.psum_scatter(
            terms[12].astype(jnp.bfloat16), "fsdp", scatter_dimension=0, tiled=True
        ).astype(jnp.float32),
    )
    owned = (
        lax.psum(owned[0].astype(jnp.bfloat16), "ctx").astype(jnp.float32),
        lax.psum(owned[1].astype(jnp.bfloat16), "ctx").astype(jnp.float32),
        lax.psum(owned[2].astype(jnp.bfloat16), "ctx").astype(jnp.float32),
        lax.psum(owned[3].astype(jnp.bfloat16), "ctx").astype(jnp.float32),
        lax.psum(owned[4].astype(jnp.bfloat16), "ctx").astype(jnp.float32),
        lax.psum(owned[5].astype(jnp.bfloat16), "ctx").astype(jnp.float32),
        lax.psum(owned[6].astype(jnp.bfloat16), "ctx").astype(jnp.float32),
        lax.psum(owned[7].astype(jnp.bfloat16), "ctx").astype(jnp.float32),
        lax.psum(owned[8].astype(jnp.bfloat16), "ctx").astype(jnp.float32),
        lax.psum(owned[9].astype(jnp.bfloat16), "ctx").astype(jnp.float32),
        lax.psum(owned[10].astype(jnp.bfloat16), "ctx").astype(jnp.float32),
        lax.psum(owned[11].astype(jnp.bfloat16), "ctx").astype(jnp.float32),
        lax.psum(owned[12].astype(jnp.bfloat16), "ctx").astype(jnp.float32),
    )
    return (
        result.reshape(seqs, block, width),
        tokens_grad.reshape(seqs, block, width),
        owned[0],
        owned[1],
        owned[2],
        owned[3],
        owned[4],
        owned[5],
        owned[6],
        owned[7],
        owned[8],
        owned[9],
        owned[10],
        owned[11],
        owned[12],
    )


def solution(mesh):
    return jax.shard_map(
        per_device,
        mesh=mesh,
        in_specs=(
            P("fsdp", "ctx", None),
            P("fsdp"),
            P("fsdp", None),
            P("fsdp"),
            P("fsdp"),
            P("fsdp", None),
            P("fsdp"),
            P("fsdp"),
            P("fsdp"),
            P("fsdp", None),
            P("fsdp"),
            P("fsdp", None),
            P("fsdp"),
            P("fsdp"),
            P("fsdp"),
            P("fsdp", "ctx", None),
        ),
        out_specs=(
            P("fsdp", "ctx", None),
            P("fsdp", "ctx", None),
            P("fsdp", None),
            P("fsdp"),
            P("fsdp"),
            P("fsdp", None),
            P("fsdp"),
            P("fsdp"),
            P("fsdp"),
            P("fsdp", None),
            P("fsdp"),
            P("fsdp", None),
            P("fsdp"),
            P("fsdp"),
            P("fsdp"),
        ),
        check_vma=False,
    )
```

profile of v0, /device:TPU:0, one launch (start us, length us, event | category | flops | bytes accessed | tf_op | source)
XLA Modules:
  0.0 1436.7 jit_solution(6300764722296071180)
XLA Ops:
  15.8 13.4 all-reduce.20
  30.7 12.6 all-gather.8.cloned.1.call-done
  61.6 89.5 %all-gather.12.cloned.1.call-done = bf16[2,2048,768]{1,2,0:T(8,128)(2,1)} async-done(((bf16[2,256,768]{1,2,0:T(8,128)(2,1)}), bf16[2,2048,768]{1,2,0:T(8,128)(2,1)}) %all-gather.12.cloned.1.call-update) | async-done | bytes 6291472 | tf_op jit(solution)/shard_map/all_gather | solution.py:128
  151.1 100.2 %all-gather.10.cloned.1.call-done = bf16[2,2048,768]{1,2,0:T(8,128)(2,1)} async-done(((bf16[2,256,768]{1,2,0:T(8,128)(2,1)}), bf16[2,2048,768]{1,2,0:T(8,128)(2,1)}) %all-gather.10.cloned.1.call-update) | async-done | bytes 6291472 | tf_op jit(solution)/shard_map/all_gather | solution.py:127
  251.3 103.2 %while.39 = (s32[]{:T(128)}, f32[2,12,256]{2,1,0:T(8,128)S(1)}, f32[2,12,256]{2,1,0:T(8,128)S(1)}, f32[2,256,12,64]{1,3,2,0:T(8,128)}, s32[4]{0:T(128)S(1)}, /*i...) while((s32[]{:T(128)}, f32[2,12,256]{2,1,0:T(8,128)S(1)}, ...), condition=%wide.region_3.4_spmd.clone, body=%wide.region_0.3_spmd.clone.sunk | while | flops 841158144 | bytes 101900504 | solution.py:150
  315.6 9.1 bitcast_add_fusion.7
  363.0 19.9 %multiply_convert_fusion.1 = (bf16[512,3072]{1,0:T(8,128)(2,1)}, f32[512,3072]{1,0:T(8,128)}, f32[512,3072]{1,0:T(8,128)}) fusion(f32[3072]{0:T(1024)S(1)} %bitcast.173, bf16[768,3072]{1,0:T(8,128)(2,1)} %all-gather.16.cloned.1.call-done, f32[512,768]{1,0:T(8,128)S(1)} %get-tuple-element.642, f32[768]{0:T(1024)S(1)} %convert_element_type.236, ...), kind=kOutput, calls=%fused_computation.44 | convolution fusion | flops 2521694208 | bytes 22042624 | tf_op jit(solution)/shard_map/dot_general | solution.py:162
  392.7 8.4 fusion.42
  416.9 666.1 %while.40 = (s32[]{:T(128)}, bf16[2,256,768]{1,2,0:T(8,128)(2,1)}, bf16[2,256,768]{1,2,0:T(8,128)(2,1)}, f32[2,256,768]{1,2,0:T(8,128)}, f32[2,256,768]{1,2,0:T(...) while((s32[]{:T(128)}, bf16[2,256,768]{1,2,0:T(8,128)(2,1)}, ...), condition=%wide.region_14.15_spmd.clone, body=%wide.region_13.14_spmd.clone.sunk | while | flops 1027087104 | bytes 90566744 | solution.py:209
  442.0 11.7 collective-permute-done.2
  456.0 14.5 %collective-permute-done.3 = bf16[2,256,768]{1,2,0:T(8,128)(2,1)} collective-permute-done((bf16[2,256,768]{1,2,0:T(8,128)(2,1)}, bf16[2,256,768]{1,2,0:T(8,128)(2,1)}, u32[]{:S(2)}, u32[]{:S(2)}) %collective-permute-start.3) | collective-permute-done | bytes 786464 | tf_op jit(solution)/shard_map/while/body/eval_jaxpr/ppermute | solution.py:21
  472.9 14.5 %collective-permute-done = bf16[2,256,768]{1,2,0:T(8,128)(2,1)} collective-permute-done((bf16[2,256,768]{1,2,0:T(8,128)(2,1)}, bf16[2,256,768]{1,2,0:T(8,128)(2,1)}, u32[]{:S(2)}, u32[]{:S(2)}) %collective-permute-start) | collective-permute-done | bytes 786464 | tf_op jit(solution)/shard_map/while/body/eval_jaxpr/ppermute | solution.py:21
  487.4 15.9 %collective-permute-done.1 = bf16[2,256,768]{1,2,0:T(8,128)(2,1)} collective-permute-done((bf16[2,256,768]{1,2,0:T(8,128)(2,1)}, bf16[2,256,768]{1,2,0:T(8,128)(2,1)}, u32[]{:S(2)}, u32[]{:S(2)}) %collective-permute-start.1) | collective-permute-done | bytes 786464 | tf_op jit(solution)/shard_map/while/body/eval_jaxpr/ppermute | solution.py:21
  526.3 13.8 collective-permute-done.2
  542.5 14.5 %collective-permute-done.3 = bf16[2,256,768]{1,2,0:T(8,128)(2,1)} collective-permute-done((bf16[2,256,768]{1,2,0:T(8,128)(2,1)}, bf16[2,256,768]{1,2,0:T(8,128)(2,1)}, u32[]{:S(2)}, u32[]{:S(2)}) %collective-permute-start.3) | collective-permute-done | bytes 786464 | tf_op jit(solution)/shard_map/while/body/eval_jaxpr/ppermute | solution.py:21
  559.4 14.5 %collective-permute-done = bf16[2,256,768]{1,2,0:T(8,128)(2,1)} collective-permute-done((bf16[2,256,768]{1,2,0:T(8,128)(2,1)}, bf16[2,256,768]{1,2,0:T(8,128)(2,1)}, u32[]{:S(2)}, u32[]{:S(2)}) %collective-permute-start) | collective-permute-done | bytes 786464 | tf_op jit(solution)/shard_map/while/body/eval_jaxpr/ppermute | solution.py:21
  573.8 15.0 %collective-permute-done.1 = bf16[2,256,768]{1,2,0:T(8,128)(2,1)} collective-permute-done((bf16[2,256,768]{1,2,0:T(8,128)(2,1)}, bf16[2,256,768]{1,2,0:T(8,128)(2,1)}, u32[]{:S(2)}, u32[]{:S(2)}) %collective-permute-start.1) | collective-permute-done | bytes 786464 | tf_op jit(solution)/shard_map/while/body/eval_jaxpr/ppermute | solution.py:21
  609.3 16.4 %collective-permute-done.2 = bf16[2,256,768]{1,2,0:T(8,128)(2,1)} collective-permute-done((bf16[2,256,768]{1,2,0:T(8,128)(2,1)}, bf16[2,256,768]{1,2,0:T(8,128)(2,1)}, u32[]{:S(2)}, u32[]{:S(2)}) %collective-permute-start.2) | collective-permute-done | bytes 786464 | tf_op jit(solution)/shard_map/while/body/eval_jaxpr/ppermute | solution.py:21
  628.1 14.5 %collective-permute-done.3 = bf16[2,256,768]{1,2,0:T(8,128)(2,1)} collective-permute-done((bf16[2,256,768]{1,2,0:T(8,128)(2,1)}, bf16[2,256,768]{1,2,0:T(8,128)(2,1)}, u32[]{:S(2)}, u32[]{:S(2)}) %collective-permute-start.3) | collective-permute-done | bytes 786464 | tf_op jit(solution)/shard_map/while/body/eval_jaxpr/ppermute | solution.py:21
  644.9 14.5 %collective-permute-done = bf16[2,256,768]{1,2,0:T(8,128)(2,1)} collective-permute-done((bf16[2,256,768]{1,2,0:T(8,128)(2,1)}, bf16[2,256,768]{1,2,0:T(8,128)(2,1)}, u32[]{:S(2)}, u32[]{:S(2)}) %collective-permute-start) | collective-permute-done | bytes 786464 | tf_op jit(solution)/shard_map/while/body/eval_jaxpr/ppermute | solution.py:21
  659.4 14.1 collective-permute-done.1
  693.4 16.9 %collective-permute-done.2 = bf16[2,256,768]{1,2,0:T(8,128)(2,1)} collective-permute-done((bf16[2,256,768]{1,2,0:T(8,128)(2,1)}, bf16[2,256,768]{1,2,0:T(8,128)(2,1)}, u32[]{:S(2)}, u32[]{:S(2)}) %collective-permute-start.2) | collective-permute-done | bytes 786464 | tf_op jit(solution)/shard_map/while/body/eval_jaxpr/ppermute | solution.py:21
  712.7 14.5 %collective-permute-done.3 = bf16[2,256,768]{1,2,0:T(8,128)(2,1)} collective-permute-done((bf16[2,256,768]{1,2,0:T(8,128)(2,1)}, bf16[2,256,768]{1,2,0:T(8,128)(2,1)}, u32[]{:S(2)}, u32[]{:S(2)}) %collective-permute-start.3) | collective-permute-done | bytes 786464 | tf_op jit(solution)/shard_map/while/body/eval_jaxpr/ppermute | solution.py:21
  729.6 14.5 %collective-permute-done = bf16[2,256,768]{1,2,0:T(8,128)(2,1)} collective-permute-done((bf16[2,256,768]{1,2,0:T(8,128)(2,1)}, bf16[2,256,768]{1,2,0:T(8,128)(2,1)}, u32[]{:S(2)}, u32[]{:S(2)}) %collective-permute-start) | collective-permute-done | bytes 786464 | tf_op jit(solution)/shard_map/while/body/eval_jaxpr/ppermute | solution.py:21
  744.0 13.1 collective-permute-done.1
  777.1 16.9 %collective-permute-done.2 = bf16[2,256,768]{1,2,0:T(8,128)(2,1)} collective-permute-done((bf16[2,256,768]{1,2,0:T(8,128)(2,1)}, bf16[2,256,768]{1,2,0:T(8,128)(2,1)}, u32[]{:S(2)}, u32[]{:S(2)}) %collective-permute-start.2) | collective-permute-done | bytes 786464 | tf_op jit(solution)/shard_map/while/body/eval_jaxpr/ppermute | solution.py:21
  796.4 14.5 %collective-permute-done.3 = bf16[2,256,768]{1,2,0:T(8,128)(2,1)} collective-permute-done((bf16[2,256,768]{1,2,0:T(8,128)(2,1)}, bf16[2,256,768]{1,2,0:T(8,128)(2,1)}, u32[]{:S(2)}, u32[]{:S(2)}) %collective-permute-start.3) | collective-permute-done | bytes 786464 | tf_op jit(solution)/shard_map/while/body/eval_jaxpr/ppermute | solution.py:21
  813.3 14.5 %collective-permute-done = bf16[2,256,768]{1,2,0:T(8,128)(2,1)} collective-permute-done((bf16[2,256,768]{1,2,0:T(8,128)(2,1)}, bf16[2,256,768]{1,2,0:T(8,128)(2,1)}, u32[]{:S(2)}, u32[]{:S(2)}) %collective-permute-start) | collective-permute-done | bytes 786464 | tf_op jit(solution)/shard_map/while/body/eval_jaxpr/ppermute | solution.py:21
  827.8 12.2 collective-permute-done.1
  859.9 16.9 %collective-permute-done.2 = bf16[2,256,768]{1,2,0:T(8,128)(2,1)} collective-permute-done((bf16[2,256,768]{1,2,0:T(8,128)(2,1)}, bf16[2,256,768]{1,2,0:T(8,128)(2,1)}, u32[]{:S(2)}, u32[]{:S(2)}) %collective-permute-start.2) | collective-permute-done | bytes 786464 | tf_op jit(solution)/shard_map/while/body/eval_jaxpr/ppermute | solution.py:21
  879.2 14.5 %collective-permute-done.3 = bf16[2,256,768]{1,2,0:T(8,128)(2,1)} collective-permute-done((bf16[2,256,768]{1,2,0:T(8,128)(2,1)}, bf16[2,256,768]{1,2,0:T(8,128)(2,1)}, u32[]{:S(2)}, u32[]{:S(2)}) %collective-permute-start.3) | collective-permute-done | bytes 786464 | tf_op jit(solution)/shard_map/while/body/eval_jaxpr/ppermute | solution.py:21
  896.1 14.5 %collective-permute-done = bf16[2,256,768]{1,2,0:T(8,128)(2,1)} collective-permute-done((bf16[2,256,768]{1,2,0:T(8,128)(2,1)}, bf16[2,256,768]{1,2,0:T(8,128)(2,1)}, u32[]{:S(2)}, u32[]{:S(2)}) %collective-permute-start) | collective-permute-done | bytes 786464 | tf_op jit(solution)/shard_map/while/body/eval_jaxpr/ppermute | solution.py:21
  910.5 11.3 collective-permute-done.1
  941.8 16.9 %collective-permute-done.2 = bf16[2,256,768]{1,2,0:T(8,128)(2,1)} collective-permute-done((bf16[2,256,768]{1,2,0:T(8,128)(2,1)}, bf16[2,256,768]{1,2,0:T(8,128)(2,1)}, u32[]{:S(2)}, u32[]{:S(2)}) %collective-permute-start.2) | collective-permute-done | bytes 786464 | tf_op jit(solution)/shard_map/while/body/eval_jaxpr/ppermute | solution.py:21
  961.1 14.5 %collective-permute-done.3 = bf16[2,256,768]{1,2,0:T(8,128)(2,1)} collective-permute-done((bf16[2,256,768]{1,2,0:T(8,128)(2,1)}, bf16[2,256,768]{1,2,0:T(8,128)(2,1)}, u32[]{:S(2)}, u32[]{:S(2)}) %collective-permute-start.3) | collective-permute-done | bytes 786464 | tf_op jit(solution)/shard_map/while/body/eval_jaxpr/ppermute | solution.py:21
  978.0 14.5 %collective-permute-done = bf16[2,256,768]{1,2,0:T(8,128)(2,1)} collective-permute-done((bf16[2,256,768]{1,2,0:T(8,128)(2,1)}, bf16[2,256,768]{1,2,0:T(8,128)(2,1)}, u32[]{:S(2)}, u32[]{:S(2)}) %collective-permute-start) | collective-permute-done | bytes 786464 | tf_op jit(solution)/shard_map/while/body/eval_jaxpr/ppermute | solution.py:21
  992.4 10.4 collective-permute-done.1
  1022.7 16.9 %collective-permute-done.2 = bf16[2,256,768]{1,2,0:T(8,128)(2,1)} collective-permute-done((bf16[2,256,768]{1,2,0:T(8,128)(2,1)}, bf16[2,256,768]{1,2,0:T(8,128)(2,1)}, u32[]{:S(2)}, u32[]{:S(2)}) %collective-permute-start.2) | collective-permute-done | bytes 786464 | tf_op jit(solution)/shard_map/while/body/eval_jaxpr/ppermute | solution.py:21
  1042.1 14.5 %collective-permute-done.3 = bf16[2,256,768]{1,2,0:T(8,128)(2,1)} collective-permute-done((bf16[2,256,768]{1,2,0:T(8,128)(2,1)}, bf16[2,256,768]{1,2,0:T(8,128)(2,1)}, u32[]{:S(2)}, u32[]{:S(2)}) %collective-permute-start.3) | collective-permute-done | bytes 786464 | tf_op jit(solution)/shard_map/while/body/eval_jaxpr/ppermute | solution.py:21
  1058.9 14.5 %collective-permute-done = bf16[2,256,768]{1,2,0:T(8,128)(2,1)} collective-permute-done((bf16[2,256,768]{1,2,0:T(8,128)(2,1)}, bf16[2,256,768]{1,2,0:T(8,128)(2,1)}, u32[]{:S(2)}, u32[]{:S(2)}) %collective-permute-start) | collective-permute-done | bytes 786464 | tf_op jit(solution)/shard_map/while/body/eval_jaxpr/ppermute | solution.py:21
  1073.4 9.5 collective-permute-done.1
  1121.4 18.3 %reduce-scatter.13.cloned.1.call-done = bf16[192,2304]{1,0:T(8,128)(2,1)} async-done(((bf16[768,2304]{1,0:T(8,128)(2,1)}), bf16[192,2304]{1,0:T(8,128)(2,1)}) %reduce-scatter.13.cloned.1.call-update) | async-done | bytes 884752
  1142.0 26.7 %reduce-scatter.7.cloned.1.call-done = bf16[192,768]{1,0:T(8,128)(2,1)} async-done(((bf16[768,768]{1,0:T(8,128)(2,1)}), bf16[192,768]{1,0:T(8,128)(2,1)}) %reduce-scatter.7.cloned.1.call-update) | async-done | bytes 294928 | tf_op jit(solution)/shard_map/reduce_scatter | solution.py:245
  1168.7 50.4 %reduce-scatter.9.cloned.1.call-done = bf16[192,3072]{1,0:T(8,128)(2,1)} async-done(((bf16[768,3072]{1,0:T(8,128)(2,1)}), bf16[192,3072]{1,0:T(8,128)(2,1)}) %reduce-scatter.9.cloned.1.call-update) | async-done | bytes 1179664 | tf_op jit(solution)/shard_map/reduce_scatter | solution.py:257
  1219.2 50.4 %reduce-scatter.11.cloned.1.call-done = bf16[768,768]{1,0:T(8,128)(2,1)} async-done(((bf16[3072,768]{1,0:T(8,128)(2,1)}), bf16[768,768]{1,0:T(8,128)(2,1)}) %reduce-scatter.11.cloned.1.call-update) | async-done | bytes 1179664 | tf_op jit(solution)/shard_map/reduce_scatter | solution.py:263
  1273.1 10.4 all-reduce.19
  1284.2 23.6 %all-reduce.17 = (bf16[192]{0:T(256)(128)(2,1)S(1)}, bf16[192]{0:T(256)(128)(2,1)S(1)}, bf16[192]{0:T(256)(128)(2,1)S(1)}, bf16[192]{0:T(256)(128)(2,1)S(1)}, bf...) all-reduce(bf16[192]{0:T(256)(128)(2,1)S(1)} %dynamic-slice.9, ...), channel_id=1, replica_groups=mesh['ctx'=8,'fsdp'=4] {'ctx'}, use_global_device_ids=true, to_apply=%region_19.20 | all-reduce | flops 2304 | bytes 9216 | tf_op jit(solution)/shard_map/psum | solution.py:278
  1319.9 103.0 %all-reduce.23.cloned.1.call-done = (bf16[192,2304]{0,1:T(8,128)(2,1)}, bf16[192,768]{1,0:T(8,128)(2,1)}, bf16[192,3072]{1,0:T(8,128)(2,1)}, bf16[768,768]{1,0:T(8,128)(2,1)}) async-done(((bf16[192,2304]{0,1:T(8,128)(2,1)}, bf16[192,768]{1,0:T(8,128)(2,1)}, bf16[192,3072]{1,0:T(8,128)(2,1)}, bf16[768,768]{1,0:T(8,128)(2,1)}), (bf16[192,2304]{0,1:T(8,128)(2,1)}, bf16[192,768]{1,0:T(8,128)(2,1)}, ...) | async-done | bytes 3538960 | tf_op jit(solution)/shard_map/psum | solution.py:277
  (469 shorter events, 415.9 us)
Async XLA Ops:
  7.2 36.1 %all-gather.8.cloned.1.call-start = ((), (), s32[]{:S(2)}) async-start(), calls=%async_computation.4 | async-start | bytes 4423680 | tf_op jit(solution)/shard_map/all_gather | solution.py:92
  7.9 143.1 %all-gather.12.cloned.1.call-start = ((), (), s32[]{:S(2)}) async-start(), calls=%async_computation.6 | async-start | bytes 7077888 | tf_op jit(solution)/shard_map/all_gather | solution.py:128
  50.9 200.4 %all-gather.10.cloned.1.call-start = ((), (), s32[]{:S(2)}) async-start(), calls=%async_computation.5 | async-start | bytes 7077888 | tf_op jit(solution)/shard_map/all_gather | solution.py:127
  53.6 306.1 %all-gather.14.cloned.1.call-start = ((), (), s32[]{:S(2)}) async-start(), calls=%async_computation.7 | async-start | bytes 1474560 | tf_op jit(solution)/shard_map/all_gather | solution.py:95
  54.2 308.8 %all-gather.16.cloned.1.call-start = ((), (), s32[]{:S(2)}) async-start(), calls=%async_computation.8 | async-start | bytes 5898240 | tf_op jit(solution)/shard_map/all_gather | solution.py:99
  54.8 196.5 %copy-start.26 = (s32[2]{0:T(128)S(1)}, s32[2]{0:T(128)}, u32[]{:S(2)}) copy-start(s32[2]{0:T(128)} %param.21) | copy-start | bytes 28
  54.8 328.1 %all-gather.18.cloned.1.call-start = ((), (), s32[]{:S(2)}) async-start(), calls=%async_computation.9 | async-start | bytes 5898240 | tf_op jit(solution)/shard_map/all_gather | solution.py:101
  55.4 1084.3 %reduce-scatter.13.cloned.1.call-start = ((), (), s32[]{:S(2)}) async-start(), calls=%async_computation.13 | async-start | bytes 4423680
  430.2 23.4 %collective-permute-start.2 = (bf16[2,256,768]{1,2,0:T(8,128)(2,1)}, bf16[2,256,768]{1,2,0:T(8,128)(2,1)}, u32[]{:S(2)}, u32[]{:S(2)}) collective-permute-start(bf16[2,256,768]{1,2,0:T(8,128)(2,1)} %fusion.126), channel_id=1, source_target_pairs={{0,4},{4,8},{8,12},{12,16},{16,20},{20,24},{24,28},{28,0},{1,5},{5... | collective-permute-start | bytes 2359304 | tf_op jit(solution)/shard_map/while/body/eval_jaxpr/ppermute | solution.py:21
  434.6 35.9 %collective-permute-start.3 = (bf16[2,256,768]{1,2,0:T(8,128)(2,1)}, bf16[2,256,768]{1,2,0:T(8,128)(2,1)}, u32[]{:S(2)}, u32[]{:S(2)}) collective-permute-start(bf16[2,256,768]{1,2,0:T(8,128)(2,1)} %fusion.128), channel_id=1, source_target_pairs={{0,4},{4,8},{8,12},{12,16},{16,20},{20,24},{24,28},{28,0},{1,5},{5... | collective-permute-start | bytes 2359304 | tf_op jit(solution)/shard_map/while/body/eval_jaxpr/ppermute | solution.py:21
  434.6 52.8 %collective-permute-start = (bf16[2,256,768]{1,2,0:T(8,128)(2,1)}, bf16[2,256,768]{1,2,0:T(8,128)(2,1)}, u32[]{:S(2)}, u32[]{:S(2)}) collective-permute-start(bf16[2,256,768]{1,2,0:T(8,128)(2,1)} %copy.116), channel_id=1, source_target_pairs={{0,4},{4,8},{8,12},{12,16},{16,20},{20,24},{24,28},{28,0},{1,5},{5... | collective-permute-start | bytes 2359304 | tf_op jit(solution)/shard_map/while/body/eval_jaxpr/ppermute | solution.py:21
  435.1 68.1 %collective-permute-start.1 = (bf16[2,256,768]{1,2,0:T(8,128)(2,1)}, bf16[2,256,768]{1,2,0:T(8,128)(2,1)}, u32[]{:S(2)}, u32[]{:S(2)}) collective-permute-start(bf16[2,256,768]{1,2,0:T(8,128)(2,1)} %copy.117), channel_id=1, source_target_pairs={{0,4},{4,8},{8,12},{12,16},{16,20},{20,24},{24,28},{28,0},{1,5},{5... | collective-permute-start | bytes 2359304 | tf_op jit(solution)/shard_map/while/body/eval_jaxpr/ppermute | solution.py:21
  516.6 23.5 %collective-permute-start.2 = (bf16[2,256,768]{1,2,0:T(8,128)(2,1)}, bf16[2,256,768]{1,2,0:T(8,128)(2,1)}, u32[]{:S(2)}, u32[]{:S(2)}) collective-permute-start(bf16[2,256,768]{1,2,0:T(8,128)(2,1)} %fusion.126), channel_id=1, source_target_pairs={{0,4},{4,8},{8,12},{12,16},{16,20},{20,24},{24,28},{28,0},{1,5},{5... | collective-permute-start | bytes 2359304 | tf_op jit(solution)/shard_map/while/body/eval_jaxpr/ppermute | solution.py:21
  519.3 37.7 %collective-permute-start.3 = (bf16[2,256,768]{1,2,0:T(8,128)(2,1)}, bf16[2,256,768]{1,2,0:T(8,128)(2,1)}, u32[]{:S(2)}, u32[]{:S(2)}) collective-permute-start(bf16[2,256,768]{1,2,0:T(8,128)(2,1)} %fusion.128), channel_id=1, source_target_pairs={{0,4},{4,8},{8,12},{12,16},{16,20},{20,24},{24,28},{28,0},{1,5},{5... | collective-permute-start | bytes 2359304 | tf_op jit(solution)/shard_map/while/body/eval_jaxpr/ppermute | solution.py:21
  519.7 54.1 %collective-permute-start = (bf16[2,256,768]{1,2,0:T(8,128)(2,1)}, bf16[2,256,768]{1,2,0:T(8,128)(2,1)}, u32[]{:S(2)}, u32[]{:S(2)}) collective-permute-start(bf16[2,256,768]{1,2,0:T(8,128)(2,1)} %copy.116), channel_id=1, source_target_pairs={{0,4},{4,8},{8,12},{12,16},{16,20},{20,24},{24,28},{28,0},{1,5},{5... | collective-permute-start | bytes 2359304 | tf_op jit(solution)/shard_map/while/body/eval_jaxpr/ppermute | solution.py:21
  519.7 69.1 %collective-permute-start.1 = (bf16[2,256,768]{1,2,0:T(8,128)(2,1)}, bf16[2,256,768]{1,2,0:T(8,128)(2,1)}, u32[]{:S(2)}, u32[]{:S(2)}) collective-permute-start(bf16[2,256,768]{1,2,0:T(8,128)(2,1)} %copy.117), channel_id=1, source_target_pairs={{0,4},{4,8},{8,12},{12,16},{16,20},{20,24},{24,28},{28,0},{1,5},{5... | collective-permute-start | bytes 2359304 | tf_op jit(solution)/shard_map/while/body/eval_jaxpr/ppermute | solution.py:21
  602.2 23.5 %collective-permute-start.2 = (bf16[2,256,768]{1,2,0:T(8,128)(2,1)}, bf16[2,256,768]{1,2,0:T(8,128)(2,1)}, u32[]{:S(2)}, u32[]{:S(2)}) collective-permute-start(bf16[2,256,768]{1,2,0:T(8,128)(2,1)} %fusion.126), channel_id=1, source_target_pairs={{0,4},{4,8},{8,12},{12,16},{16,20},{20,24},{24,28},{28,0},{1,5},{5... | collective-permute-start | bytes 2359304 | tf_op jit(solution)/shard_map/while/body/eval_jaxpr/ppermute | solution.py:21
  604.8 37.7 %collective-permute-start.3 = (bf16[2,256,768]{1,2,0:T(8,128)(2,1)}, bf16[2,256,768]{1,2,0:T(8,128)(2,1)}, u32[]{:S(2)}, u32[]{:S(2)}) collective-permute-start(bf16[2,256,768]{1,2,0:T(8,128)(2,1)} %fusion.128), channel_id=1, source_target_pairs={{0,4},{4,8},{8,12},{12,16},{16,20},{20,24},{24,28},{28,0},{1,5},{5... | collective-permute-start | bytes 2359304 | tf_op jit(solution)/shard_map/while/body/eval_jaxpr/ppermute | solution.py:21
  604.8 54.5 %collective-permute-start = (bf16[2,256,768]{1,2,0:T(8,128)(2,1)}, bf16[2,256,768]{1,2,0:T(8,128)(2,1)}, u32[]{:S(2)}, u32[]{:S(2)}) collective-permute-start(bf16[2,256,768]{1,2,0:T(8,128)(2,1)} %copy.116), channel_id=1, source_target_pairs={{0,4},{4,8},{8,12},{12,16},{16,20},{20,24},{24,28},{28,0},{1,5},{5... | collective-permute-start | bytes 2359304 | tf_op jit(solution)/shard_map/while/body/eval_jaxpr/ppermute | solution.py:21
  604.9 68.6 %collective-permute-start.1 = (bf16[2,256,768]{1,2,0:T(8,128)(2,1)}, bf16[2,256,768]{1,2,0:T(8,128)(2,1)}, u32[]{:S(2)}, u32[]{:S(2)}) collective-permute-start(bf16[2,256,768]{1,2,0:T(8,128)(2,1)} %copy.117), channel_id=1, source_target_pairs={{0,4},{4,8},{8,12},{12,16},{16,20},{20,24},{24,28},{28,0},{1,5},{5... | collective-permute-start | bytes 2359304 | tf_op jit(solution)/shard_map/while/body/eval_jaxpr/ppermute | solution.py:21
  609.3 64.2 %copy-start.2 = (bf16[2,256,12,64]{1,3,2,0:T(8,128)(2,1)S(1)}, bf16[2,256,12,64]{1,3,2,0:T(8,128)(2,1)}, u32[]{:S(2)}) copy-start(bf16[2,256,12,64]{1,3,2,0:T(8,128)(2,1)} %copy-done.1) | copy-start | bytes 2359300 | tf_op jit(solution)/shard_map/while
  686.8 23.5 %collective-permute-start.2 = (bf16[2,256,768]{1,2,0:T(8,128)(2,1)}, bf16[2,256,768]{1,2,0:T(8,128)(2,1)}, u32[]{:S(2)}, u32[]{:S(2)}) collective-permute-start(bf16[2,256,768]{1,2,0:T(8,128)(2,1)} %fusion.126), channel_id=1, source_target_pairs={{0,4},{4,8},{8,12},{12,16},{16,20},{20,24},{24,28},{28,0},{1,5},{5... | collective-permute-start | bytes 2359304 | tf_op jit(solution)/shard_map/while/body/eval_jaxpr/ppermute | solution.py:21
  689.5 37.7 %collective-permute-start.3 = (bf16[2,256,768]{1,2,0:T(8,128)(2,1)}, bf16[2,256,768]{1,2,0:T(8,128)(2,1)}, u32[]{:S(2)}, u32[]{:S(2)}) collective-permute-start(bf16[2,256,768]{1,2,0:T(8,128)(2,1)} %fusion.128), channel_id=1, source_target_pairs={{0,4},{4,8},{8,12},{12,16},{16,20},{20,24},{24,28},{28,0},{1,5},{5... | collective-permute-start | bytes 2359304 | tf_op jit(solution)/shard_map/while/body/eval_jaxpr/ppermute | solution.py:21
  689.5 54.5 %collective-permute-start = (bf16[2,256,768]{1,2,0:T(8,128)(2,1)}, bf16[2,256,768]{1,2,0:T(8,128)(2,1)}, u32[]{:S(2)}, u32[]{:S(2)}) collective-permute-start(bf16[2,256,768]{1,2,0:T(8,128)(2,1)} %copy.116), channel_id=1, source_target_pairs={{0,4},{4,8},{8,12},{12,16},{16,20},{20,24},{24,28},{28,0},{1,5},{5... | collective-permute-start | bytes 2359304 | tf_op jit(solution)/shard_map/while/body/eval_jaxpr/ppermute | solution.py:21
  689.5 67.7 %collective-permute-start.1 = (bf16[2,256,768]{1,2,0:T(8,128)(2,1)}, bf16[2,256,768]{1,2,0:T(8,128)(2,1)}, u32[]{:S(2)}, u32[]{:S(2)}) collective-permute-start(bf16[2,256,768]{1,2,0:T(8,128)(2,1)} %copy.117), channel_id=1, source_target_pairs={{0,4},{4,8},{8,12},{12,16},{16,20},{20,24},{24,28},{28,0},{1,5},{5... | collective-permute-start | bytes 2359304 | tf_op jit(solution)/shard_map/while/body/eval_jaxpr/ppermute | solution.py:21
  693.4 63.8 %copy-start.2 = (bf16[2,256,12,64]{1,3,2,0:T(8,128)(2,1)S(1)}, bf16[2,256,12,64]{1,3,2,0:T(8,128)(2,1)}, u32[]{:S(2)}) copy-start(bf16[2,256,12,64]{1,3,2,0:T(8,128)(2,1)} %copy-done.1) | copy-start | bytes 2359300 | tf_op jit(solution)/shard_map/while
  770.6 23.5 %collective-permute-start.2 = (bf16[2,256,768]{1,2,0:T(8,128)(2,1)}, bf16[2,256,768]{1,2,0:T(8,128)(2,1)}, u32[]{:S(2)}, u32[]{:S(2)}) collective-permute-start(bf16[2,256,768]{1,2,0:T(8,128)(2,1)} %fusion.126), channel_id=1, source_target_pairs={{0,4},{4,8},{8,12},{12,16},{16,20},{20,24},{24,28},{28,0},{1,5},{5... | collective-permute-start | bytes 2359304 | tf_op jit(solution)/shard_map/while/body/eval_jaxpr/ppermute | solution.py:21
  773.2 37.7 %collective-permute-start.3 = (bf16[2,256,768]{1,2,0:T(8,128)(2,1)}, bf16[2,256,768]{1,2,0:T(8,128)(2,1)}, u32[]{:S(2)}, u32[]{:S(2)}) collective-permute-start(bf16[2,256,768]{1,2,0:T(8,128)(2,1)} %fusion.128), channel_id=1, source_target_pairs={{0,4},{4,8},{8,12},{12,16},{16,20},{20,24},{24,28},{28,0},{1,5},{5... | collective-permute-start | bytes 2359304 | tf_op jit(solution)/shard_map/while/body/eval_jaxpr/ppermute | solution.py:21
  773.2 54.5 %collective-permute-start = (bf16[2,256,768]{1,2,0:T(8,128)(2,1)}, bf16[2,256,768]{1,2,0:T(8,128)(2,1)}, u32[]{:S(2)}, u32[]{:S(2)}) collective-permute-start(bf16[2,256,768]{1,2,0:T(8,128)(2,1)} %copy.116), channel_id=1, source_target_pairs={{0,4},{4,8},{8,12},{12,16},{16,20},{20,24},{24,28},{28,0},{1,5},{5... | collective-permute-start | bytes 2359304 | tf_op jit(solution)/shard_map/while/body/eval_jaxpr/ppermute | solution.py:21
  773.2 66.8 %collective-permute-start.1 = (bf16[2,256,768]{1,2,0:T(8,128)(2,1)}, bf16[2,256,768]{1,2,0:T(8,128)(2,1)}, u32[]{:S(2)}, u32[]{:S(2)}) collective-permute-start(bf16[2,256,768]{1,2,0:T(8,128)(2,1)} %copy.117), channel_id=1, source_target_pairs={{0,4},{4,8},{8,12},{12,16},{16,20},{20,24},{24,28},{28,0},{1,5},{5... | collective-permute-start | bytes 2359304 | tf_op jit(solution)/shard_map/while/body/eval_jaxpr/ppermute | solution.py:21
  777.1 62.9 %copy-start.2 = (bf16[2,256,12,64]{1,3,2,0:T(8,128)(2,1)S(1)}, bf16[2,256,12,64]{1,3,2,0:T(8,128)(2,1)}, u32[]{:S(2)}) copy-start(bf16[2,256,12,64]{1,3,2,0:T(8,128)(2,1)} %copy-done.1) | copy-start | bytes 2359300 | tf_op jit(solution)/shard_map/while
  853.3 23.5 %collective-permute-start.2 = (bf16[2,256,768]{1,2,0:T(8,128)(2,1)}, bf16[2,256,768]{1,2,0:T(8,128)(2,1)}, u32[]{:S(2)}, u32[]{:S(2)}) collective-permute-start(bf16[2,256,768]{1,2,0:T(8,128)(2,1)} %fusion.126), channel_id=1, source_target_pairs={{0,4},{4,8},{8,12},{12,16},{16,20},{20,24},{24,28},{28,0},{1,5},{5... | collective-permute-start | bytes 2359304 | tf_op jit(solution)/shard_map/while/body/eval_jaxpr/ppermute | solution.py:21
  856.0 37.7 %collective-permute-start.3 = (bf16[2,256,768]{1,2,0:T(8,128)(2,1)}, bf16[2,256,768]{1,2,0:T(8,128)(2,1)}, u32[]{:S(2)}, u32[]{:S(2)}) collective-permute-start(bf16[2,256,768]{1,2,0:T(8,128)(2,1)} %fusion.128), channel_id=1, source_target_pairs={{0,4},{4,8},{8,12},{12,16},{16,20},{20,24},{24,28},{28,0},{1,5},{5... | collective-permute-start | bytes 2359304 | tf_op jit(solution)/shard_map/while/body/eval_jaxpr/ppermute | solution.py:21
  856.0 54.5 %collective-permute-start = (bf16[2,256,768]{1,2,0:T(8,128)(2,1)}, bf16[2,256,768]{1,2,0:T(8,128)(2,1)}, u32[]{:S(2)}, u32[]{:S(2)}) collective-permute-start(bf16[2,256,768]{1,2,0:T(8,128)(2,1)} %copy.116), channel_id=1, source_target_pairs={{0,4},{4,8},{8,12},{12,16},{16,20},{20,24},{24,28},{28,0},{1,5},{5... | collective-permute-start | bytes 2359304 | tf_op jit(solution)/shard_map/while/body/eval_jaxpr/ppermute | solution.py:21
  856.0 65.8 %collective-permute-start.1 = (bf16[2,256,768]{1,2,0:T(8,128)(2,1)}, bf16[2,256,768]{1,2,0:T(8,128)(2,1)}, u32[]{:S(2)}, u32[]{:S(2)}) collective-permute-start(bf16[2,256,768]{1,2,0:T(8,128)(2,1)} %copy.117), channel_id=1, source_target_pairs={{0,4},{4,8},{8,12},{12,16},{16,20},{20,24},{24,28},{28,0},{1,5},{5... | collective-permute-start | bytes 2359304 | tf_op jit(solution)/shard_map/while/body/eval_jaxpr/ppermute | solution.py:21
  935.2 23.5 %collective-permute-start.2 = (bf16[2,256,768]{1,2,0:T(8,128)(2,1)}, bf16[2,256,768]{1,2,0:T(8,128)(2,1)}, u32[]{:S(2)}, u32[]{:S(2)}) collective-permute-start(bf16[2,256,768]{1,2,0:T(8,128)(2,1)} %fusion.126), channel_id=1, source_target_pairs={{0,4},{4,8},{8,12},{12,16},{16,20},{20,24},{24,28},{28,0},{1,5},{5... | collective-permute-start | bytes 2359304 | tf_op jit(solution)/shard_map/while/body/eval_jaxpr/ppermute | solution.py:21
  937.9 37.7 %collective-permute-start.3 = (bf16[2,256,768]{1,2,0:T(8,128)(2,1)}, bf16[2,256,768]{1,2,0:T(8,128)(2,1)}, u32[]{:S(2)}, u32[]{:S(2)}) collective-permute-start(bf16[2,256,768]{1,2,0:T(8,128)(2,1)} %fusion.128), channel_id=1, source_target_pairs={{0,4},{4,8},{8,12},{12,16},{16,20},{20,24},{24,28},{28,0},{1,5},{5... | collective-permute-start | bytes 2359304 | tf_op jit(solution)/shard_map/while/body/eval_jaxpr/ppermute | solution.py:21
  937.9 54.5 %collective-permute-start = (bf16[2,256,768]{1,2,0:T(8,128)(2,1)}, bf16[2,256,768]{1,2,0:T(8,128)(2,1)}, u32[]{:S(2)}, u32[]{:S(2)}) collective-permute-start(bf16[2,256,768]{1,2,0:T(8,128)(2,1)} %copy.116), channel_id=1, source_target_pairs={{0,4},{4,8},{8,12},{12,16},{16,20},{20,24},{24,28},{28,0},{1,5},{5... | collective-permute-start | bytes 2359304 | tf_op jit(solution)/shard_map/while/body/eval_jaxpr/ppermute | solution.py:21
  937.9 64.9 %collective-permute-start.1 = (bf16[2,256,768]{1,2,0:T(8,128)(2,1)}, bf16[2,256,768]{1,2,0:T(8,128)(2,1)}, u32[]{:S(2)}, u32[]{:S(2)}) collective-permute-start(bf16[2,256,768]{1,2,0:T(8,128)(2,1)} %copy.117), channel_id=1, source_target_pairs={{0,4},{4,8},{8,12},{12,16},{16,20},{20,24},{24,28},{28,0},{1,5},{5... | collective-permute-start | bytes 2359304 | tf_op jit(solution)/shard_map/while/body/eval_jaxpr/ppermute | solution.py:21
  1016.2 23.5 %collective-permute-start.2 = (bf16[2,256,768]{1,2,0:T(8,128)(2,1)}, bf16[2,256,768]{1,2,0:T(8,128)(2,1)}, u32[]{:S(2)}, u32[]{:S(2)}) collective-permute-start(bf16[2,256,768]{1,2,0:T(8,128)(2,1)} %fusion.126), channel_id=1, source_target_pairs={{0,4},{4,8},{8,12},{12,16},{16,20},{20,24},{24,28},{28,0},{1,5},{5... | collective-permute-start | bytes 2359304 | tf_op jit(solution)/shard_map/while/body/eval_jaxpr/ppermute | solution.py:21
  1018.8 37.7 %collective-permute-start.3 = (bf16[2,256,768]{1,2,0:T(8,128)(2,1)}, bf16[2,256,768]{1,2,0:T(8,128)(2,1)}, u32[]{:S(2)}, u32[]{:S(2)}) collective-permute-start(bf16[2,256,768]{1,2,0:T(8,128)(2,1)} %fusion.128), channel_id=1, source_target_pairs={{0,4},{4,8},{8,12},{12,16},{16,20},{20,24},{24,28},{28,0},{1,5},{5... | collective-permute-start | bytes 2359304 | tf_op jit(solution)/shard_map/while/body/eval_jaxpr/ppermute | solution.py:21
  1018.8 54.5 %collective-permute-start = (bf16[2,256,768]{1,2,0:T(8,128)(2,1)}, bf16[2,256,768]{1,2,0:T(8,128)(2,1)}, u32[]{:S(2)}, u32[]{:S(2)}) collective-permute-start(bf16[2,256,768]{1,2,0:T(8,128)(2,1)} %copy.116), channel_id=1, source_target_pairs={{0,4},{4,8},{8,12},{12,16},{16,20},{20,24},{24,28},{28,0},{1,5},{5... | collective-permute-start | bytes 2359304 | tf_op jit(solution)/shard_map/while/body/eval_jaxpr/ppermute | solution.py:21
  1018.8 64.0 %collective-permute-start.1 = (bf16[2,256,768]{1,2,0:T(8,128)(2,1)}, bf16[2,256,768]{1,2,0:T(8,128)(2,1)}, u32[]{:S(2)}, u32[]{:S(2)}) collective-permute-start(bf16[2,256,768]{1,2,0:T(8,128)(2,1)} %copy.117), channel_id=1, source_target_pairs={{0,4},{4,8},{8,12},{12,16},{16,20},{20,24},{24,28},{28,0},{1,5},{5... | collective-permute-start | bytes 2359304 | tf_op jit(solution)/shard_map/while/body/eval_jaxpr/ppermute | solution.py:21
  1102.8 65.9 %reduce-scatter.7.cloned.1.call-start = ((), (), s32[]{:S(2)}) async-start(), calls=%async_computation.10 | async-start | bytes 1474560 | tf_op jit(solution)/shard_map/reduce_scatter | solution.py:245
  1106.1 113.0 %reduce-scatter.9.cloned.1.call-start = ((), (), s32[]{:S(2)}) async-start(), calls=%async_computation.11 | async-start | bytes 5898240 | tf_op jit(solution)/shard_map/reduce_scatter | solution.py:257
  1113.5 156.1 %reduce-scatter.11.cloned.1.call-start = ((), (), s32[]{:S(2)}) async-start(), calls=%async_computation.12 | async-start | bytes 5898240 | tf_op jit(solution)/shard_map/reduce_scatter | solution.py:263
  1121.3 301.5 %all-reduce.23.cloned.1.call-start = ((), (), s32[]{:S(2)}) async-start(), calls=%async_computation.14 | async-start | bytes 7667712 | tf_op jit(solution)/shard_map/psum | solution.py:277
  1142.0 130.6 %copy-start.30 = (bf16[192]{0:T(256)(128)(2,1)S(1)}, bf16[192]{0:T(256)(128)(2,1)}, u32[]{:S(2)}) copy-start(bf16[192]{0:T(256)(128)(2,1)} %param.34) | copy-start | bytes 1156
  (67 other events, 680.4 us)
Sparse Core Ops, SparseCore 0:
  9.6 33.6 all-gather.7
  51.0 100.0 all-gather.11
  153.1 98.1 all-gather.9
  252.7 15.6 all-gather.13
  269.8 37.5 all-gather.15
  308.7 37.4 all-gather.17
  1102.9 36.7 reduce-scatter.12
  1143.0 25.7 reduce-scatter.6
  1171.3 47.8 reduce-scatter.8
  1221.7 47.8 reduce-scatter.10
  1274.2 148.6 all-reduce.22
where the time goes:
time: 1440 us
  waiting for transfers between devices  913 us (63%)
  matrix products  235 us (16%)
  other arithmetic  102 us (7%)
  local copies, waits for them, and re-layouts  98.6 us (7%)
  blocking collectives  52.7 us (4%)
  between operations  16.7 us (1%)
    ppermute x32, waiting for transfers between devices, shifted(): return lax.ppermute(value, axis, pairs)  459 us
    psum x1, waiting for transfers between devices, per_device(): lax.psum(owned[0].astype(jnp.bfloat16), 'ctx').astype(jnp.float32)  103 us
    all_gather x1, waiting for transfers between devices, per_device(): piece_keys = lax.all_gather(keys3, 'ctx', axis=1, tiled=True)  100 us
    all_gather x1, waiting for transfers between devices, per_device(): piece_values = lax.all_gather(values3, 'ctx', axis=1, tiled=True)  89.5 us
    reduce_scatter x1, waiting for transfers between devices, per_device(): lax.psum_scatter(terms[7].astype(jnp.bfloat16), 'fsdp', scatter_dimension...  50.4 us
    reduce_scatter x1, waiting for transfers between devices, per_device(): lax.psum_scatter(terms[9].astype(jnp.bfloat16), 'fsdp', scatter_dimension...  50.4 us
    dot_general x12, matrix products, block_scores(): jnp.einsum('sqhd,skhd->shqk', query4, keys4, preferred_element_type=jnp.f...  42.1 us
    while x108, local copies, waits for them, and re-layouts  40.6 us
  transfers between devices with their start and end apart: 43, of which 40 were waited for; matrix products, arithmetic and copies ran while one was open for 18% of the time, Pallas kernels for 0%

commit v1 on v0

v1 whole, which is shorter than its diff:
```python
import functools
import math

import jax
import jax.numpy as jnp
from jax import lax
from jax.experimental import pallas as pl
from jax.experimental.pallas import tpu as pltpu
from jax.sharding import PartitionSpec as P

HEAD_DIM = 64
LANES = 128
EPS = 1e-12
SCALE = 0.125
LOG2E = math.log2(math.e)
COEF = SCALE * LOG2E
MASKED = -1e30
SAFE = 60.0
MASK_LANE = 127
CORR_LANE = 36
VMEM = 48 * 1024 * 1024

f32 = jnp.float32
b16 = jnp.bfloat16


def xor_pairs(count, bit):
    return [(i, i ^ bit) for i in range(count)]


def ring_order(count):
    half = count // 2
    return [2 * p if p < half else 2 * (count - 1 - p) + 1 for p in range(count)]


def ring_slots(axis):
    count = lax.axis_size(axis)
    order = jnp.asarray(ring_order(count), jnp.int32)
    place = lax.axis_index(axis)
    spot = jnp.where(place % 2 == 0, place // 2, count - 1 - place // 2)
    steps = [0]
    for s in range(1, count // 2):
        steps += [-s, s]
    steps.append(count // 2)
    return order[jnp.mod(spot + jnp.asarray(steps, jnp.int32), count)]


def ring_gather(x, axis):
    count = lax.axis_size(axis)
    order = ring_order(count)
    right = [(order[p], order[(p + 1) % count]) for p in range(count)]
    left = [(d, s) for s, d in right]
    slots = [x]
    r = l = x
    for _ in range(1, count // 2):
        r = lax.ppermute(r, axis, right)
        l = lax.ppermute(l, axis, left)
        slots += [r, l]
    slots.append(
        jnp.concatenate(
            [lax.ppermute(r[:1], axis, right), lax.ppermute(l[1:], axis, left)], axis=0
        )
    )
    return slots


def bits_of(count):
    return [1 << k for k in range(count.bit_length() - 1)]


def gather_rows(w, axis):
    count = lax.axis_size(axis)
    i = lax.axis_index(axis)
    cur = w[None]
    for bit in bits_of(count)[1:]:
        other = lax.ppermute(cur, axis, xor_pairs(count, bit))
        low = (i // bit) % 2 == 0
        cur = jnp.concatenate([jnp.where(low, cur, other), jnp.where(low, other, cur)], 0)
    other = lax.ppermute(cur, axis, xor_pairs(count, 1))
    low = i % 2 == 0
    cur = jnp.stack([jnp.where(low, cur, other), jnp.where(low, other, cur)], 1)
    return cur.reshape((-1,) + w.shape[1:])


def halve(x, axis, bit):
    count = lax.axis_size(axis)
    upper = (lax.axis_index(axis) // bit) % 2
    half = x.shape[0] // 2
    send = lax.dynamic_slice_in_dim(x, (1 - upper) * half, half, 0)
    keep = lax.dynamic_slice_in_dim(x, upper * half, half, 0)
    got = lax.ppermute(send, axis, xor_pairs(count, bit))
    return (keep.astype(f32) + got.astype(f32)).astype(b16)


def unhalve(x, axis, bit):
    count = lax.axis_size(axis)
    low = (lax.axis_index(axis) // bit) % 2 == 0
    other = lax.ppermute(x, axis, xor_pairs(count, bit))
    return jnp.concatenate([jnp.where(low, x, other), jnp.where(low, other, x)], 0)


def reduce_rows(g):
    owners = lax.axis_size("fsdp")
    blocks = lax.axis_size("ctx")
    width = g.shape[-1]
    x = g.reshape(owners // 2, 2, -1, width).swapaxes(0, 1).reshape(g.shape)
    for bit in [1] + bits_of(owners)[1:][::-1]:
        x = halve(x, "fsdp", bit)
    if x.shape[0] % (8 * blocks):
        return lax.psum(x, "ctx").astype(f32)
    first = bits_of(blocks)
    second = [first[1], first[0]] + first[2:]
    half = width // 2
    a, b = x[:, :half], x[:, half:]
    for ba, bb in zip(first, second):
        a, b = halve(a, "ctx", ba), halve(b, "ctx", bb)
    for ba, bb in zip(first[::-1], second[::-1]):
        a, b = unhalve(a, "ctx", ba), unhalve(b, "ctx", bb)
    return jnp.concatenate([a, b], 1).astype(f32)


def dot_nt(a, b):
    return lax.dot_general(a, b, (((1,), (1,)), ((), ())), preferred_element_type=f32)


def dot_nn(a, b):
    return lax.dot_general(a, b, (((1,), (0,)), ((), ())), preferred_element_type=f32)


def lane_iota(rows):
    return lax.broadcasted_iota(jnp.int32, (rows, LANES), 1)


def split3(x):
    hi = x.astype(b16)
    rest = x - hi.astype(f32)
    mid = rest.astype(b16)
    low = (rest - mid.astype(f32)).astype(b16)
    return hi, mid, low


def place3(x, lane, at):
    hi, mid, low = (p.astype(f32) for p in split3(x))
    zero = jnp.zeros_like(x)
    return jnp.where(
        lane == at, hi, jnp.where(lane == at + 1, mid, jnp.where(lane == at + 2, low, zero))
    )


def stack_heads(pair):
    rows = pair.shape[0]
    lane = lane_iota(rows)
    zero = jnp.zeros_like(pair)
    return jnp.concatenate(
        [jnp.where(lane < HEAD_DIM, pair, zero), jnp.where(lane >= HEAD_DIM, pair, zero)], 0
    )


def join_heads(x):
    rows = x.shape[0] // 2
    return jnp.where(lane_iota(rows) < HEAD_DIM, x[:rows], x[rows:])


def key_extra(rows, base, length):
    lane = lane_iota(rows)
    dead = base + lax.broadcasted_iota(jnp.int32, (rows, LANES), 0) >= length
    mask = jnp.where(dead, MASKED, 0.0)
    return jnp.where(lane == MASK_LANE, mask, -1.0).astype(b16)


def forward_kernel(slots, bases, lengths, safe, q_ref, *refs):
    k_refs, v_refs = refs[:slots], refs[slots : 2 * slots]
    out_ref, extra_ref, level_ref = refs[2 * slots :]
    seq, pair = pl.program_id(0), pl.program_id(1)
    length = lengths[seq]
    rows = q_ref.shape[1]
    block = k_refs[0].shape[1]
    lane2 = lane_iota(2 * rows)
    stacked = stack_heads(q_ref[0])
    onehot = jnp.where(lane2 == MASK_LANE, 1.0, 0.0)
    level_ref[...] = jnp.zeros_like(level_ref)

    @pl.when(safe[seq * pl.num_programs(1) + pair] == 0)
    def _():
        top = jnp.full((2 * rows, 1), MASKED, f32)
        probe = jnp.concatenate([stacked, onehot.astype(b16)], 1)
        for s in range(slots):
            extra = key_extra(block, bases[s], length)
            scores = dot_nt(probe, jnp.concatenate([k_refs[s][0], extra], 1))
            top = jnp.maximum(top, jnp.max(scores, axis=1, keepdims=True))
        level_ref[...] = jnp.broadcast_to(jnp.ceil(top * COEF), level_ref.shape)

    level = level_ref[...]
    query = jnp.concatenate([stacked, (place3(level / COEF, lane2, 0) + onehot).astype(b16)], 1)
    ones = jnp.ones((block, LANES), b16)
    total = jnp.zeros((2 * rows, 2 * LANES), f32)
    for s in range(slots):
        extra = key_extra(block, bases[s], length)
        scores = dot_nt(query, jnp.concatenate([k_refs[s][0], extra], 1))
        weights = jnp.exp2(scores * COEF).astype(b16)
        total = total + dot_nn(weights, jnp.concatenate([v_refs[s][0], ones], 1))
    sums = total[:, LANES:]
    out_ref[0] = join_heads(total[:, :LANES] / sums)
    whole = (level + jnp.log2(sums)) / COEF
    lane = lane_iota(rows)
    mine = place3(whole[:rows], lane, 6 * pair) + place3(whole[rows:], lane, 6 * pair + 3)

    @pl.when(pair == 0)
    def _():
        extra_ref[0] = jnp.where(lane == MASK_LANE, 1.0, 0.0)

    extra_ref[0] += mine


def corr_kernel(grad_ref, value_ref, extra_ref, out_ref):
    width = grad_ref.shape[1]
    grad = grad_ref[...]
    feature = lax.broadcasted_iota(jnp.int32, (width, LANES), 0) // HEAD_DIM
    lane = lax.broadcasted_iota(jnp.int32, (width, LANES), 1)
    pick = jnp.where(
        (lane >= CORR_LANE) & (feature == (lane - CORR_LANE) // 3), 1.0, 0.0
    ).astype(b16)
    corr = sum(dot_nn(p, pick) for p in split3(grad * value_ref[...]))
    rows = grad.shape[0]
    lane = lane_iota(rows)
    hi, mid, low = (p.astype(f32) for p in split3(corr))
    part = lax.rem(lane, 3)
    placed = jnp.where(part == 0, hi, jnp.where(part == 1, mid, low))
    inside = (lane >= CORR_LANE) & (lane < CORR_LANE + 3 * (width // HEAD_DIM))
    out_ref[:, :width] = grad.astype(b16)
    out_ref[:, width:] = (extra_ref[...] + jnp.where(inside, placed, 0.0)).astype(b16)


def keep_lanes(x, lane, at):
    return jnp.where((lane >= at) & (lane < at + 3), x, jnp.zeros_like(x))


def query_kernel(slots, bases, lengths, q_ref, grad_ref, extra_ref, *refs):
    k_refs, v_refs = refs[:slots], refs[slots : 2 * slots]
    out_ref = refs[2 * slots]
    seq, pair = pl.program_id(0), pl.program_id(1)
    length = lengths[seq]
    block = k_refs[0].shape[1]
    rows = q_ref.shape[1]
    lane = lane_iota(rows)
    extra = extra_ref[0]
    onehot = jnp.where(lane == MASK_LANE, 1.0, 0.0).astype(b16)
    levels = [keep_lanes(extra, lane, 6 * pair + 3 * h) + onehot for h in range(2)]
    corrs = [keep_lanes(extra, lane, CORR_LANE + 6 * pair + 3 * h) for h in range(2)]
    query = jnp.concatenate([stack_heads(q_ref[0]), jnp.concatenate(levels, 0)], 1)
    grad = jnp.concatenate([stack_heads(grad_ref[0]), jnp.concatenate(corrs, 0)], 1)
    total = jnp.zeros((2 * rows, LANES), f32)
    for s in range(slots):
        meet = key_extra(block, bases[s], length)
        keys = k_refs[s][0]
        weights = jnp.exp2(dot_nt(query, jnp.concatenate([keys, meet], 1)) * COEF)
        terms = dot_nt(grad, jnp.concatenate([v_refs[s][0], meet], 1))
        total = total + dot_nn((weights * terms).astype(b16), keys)
    out_ref[0] = (join_heads(total) * SCALE).astype(b16)


def key_kernel(slots, place, lengths, k_ref, v_ref, *refs):
    q_refs, g_refs, e_refs = refs[:slots], refs[slots : 2 * slots], refs[2 * slots : 3 * slots]
    dk_ref, dv_ref = refs[3 * slots :]
    seq, pair = pl.program_id(0), pl.program_id(1)
    length = lengths[seq]
    rows = k_ref.shape[1]
    lane = lane_iota(rows)
    dead = place[0] * rows + lax.broadcasted_iota(jnp.int32, (rows, LANES), 0) >= length
    mask = jnp.where((lane == MASK_LANE) & dead, MASKED, 0.0)
    minus = jnp.full((rows, LANES), -1.0, f32)
    levels = [(keep_lanes(minus, lane, 6 * pair + 3 * h) + mask).astype(b16) for h in range(2)]
    corrs = [keep_lanes(minus, lane, CORR_LANE + 6 * pair + 3 * h).astype(b16) for h in range(2)]
    keys = jnp.concatenate([stack_heads(k_ref[0]), jnp.concatenate(levels, 0)], 1)
    values = jnp.concatenate([stack_heads(v_ref[0]), jnp.concatenate(corrs, 0)], 1)
    dkeys = jnp.zeros((2 * rows, LANES), f32)
    dvalues = jnp.zeros((2 * rows, LANES), f32)
    for s in range(slots):
        query, grad, extra = q_refs[s][0], g_refs[s][0], e_refs[s][0]
        weights = jnp.exp2(dot_nt(keys, jnp.concatenate([query, extra], 1)) * COEF)
        terms = dot_nt(values, jnp.concatenate([grad, extra], 1))
        dvalues = dvalues + dot_nn(weights.astype(b16), grad)
        dkeys = dkeys + dot_nn((weights * terms).astype(b16), query)
    dk_ref[0] = (join_heads(dkeys) * SCALE).astype(b16)
    dv_ref[0] = join_heads(dvalues).astype(b16)


def column(offset):
    return lambda seq, pair, *_: (seq, 0, offset + pair)


def attend_forward(slots_qkv, bases, lengths, safe):
    slots = len(slots_qkv)
    seqs, block, triple = slots_qkv[0].shape
    width = triple // 3
    pairs = width // LANES
    spec = lambda offset: pl.BlockSpec((1, block, LANES), column(offset))
    return pl.pallas_call(
        functools.partial(forward_kernel, slots),
        grid_spec=pltpu.PrefetchScalarGridSpec(
            num_scalar_prefetch=3,
            grid=(seqs, pairs),
            in_specs=[spec(0)] + [spec(pairs)] * slots + [spec(2 * pairs)] * slots,
            out_specs=[spec(0), pl.BlockSpec((1, block, LANES), lambda seq, pair, *_: (seq, 0, 0))],
            scratch_shapes=[pltpu.VMEM((2 * block, LANES), f32)],
        ),
        out_shape=[
            jax.ShapeDtypeStruct((seqs, block, width), f32),
            jax.ShapeDtypeStruct((seqs, block, LANES), f32),
        ],
        compiler_params=pltpu.CompilerParams(vmem_limit_bytes=VMEM),
        cost_estimate=pl.CostEstimate(
            flops=4 * seqs * block * block * slots * width * 4,
            bytes_accessed=slots * seqs * block * width * 4,
            transcendentals=0,
        ),
    )(bases, lengths, safe, slots_qkv[0], *slots_qkv, *slots_qkv)


def attend_query(slots_qkv, grads, bases, lengths):
    slots = len(slots_qkv)
    seqs, block, triple = slots_qkv[0].shape
    width = triple // 3
    pairs = width // LANES
    spec = lambda offset: pl.BlockSpec((1, block, LANES), column(offset))
    last = pl.BlockSpec((1, block, LANES), lambda seq, pair, *_: (seq, 0, pairs))
    return pl.pallas_call(
        functools.partial(query_kernel, slots),
        grid_spec=pltpu.PrefetchScalarGridSpec(
            num_scalar_prefetch=2,
            grid=(seqs, pairs),
            in_specs=[spec(0), spec(0), last] + [spec(pairs)] * slots + [spec(2 * pairs)] * slots,
            out_specs=spec(0),
        ),
        out_shape=jax.ShapeDtypeStruct((seqs, block, width), b16),
        compiler_params=pltpu.CompilerParams(vmem_limit_bytes=VMEM),
        cost_estimate=pl.CostEstimate(
            flops=6 * seqs * block * block * slots * width * 4,
            bytes_accessed=slots * seqs * block * width * 4,
            transcendentals=0,
        ),
    )(bases, lengths, slots_qkv[0], grads, grads, *slots_qkv, *slots_qkv)


def attend_keys(slots_qkv, slots_grads, place, lengths):
    slots = len(slots_qkv)
    seqs, block, triple = slots_qkv[0].shape
    width = triple // 3
    pairs = width // LANES
    spec = lambda offset: pl.BlockSpec((1, block, LANES), column(offset))
    last = pl.BlockSpec((1, block, LANES), lambda seq, pair, *_: (seq, 0, pairs))
    shape = jax.ShapeDtypeStruct((seqs, block, width), b16)
    return pl.pallas_call(
        functools.partial(key_kernel, slots),
        grid_spec=pltpu.PrefetchScalarGridSpec(
            num_scalar_prefetch=2,
            grid=(seqs, pairs),
            in_specs=[spec(pairs), spec(2 * pairs)] + [spec(0)] * (2 * slots) + [last] * slots,
            out_specs=[spec(0), spec(0)],
        ),
        out_shape=[shape, shape],
        compiler_params=pltpu.CompilerParams(vmem_limit_bytes=VMEM),
        cost_estimate=pl.CostEstimate(
            flops=8 * seqs * block * block * slots * width * 4,
            bytes_accessed=slots * seqs * block * width * 4,
            transcendentals=0,
        ),
    )(place, lengths, slots_qkv[0], slots_qkv[0], *slots_qkv, *slots_grads, *slots_grads)


def place_corr(dattended, attended, extra):
    rows, width = dattended.shape
    return pl.pallas_call(
        corr_kernel,
        out_shape=jax.ShapeDtypeStruct((rows, width + LANES), b16),
        compiler_params=pltpu.CompilerParams(vmem_limit_bytes=VMEM),
    )(dattended, attended, extra)


def layer_norm(value, gain, shift):
    mean = jnp.mean(value, axis=-1, keepdims=True)
    centred = value - mean
    spread = jnp.mean(centred * centred, axis=-1, keepdims=True)
    return centred * lax.rsqrt(spread + EPS) * gain + shift


def gelu_exact(value):
    return jax.nn.gelu(value, approximate=False)


def largest_norm(rows3):
    seqs, block, width = rows3.shape
    heads = width // HEAD_DIM
    pick = (jnp.arange(width)[:, None] // HEAD_DIM == jnp.arange(heads)[None]).astype(b16)
    squares = rows3.astype(f32)
    squares = (squares * squares).astype(b16)
    sums = jnp.einsum("sbw,wh->sbh", squares, pick, preferred_element_type=f32)
    return jnp.max(sums, axis=1)


def per_device(
    tokens,
    lengths,
    attend_weight,
    query_bias,
    value_bias,
    mixing_weight,
    mixing_bias,
    first_gain,
    first_shift,
    up_weight,
    up_bias,
    down_weight,
    down_bias,
    second_gain,
    second_shift,
    cotangent,
):
    seqs, block, width = tokens.shape
    rows = seqs * block
    owners = lax.axis_size("fsdp")
    owner = lax.axis_index("fsdp")
    place = lax.axis_index("ctx")

    small = [
        query_bias, value_bias, mixing_bias, first_gain, first_shift,
        down_bias, second_gain, second_shift, up_bias,
    ]
    small_full = lax.all_gather(jnp.concatenate(small), "fsdp", axis=0)
    cuts, at = [], 0
    for part in small:
        size = part.shape[0]
        cuts.append(small_full[:, at : at + size].reshape(-1).astype(f32))
        at += size
    qbias, vbias, mixbias, fgain, fshift, downbias, sgain, sshift, upbias = cuts

    flat = tokens.reshape(rows, width)
    flat_low = flat.astype(b16)
    attend_full = gather_rows(attend_weight, "fsdp")
    token_slots = ring_gather(flat_low.reshape(seqs, block, width), "ctx")
    mixing_full = gather_rows(mixing_weight, "fsdp")
    up_full = gather_rows(up_weight, "fsdp")
    down_full = gather_rows(down_weight, "fsdp")

    bias = jnp.concatenate([qbias, jnp.zeros_like(qbias), vbias])
    slots_qkv = [
        (jnp.dot(t.reshape(rows, width), attend_full, preferred_element_type=f32) + bias)
        .astype(b16)
        .reshape(seqs, block, 3 * width)
        for t in token_slots
    ]
    spots = ring_slots("ctx")
    bases = spots * block
    key_norm = functools.reduce(
        jnp.maximum, [largest_norm(s[..., width : 2 * width]) for s in slots_qkv]
    )
    query_norm = largest_norm(slots_qkv[0][..., :width])
    bound = jnp.sqrt(key_norm * query_norm) * COEF
    safe = jnp.all(bound.reshape(seqs, -1, 2) < SAFE, axis=-1).astype(jnp.int32).reshape(-1)

    attended3, extra = attend_forward(slots_qkv, bases, lengths, safe)
    attended = attended3.reshape(rows, width)
    attended_low = attended.astype(b16)
    mixed = jnp.dot(attended_low, mixing_full, preferred_element_type=f32) + mixbias
    hidden = flat + mixed
    first = layer_norm(hidden, fgain, fshift)
    first_low = first.astype(b16)
    pre = jnp.dot(first_low, up_full, preferred_element_type=f32) + upbias
    act, gelu_back = jax.vjp(gelu_exact, pre)
    act_low = act.astype(b16)
    branch = jnp.dot(act_low, down_full, preferred_element_type=f32) + downbias
    summed = first + branch
    result, second_back = jax.vjp(layer_norm, summed, sgain, sshift)
    dsummed, grad_sgain, grad_sshift = second_back(cotangent.reshape(rows, width))
    dbranch = dsummed.astype(b16)
    dact = jnp.einsum("rd,fd->rf", dbranch, down_full, preferred_element_type=f32)
    dpre = gelu_back(dact)[0].astype(b16)
    dfirst = dsummed + jnp.einsum("rf,df->rd", dpre, up_full, preferred_element_type=f32)
    _, first_back = jax.vjp(layer_norm, hidden, fgain, fshift)
    dhidden, grad_fgain, grad_fshift = first_back(dfirst)
    dmixed = dhidden.astype(b16)
    dattended = jnp.einsum("re,de->rd", dmixed, mixing_full, preferred_element_type=f32)

    grads = place_corr(dattended, attended, extra.reshape(rows, LANES))
    grads = grads.reshape(seqs, block, width + LANES)
    slots_grads = ring_gather(grads, "ctx")

    grad_down = jnp.einsum("rf,rd->fd", act_low, dbranch, preferred_element_type=f32)
    grad_up = jnp.einsum("rd,rf->df", first_low, dpre, preferred_element_type=f32)
    grad_mixing = jnp.einsum("rd,re->de", attended_low, dmixed, preferred_element_type=f32)
    own_down = reduce_rows(grad_down.astype(b16))
    own_up = reduce_rows(grad_up.astype(b16))
    own_mixing = reduce_rows(grad_mixing.astype(b16))

    dquery = attend_query(slots_qkv, grads, bases, lengths)
    dkeys, dvalues = attend_keys(slots_qkv, slots_grads, place.reshape(1), lengths)
    dprojected = jnp.concatenate([dquery, dkeys, dvalues], axis=2).reshape(rows, 3 * width)
    grad_attend = jnp.einsum("rd,re->de", flat_low, dprojected, preferred_element_type=f32)
    own_attend = reduce_rows(grad_attend.astype(b16))
    tokens_grad = dhidden + jnp.einsum(
        "re,de->rd", dprojected, attend_full, preferred_element_type=f32
    )

    def summed_rows(x):
        return jnp.sum(x.astype(f32), axis=0)

    sums = [
        summed_rows(dmixed), grad_fgain, grad_fshift, summed_rows(dbranch),
        grad_sgain, grad_sshift, summed_rows(dpre),
    ]
    early = lax.psum(jnp.concatenate([v.reshape(owners, -1) for v in sums], 1), ("fsdp", "ctx"))
    late = [summed_rows(dquery.reshape(rows, width)), summed_rows(dvalues.reshape(rows, width))]
    late = lax.psum(jnp.concatenate([v.reshape(owners, -1) for v in late], 1), ("fsdp", "ctx"))
    mine = jnp.concatenate(
        [
            lax.dynamic_index_in_dim(late, owner, 0, keepdims=False),
            lax.dynamic_index_in_dim(early, owner, 0, keepdims=False),
        ]
    )
    share = width // owners
    (
        own_qbias, own_vbias, own_mixbias, own_fgain, own_fshift,
        own_downbias, own_sgain, own_sshift,
    ) = (mine[k * share : (k + 1) * share] for k in range(8))
    own_upbias = mine[8 * share :]
    return (
        result.reshape(seqs, block, width),
        tokens_grad.reshape(seqs, block, width),
        own_attend,
        own_qbias,
        own_vbias,
        own_mixing,
        own_mixbias,
        own_fgain,
        own_fshift,
        own_up,
        own_upbias,
        own_down,
        own_downbias,
        own_sgain,
        own_sshift,
    )


def solution(mesh):
    rows = P("fsdp", "ctx", None)
    matrix = P("fsdp", None)
    vector = P("fsdp")
    return jax.shard_map(
        per_device,
        mesh=mesh,
        in_specs=(
            rows, vector, matrix, vector, vector, matrix, vector, vector, vector,
            matrix, vector, matrix, vector, vector, vector, rows,
        ),
        out_specs=(
            rows, rows, matrix, vector, vector, matrix, vector, vector, vector,
            matrix, vector, matrix, vector, vector, vector,
        ),
        check_vma=False,
    )
```

time: 1440 us -> 605 us (0.42)
  waiting for transfers between devices: 913 us -> 153 us
  matrix products: 235 us -> 76.4 us
  Pallas kernels: 0 us -> 95.5 us
  starting transfers between devices: 9.98 us -> 94.4 us
  other arithmetic: 102 us -> 45.2 us
  local copies, waits for them, and re-layouts: 98.6 us -> 49 us
  blocking collectives: 52.7 us -> 83.6 us
    ppermute x32 -> x80, waiting for transfers between devices: 459 us -> 153 us  [the longest x32 74.2 us: halve(): got = lax.ppermute(send, axis, xor_pairs(count, bit))]
    all_gather x6 -> x0, waiting for transfers between devices: 202 us -> none  [the longest x1 100 us: per_device(): piece_keys = lax.all_gather(keys3, 'ctx', axis=1, tiled=True)]
    dot_general x52 -> x20, matrix products: 194 us -> 45.3 us  [the longest x8 19.5 us: per_device(): jnp.dot(t.reshape(rows, width), attend_full, preferred_element_type=f32)]
    reduce_scatter x3 -> x0, waiting for transfers between devices: 128 us -> none  [the longest x1 50.4 us: per_device(): lax.psum_scatter(terms[7].astype(jnp.bfloat16), 'fsdp', scatter_dimension...]
    psum x1 -> x0, waiting for transfers between devices: 103 us -> none  [per_device(): lax.psum(owned[0].astype(jnp.bfloat16), 'ctx').astype(jnp.float32)]
    pallas_call x0 -> x4, Pallas kernels: none -> 95.5 us  [the longest x1 32.9 us: attend_forward(): pl.pallas_call(functools.partial(forward_kernel, slots), grid_spec=pltpu....]
    ppermute x32 -> x80, starting transfers between devices: 9.54 us -> 94.4 us  [the longest x32 38.9 us: halve(): got = lax.ppermute(send, axis, xor_pairs(count, bit))]
    convert_element_type x54 -> x39, other arithmetic: 67.2 us -> 19.7 us  [the longest x32 13.6 us: halve(): return (keep.astype(f32) + got.astype(f32)).astype(b16)]
  transfers between devices with their start and end apart: 43 -> 80, of which waited for: 40 -> 47; matrix products, arithmetic and copies ran while one was open for 18% -> 18% of each run, Pallas kernels for 0% -> 16%
where the time goes in v1:
time: 605 us; the launch traced here: 599 us
  waiting for transfers between devices  153 us (25%)
  Pallas kernels  95.5 us (16%)
  starting transfers between devices  94.4 us (16%)
  blocking collectives  83.6 us (14%)
  matrix products  76.4 us (13%)
  local copies, waits for them, and re-layouts  49 us (8%)
  other arithmetic  45.2 us (7%)
    ppermute x32, waiting for transfers between devices, halve(): got = lax.ppermute(send, axis, xor_pairs(count, bit))  74.2 us
    all_gather x1, blocking collectives, per_device(): small_full = lax.all_gather(jnp.concatenate(small), 'fsdp', axis=0)  44.5 us
    psum x1, blocking collectives, per_device(): lax.psum(jnp.concatenate([v.reshape(owners, -1) for v in late], 1), ('fsd...  39.1 us
    ppermute x32, starting transfers between devices, halve(): got = lax.ppermute(send, axis, xor_pairs(count, bit))  38.9 us
    ppermute x24, waiting for transfers between devices, unhalve(): other = lax.ppermute(x, axis, xor_pairs(count, bit))  38.7 us
    ppermute x6, waiting for transfers between devices, ring_gather(): l = lax.ppermute(l, axis, left)  34.8 us
    pallas_call x1, Pallas kernels, attend_forward(): pl.pallas_call(functools.partial(forward_kernel, slots), grid_spec=pltpu....  32.9 us
    pallas_call x1, Pallas kernels, attend_keys(): pl.pallas_call(functools.partial(key_kernel, slots), grid_spec=pltpu.Pref...  32.8 us
  transfers between devices with their start and end apart: 80, of which 47 were waited for; matrix products, arithmetic and copies ran while one was open for 18% of the time, Pallas kernels for 16%

profile of v1, /device:TPU:0, one launch (start us, length us, event | category | flops | bytes accessed | tf_op | source)
XLA Modules:
  0.0 599.5 jit_solution(6030954760439633437)
XLA Ops:
  2.3 3.0 collective-permute-start.3
  9.4 5.4 concatenate.118
  14.8 44.5 %all-gather.1 = bf16[4,1,2304]{2,1,0:T(2,128)(2,1)S(1)} all-gather(bf16[1,1,2304]{2,1,0:T(2,128)(2,1)S(1)} %reshape.436), channel_id=2, replica_groups=mesh['ctx'=8,'fsdp'=4] {'fsdp'}, dimensions={0}, use_global_device_ids=true | all-gather | bytes 23040 | tf_op jit(solution)/shard_map/all_gather | solution.py:429
  83.4 13.7 %collective-permute-done.5 = bf16[2,256,768]{2,1,0:T(8,128)(2,1)S(1)} collective-permute-done((bf16[2,256,768]{2,1,0:T(8,128)(2,1)}, bf16[2,256,768]{2,1,0:T(8,128)(2,1)S(1)}, u32[]{:S(2)}, u32[]{:S(2)}) %collective-permute-start.5) | collective-permute-done | bytes 786464 | tf_op jit(solution)/shard_map/ppermute | solution.py:57
  104.9 11.3 %collective-permute-done.7 = bf16[2,256,768]{2,1,0:T(8,128)(2,1)S(1)} collective-permute-done((bf16[2,256,768]{2,1,0:T(8,128)(2,1)S(1)}, bf16[2,256,768]{2,1,0:T(8,128)(2,1)S(1)}, u32[]{:S(2)}, u32[]{:S(2)}) %collective-permute-start.7) | collective-permute-done | bytes 786464 | tf_op jit(solution)/shard_map/ppermute | solution.py:57
  131.7 3.7 fusion.9
  135.5 3.7 fusion.8
  144.6 32.9 %shard_map.289 = (f32[2,256,768]{2,1,0:T(8,128)S(1)}, f32[2,256,128]{2,1,0:T(8,128)S(1)}) custom-call(s32[8]{0:T(128)S(1)} %broadcast_multiply_fusion.2.bases, s32[2]{0:T(128)S(1)} %copy-done.2, s32[12]{0:T(128)S(1)} %reshape.410.safe, bf16[2,256,2304]{2,1,0:T(8,128)(2,1)S(1)} %bitcast.177, bf16[2,256,2304]{2,1,0:T(8,128)(2,1)S(1)} %bitcast.178, ...), custom_call_target="tpu_custom_call" | custom-call | flops 12884901888 | bytes 12582912 | tf_op jit(solution)/shard_map/pallas_call | solution.py:298
  187.5 18.4 %multiply_convert_fusion = (bf16[512,3072]{1,0:T(8,128)(2,1)S(1)}, f32[512,3072]{1,0:T(8,128)}, f32[512,3072]{1,0:T(8,128)}) fusion(f32[3072]{0:T(1024)S(1)} %copy-done.43, bf16[768,3072]{1,0:T(8,128)(2,1)S(1)} %bitcast.195, f32[512,768]{1,0:T(8,128)S(1)} %get-tuple-element.132, f32[768]{0:T(1024)S(1)} %copy-done.46, f32[768]{0:T(1024)S(1)} %copy-done.42, ...), kind=kOutput, calls=%fused_computation.6 | convolution fusion | flops 2521694208 | bytes 22042624 | tf_op jit(solution)/shard_map/dot_general | solution.py:468
  205.9 2.8 fusion.64
  213.6 9.1 %convert_reduce_fusion = (f32[3072]{0:T(1024)S(1)}, bf16[512,3072]{1,0:T(8,128)(2,1)}) fusion(f32[512,3072]{1,0:T(8,128)} %get-tuple-element.41, f32[512,3072]{1,0:T(8,128)} %get-tuple-element.133, f32[3072]{0:T(1024)S(1)} %copy-done.43, bf16[512,768]{1,0:T(8,128)(2,1)S(1)} %get-tuple-element.33, bf16[3072,768]{1,0:T(8,128)(2,1)S(1)} %bitcast.202), kind=kOutput, calls=%fused_computation.4 | convolution fusion | flops 2442654720 | bytes 21258240 | tf_op jit(solution)/shard_map/rd,fd->rf/dot_general | solution.py:476
  222.7 5.0 multiply_reduce_fusion
  233.9 29.0 %shard_map.291 = bf16[2,256,768]{2,1,0:T(8,128)(2,1)S(1)} custom-call(s32[8]{0:T(128)S(1)} %broadcast_multiply_fusion.2.bases, s32[2]{0:T(128)S(1)} %copy-done.2, bf16[2,256,2304]{2,1,0:T(8,128)(2,1)S(1)} %bitcast.183, bf16[2,256,896]{2,1,0:T(8,128)(2,1)S(1)} %bitcast.170, bf16[2,256,896]{2,1,0:T(8,128)(2,1)S(1)} %bitcast.171, ...), custom_call_target="tpu_custom_call" | custom-call | flops 19327352832 | bytes 12582912 | tf_op jit(solution)/shard_map/pallas_call | solution.py:327
  264.8 3.4 convolution_convert_fusion.1
  276.7 4.6 convolution_convert_fusion
  287.6 6.5 %collective-permute-done.39 = bf16[192,768]{1,0:T(8,128)(2,1)S(1)} collective-permute-done((bf16[192,768]{1,0:T(8,128)(2,1)}, bf16[192,768]{1,0:T(8,128)(2,1)S(1)}, u32[]{:S(2)}, u32[]{:S(2)}) %collective-permute-start.39) | collective-permute-done | bytes 294944 | tf_op jit(solution)/shard_map/ppermute | solution.py:91
  298.7 2.3 collective-permute-start.19
  302.8 17.2 %collective-permute-done.47 = bf16[48,384]{1,0:T(8,128)(2,1)S(1)} collective-permute-done((bf16[48,384]{1,0:T(8,128)(2,1)S(1)}, bf16[48,384]{1,0:T(8,128)(2,1)S(1)}, u32[]{:S(2)}, u32[]{:S(2)}) %collective-permute-start.47) | collective-permute-done | bytes 36896 | tf_op jit(solution)/shard_map/ppermute | solution.py:91
  320.0 3.9 collective-permute-done.41
  326.1 2.6 collective-permute-done.48
  330.7 2.6 collective-permute-done.42
  335.4 2.6 collective-permute-done.49
  340.1 2.6 collective-permute-done.43
  342.7 2.5 collective-permute-start.50
  348.2 3.0 collective-permute-done.44
  352.4 4.0 collective-permute-done.51
  356.4 2.6 collective-permute-start.45
  359.0 2.9 collective-permute-done.45
  364.9 3.3 add_convert_fusion.2
  370.0 9.7 %collective-permute-done.21.refs_14_.refs_22_ = bf16[2,256,896]{2,1,0:T(8,128)(2,1)S(1)} collective-permute-done((bf16[2,256,896]{2,1,0:T(8,128)(2,1)S(1)}, bf16[2,256,896]{2,1,0:T(8,128)(2,1)S(1)}, u32[]{:S(2)}, u32[]{:S(2)}) %collective-permute-start.21) | collective-permute-done | bytes 917536 | tf_op jit(solution)/shard_map/ppermute | solution.py:57
  390.7 32.8 %shard_map.292 = (bf16[2,256,768]{2,1,0:T(8,128)(2,1)S(1)}, bf16[2,256,768]{2,1,0:T(8,128)(2,1)S(1)}) custom-call(s32[1]{0:T(128)} %bitcast.58.place, s32[2]{0:T(128)S(1)} %copy-done.2, bf16[2,256,2304]{2,1,0:T(8,128)(2,1)} %bitcast.180, bf16[2,256,2304]{2,1,0:T(8,128)(2,1)} %bitcast.181, bf16[2,256,2304]{2,1,0:T(8,128)(2,1)} %bitcast.182, ...), custom_call_target="tpu_custom_call" | custom-call | flops 25769803776 | bytes 12582912 | tf_op jit(solution)/shard_map/pallas_call | solution.py:353
  429.2 39.1 %all-reduce = (f32[4,384]{1,0:T(4,128)S(1)}, f32[4,1920]{1,0:T(4,128)S(1)}) all-reduce(f32[4,384]{1,0:T(4,128)S(1)} %pad_maximum_fusion.28, f32[4,1920]{1,0:T(4,128)S(1)} %concatenate.141), channel_id=1, replica_groups=mesh['ctx'=8,'fsdp'=4] {'fsdp','ctx'}, use_global_device_ids=true, to_apply=%region_20.21 | all-reduce | flops 9216 | bytes 73728 | tf_op jit(solution)/shard_map/psum | solution.py:513
  471.1 5.3 add_add_fusion.3
  479.9 2.3 collective-permute-start.54
  487.5 3.2 collective-permute-start.61
  494.2 2.3 collective-permute-start.75
  503.6 2.7 collective-permute-start.70
  506.3 5.6 collective-permute-done.62
  529.4 2.7 collective-permute-start.79
  535.5 6.5 %collective-permute-done.79 = bf16[384,384]{1,0:T(8,128)(2,1)S(1)} collective-permute-done((bf16[384,384]{1,0:T(8,128)(2,1)S(1)}, bf16[384,384]{1,0:T(8,128)(2,1)S(1)}, u32[]{:S(2)}, u32[]{:S(2)}) %collective-permute-start.79) | collective-permute-done | bytes 294944 | tf_op jit(solution)/shard_map/ppermute | solution.py:98
  549.2 13.5 %collective-permute-done.25 = bf16[192,2304]{1,0:T(8,128)(2,1)S(1)} collective-permute-done((bf16[192,2304]{1,0:T(8,128)(2,1)S(1)}, bf16[192,2304]{1,0:T(8,128)(2,1)S(1)}, u32[]{:S(2)}, u32[]{:S(2)}) %collective-permute-start.25) | collective-permute-done | bytes 884768 | tf_op jit(solution)/shard_map/ppermute | solution.py:91
  564.0 6.0 %collective-permute-done.32 = bf16[96,1152]{1,0:T(8,128)(2,1)S(1)} collective-permute-done((bf16[96,1152]{1,0:T(8,128)(2,1)S(1)}, bf16[96,1152]{1,0:T(8,128)(2,1)S(1)}, u32[]{:S(2)}, u32[]{:S(2)}) %collective-permute-start.32) | collective-permute-done | bytes 221216 | tf_op jit(solution)/shard_map/ppermute | solution.py:91
  571.3 3.6 collective-permute-done.33
  575.8 2.3 collective-permute-start.28
  578.1 2.7 collective-permute-done.34
  581.4 2.5 collective-permute-start.29
  586.7 2.4 collective-permute-start.30
  593.2 3.8 collective-permute-done.37
  (477 shorter events, 198.7 us)
Async XLA Ops:
  2.3 74.6 %collective-permute-start.3 = (bf16[2,256,768]{2,1,0:T(8,128)(2,1)S(1)}, bf16[2,256,768]{2,1,0:T(8,128)(2,1)}, u32[]{:S(2)}, u32[]{:S(2)}) collective-permute-start(bf16[2,256,768]{2,1,0:T(8,128)(2,1)S(1)} %convert_element_type.560), channel_id=1, source_target_pairs={{8,0},{16,8},{24,16},{28,24},{20,28},{12,20},{4,12},{0,4},{9,1},{1... | collective-permute-start | bytes 2359304 | tf_op jit(solution)/shard_map/ppermute | solution.py:57
  5.4 71.7 %collective-permute-start.2 = (bf16[2,256,768]{2,1,0:T(8,128)(2,1)S(1)}, bf16[2,256,768]{2,1,0:T(8,128)(2,1)}, u32[]{:S(2)}, u32[]{:S(2)}) collective-permute-start(bf16[2,256,768]{2,1,0:T(8,128)(2,1)S(1)} %convert_element_type.560), channel_id=1, source_target_pairs={{0,8},{8,16},{16,24},{24,28},{28,20},{20,12},{12,4},{4,0},{1,9},{9... | collective-permute-start | bytes 2359304 | tf_op jit(solution)/shard_map/ppermute | solution.py:56
  5.5 76.5 %collective-permute-start.12 = (bf16[1,192,3072]{2,1,0:T(8,128)(2,1)S(1)}, bf16[1,192,3072]{2,1,0:T(8,128)(2,1)}, u32[]{:S(2)}, u32[]{:S(2)}) collective-permute-start(bf16[1,192,3072]{2,1,0:T(8,128)(2,1)S(1)} %bitcast.219), channel_id=1, source_target_pairs={{0,2},{1,3},{2,0},{3,1},{4,6},{5,7},{6,4},{7,5},{8,10},{9,11},{10,... | collective-permute-start | bytes 3538952 | tf_op jit(solution)/shard_map/ppermute | solution.py:76
  7.4 71.2 %collective-permute-start = (bf16[1,192,2304]{2,1,0:T(8,128)(2,1)}, bf16[1,192,2304]{2,1,0:T(8,128)(2,1)}, u32[]{:S(2)}, u32[]{:S(2)}) collective-permute-start(bf16[1,192,2304]{2,1,0:T(8,128)(2,1)} %bitcast.223), channel_id=1, source_target_pairs={{0,2},{1,3},{2,0},{3,1},{4,6},{5,7},{6,4},{7,5},{8,10},{9,11},{10,... | collective-permute-start | bytes 2654216 | tf_op jit(solution)/shard_map/ppermute | solution.py:76
  7.5 66.6 %collective-permute-start.10 = (bf16[1,192,768]{2,1,0:T(8,128)(2,1)}, bf16[1,192,768]{2,1,0:T(8,128)(2,1)}, u32[]{:S(2)}, u32[]{:S(2)}) collective-permute-start(bf16[1,192,768]{2,1,0:T(8,128)(2,1)} %bitcast.227), channel_id=1, source_target_pairs={{0,2},{1,3},{2,0},{3,1},{4,6},{5,7},{6,4},{7,5},{8,10},{9,11},{10,... | collective-permute-start | bytes 884744 | tf_op jit(solution)/shard_map/ppermute | solution.py:76
  74.1 28.5 %collective-permute-start.14 = (bf16[1,768,768]{2,1,0:T(8,128)(2,1)}, bf16[1,768,768]{2,1,0:T(8,128)(2,1)S(1)}, u32[]{:S(2)}, u32[]{:S(2)}) collective-permute-start(bf16[1,768,768]{2,1,0:T(8,128)(2,1)} %bitcast.220), channel_id=1, source_target_pairs={{0,2},{1,3},{2,0},{3,1},{4,6},{5,7},{6,4},{7,5},{8,10},{9,11},{10,... | collective-permute-start | bytes 3538952 | tf_op jit(solution)/shard_map/ppermute | solution.py:76
  77.0 20.1 %collective-permute-start.5 = (bf16[2,256,768]{2,1,0:T(8,128)(2,1)}, bf16[2,256,768]{2,1,0:T(8,128)(2,1)S(1)}, u32[]{:S(2)}, u32[]{:S(2)}) collective-permute-start(bf16[2,256,768]{2,1,0:T(8,128)(2,1)} %collective-permute-done.3), channel_id=1, source_target_pairs={{8,0},{16,8},{24,16},{28,24},{20,28},{12,20},{4,12},{0,4},{9,1},{1... | collective-permute-start | bytes 2359304 | tf_op jit(solution)/shard_map/ppermute | solution.py:57
  78.6 20.1 %collective-permute-start.4 = (bf16[2,256,768]{2,1,0:T(8,128)(2,1)}, bf16[2,256,768]{2,1,0:T(8,128)(2,1)S(1)}, u32[]{:S(2)}, u32[]{:S(2)}) collective-permute-start(bf16[2,256,768]{2,1,0:T(8,128)(2,1)} %collective-permute-done.2), channel_id=1, source_target_pairs={{0,8},{8,16},{16,24},{24,28},{28,20},{20,12},{12,4},{4,0},{1,9},{9... | collective-permute-start | bytes 2359304 | tf_op jit(solution)/shard_map/ppermute | solution.py:56
  80.7 38.3 %collective-permute-start.1 = (bf16[2,192,2304]{2,1,0:T(8,128)(2,1)S(1)}, bf16[2,192,2304]{2,1,0:T(8,128)(2,1)S(1)}, u32[]{:S(2)}, u32[]{:S(2)}) collective-permute-start(bf16[2,192,2304]{2,1,0:T(8,128)(2,1)S(1)} %pad_maximum_fusion.6), channel_id=1, source_target_pairs={{0,1},{1,0},{2,3},{3,2},{4,5},{5,4},{6,7},{7,6},{8,9},{9,8},{10,11... | collective-permute-start | bytes 5308424 | tf_op jit(solution)/shard_map/ppermute | solution.py:79
  97.1 19.1 %collective-permute-start.7 = (bf16[2,256,768]{2,1,0:T(8,128)(2,1)S(1)}, bf16[2,256,768]{2,1,0:T(8,128)(2,1)S(1)}, u32[]{:S(2)}, u32[]{:S(2)}) collective-permute-start(bf16[2,256,768]{2,1,0:T(8,128)(2,1)S(1)} %collective-permute-done.5), channel_id=1, source_target_pairs={{8,0},{16,8},{24,16},{28,24},{20,28},{12,20},{4,12},{0,4},{9,1},{1... | collective-permute-start | bytes 2359304 | tf_op jit(solution)/shard_map/ppermute | solution.py:57
  98.7 19.2 %collective-permute-start.6 = (bf16[2,256,768]{2,1,0:T(8,128)(2,1)S(1)}, bf16[2,256,768]{2,1,0:T(8,128)(2,1)S(1)}, u32[]{:S(2)}, u32[]{:S(2)}) collective-permute-start(bf16[2,256,768]{2,1,0:T(8,128)(2,1)S(1)} %collective-permute-done.4), channel_id=1, source_target_pairs={{0,8},{8,16},{16,24},{24,28},{28,20},{20,12},{12,4},{4,0},{1,9},{9... | collective-permute-start | bytes 2359304 | tf_op jit(solution)/shard_map/ppermute | solution.py:56
  100.8 79.2 %collective-permute-start.13 = (bf16[2,192,3072]{2,1,0:T(8,128)(2,1)}, bf16[2,192,3072]{2,1,0:T(8,128)(2,1)}, u32[]{:S(2)}, u32[]{:S(2)}) collective-permute-start(bf16[2,192,3072]{2,1,0:T(8,128)(2,1)} %pad_maximum_fusion.3), channel_id=1, source_target_pairs={{0,1},{1,0},{2,3},{3,2},{4,5},{5,4},{6,7},{7,6},{8,9},{9,8},{10,11... | collective-permute-start | bytes 7077896 | tf_op jit(solution)/shard_map/ppermute | solution.py:79
  104.9 78.0 %collective-permute-start.15 = (bf16[2,768,768]{2,1,0:T(8,128)(2,1)}, bf16[2,768,768]{2,1,0:T(8,128)(2,1)}, u32[]{:S(2)}, u32[]{:S(2)}) collective-permute-start(bf16[2,768,768]{2,1,0:T(8,128)(2,1)} %pad_maximum_fusion.4), channel_id=1, source_target_pairs={{0,1},{1,0},{2,3},{3,2},{4,5},{5,4},{6,7},{7,6},{8,9},{9,8},{10,11... | collective-permute-start | bytes 7077896 | tf_op jit(solution)/shard_map/ppermute | solution.py:79
  116.3 24.3 %collective-permute-start.9 = (bf16[1,256,768]{2,1,0:T(8,128)(2,1)S(1)}, bf16[1,256,768]{2,1,0:T(8,128)(2,1)S(1)}, u32[]{:S(2)}, u32[]{:S(2)}) collective-permute-start(bf16[1,256,768]{2,1,0:T(8,128)(2,1)S(1)} %slice.204), channel_id=1, source_target_pairs={{8,0},{16,8},{24,16},{28,24},{20,28},{12,20},{4,12},{0,4},{9,1},{1... | collective-permute-start | bytes 1179656 | tf_op jit(solution)/shard_map/ppermute | solution.py:61
  117.9 22.7 %collective-permute-start.8 = (bf16[1,256,768]{2,1,0:T(8,128)(2,1)S(1)}, bf16[1,256,768]{2,1,0:T(8,128)(2,1)S(1)}, u32[]{:S(2)}, u32[]{:S(2)}) collective-permute-start(bf16[1,256,768]{2,1,0:T(8,128)(2,1)S(1)} %slice.203), channel_id=1, source_target_pairs={{0,8},{8,16},{16,24},{24,28},{28,20},{20,12},{12,4},{4,0},{1,9},{9... | collective-permute-start | bytes 1179656 | tf_op jit(solution)/shard_map/ppermute | solution.py:61
  231.8 64.2 %collective-permute-start.16 = (bf16[2,256,896]{2,1,0:T(8,128)(2,1)S(1)}, bf16[2,256,896]{2,1,0:T(8,128)(2,1)S(1)}, u32[]{:S(2)}, u32[]{:S(2)}) collective-permute-start(bf16[2,256,896]{2,1,0:T(8,128)(2,1)S(1)} %bitcast.168), channel_id=1, source_target_pairs={{0,8},{8,16},{16,24},{24,28},{28,20},{20,12},{12,4},{4,0},{1,9},{9... | collective-permute-start | bytes 2752520 | tf_op jit(solution)/shard_map/ppermute | solution.py:56
  233.4 64.1 %collective-permute-start.17 = (bf16[2,256,896]{2,1,0:T(8,128)(2,1)S(1)}, bf16[2,256,896]{2,1,0:T(8,128)(2,1)}, u32[]{:S(2)}, u32[]{:S(2)}) collective-permute-start(bf16[2,256,896]{2,1,0:T(8,128)(2,1)S(1)} %bitcast.169), channel_id=1, source_target_pairs={{8,0},{16,8},{24,16},{28,24},{20,28},{12,20},{4,12},{0,4},{9,1},{1... | collective-permute-start | bytes 2752520 | tf_op jit(solution)/shard_map/ppermute | solution.py:57
  269.3 12.4 %collective-permute-start.38 = (bf16[384,768]{1,0:T(8,128)(2,1)}, bf16[384,768]{1,0:T(8,128)(2,1)}, u32[]{:S(2)}, u32[]{:S(2)}) collective-permute-start(bf16[384,768]{1,0:T(8,128)(2,1)} %constant_dynamic-slice_fusion.25), channel_id=1, source_target_pairs={{0,1},{1,0},{2,3},{3,2},{4,5},{5,4},{6,7},{7,6},{8,9},{9,8},{10,11... | collective-permute-start | bytes 1769480 | tf_op jit(solution)/shard_map/ppermute | solution.py:91
  276.2 88.7 %collective-permute-start.52 = (bf16[384,3072]{1,0:T(8,128)(2,1)}, bf16[384,3072]{1,0:T(8,128)(2,1)}, u32[]{:S(2)}, u32[]{:S(2)}) collective-permute-start(bf16[384,3072]{1,0:T(8,128)(2,1)} %constant_dynamic-slice_fusion.17), channel_id=1, source_target_pairs={{0,1},{1,0},{2,3},{3,2},{4,5},{5,4},{6,7},{7,6},{8,9},{9,8},{10,11... | collective-permute-start | bytes 7077896 | tf_op jit(solution)/shard_map/ppermute | solution.py:91
  285.0 9.1 %collective-permute-start.39 = (bf16[192,768]{1,0:T(8,128)(2,1)}, bf16[192,768]{1,0:T(8,128)(2,1)S(1)}, u32[]{:S(2)}, u32[]{:S(2)}) collective-permute-start(bf16[192,768]{1,0:T(8,128)(2,1)} %constant_dynamic-slice_fusion.24), channel_id=1, source_target_pairs={{0,2},{1,3},{2,0},{3,1},{4,6},{5,7},{6,4},{7,5},{8,10},{9,11},{10,... | collective-permute-start | bytes 884744 | tf_op jit(solution)/shard_map/ppermute | solution.py:91
  286.8 95.2 %collective-permute-start.66 = (bf16[1536,768]{1,0:T(8,128)(2,1)}, bf16[1536,768]{1,0:T(8,128)(2,1)}, u32[]{:S(2)}, u32[]{:S(2)}) collective-permute-start(bf16[1536,768]{1,0:T(8,128)(2,1)} %constant_dynamic-slice_fusion.9), channel_id=1, source_target_pairs={{0,1},{1,0},{2,3},{3,2},{4,5},{5,4},{6,7},{7,6},{8,9},{9,8},{10,11... | collective-permute-start | bytes 7077896 | tf_op jit(solution)/shard_map/ppermute | solution.py:91
  297.6 65.2 %collective-permute-start.18 = (bf16[2,256,896]{2,1,0:T(8,128)(2,1)S(1)}, bf16[2,256,896]{2,1,0:T(8,128)(2,1)S(1)}, u32[]{:S(2)}, u32[]{:S(2)}) collective-permute-start(bf16[2,256,896]{2,1,0:T(8,128)(2,1)S(1)} %collective-permute-done.16.refs_9_.refs_17_), channel_id=1, source_target_pairs={{0,8},{8,16},{16,24},{24,28},{28,20},{20,12},{12,4},{4,0},{1,9},{9... | collective-permute-start | bytes 2752520 | tf_op jit(solution)/shard_map/ppermute | solution.py:56
  298.7 64.1 %collective-permute-start.19 = (bf16[2,256,896]{2,1,0:T(8,128)(2,1)}, bf16[2,256,896]{2,1,0:T(8,128)(2,1)S(1)}, u32[]{:S(2)}, u32[]{:S(2)}) collective-permute-start(bf16[2,256,896]{2,1,0:T(8,128)(2,1)} %collective-permute-done.17.refs_10_.refs_18_), channel_id=1, source_target_pairs={{8,0},{16,8},{24,16},{28,24},{20,28},{12,20},{4,12},{0,4},{9,1},{1... | collective-permute-start | bytes 2752520 | tf_op jit(solution)/shard_map/ppermute | solution.py:57
  301.2 18.8 %collective-permute-start.47 = (bf16[48,384]{1,0:T(8,128)(2,1)S(1)}, bf16[48,384]{1,0:T(8,128)(2,1)S(1)}, u32[]{:S(2)}, u32[]{:S(2)}) collective-permute-start(bf16[48,384]{1,0:T(8,128)(2,1)S(1)} %constant_dynamic-slice_fusion.19), channel_id=1, source_target_pairs={{0,4},{4,0},{8,12},{12,8},{16,20},{20,16},{24,28},{28,24},{1,5},{5... | collective-permute-start | bytes 110600 | tf_op jit(solution)/shard_map/ppermute | solution.py:91
  362.8 18.3 %collective-permute-start.20 = (bf16[2,256,896]{2,1,0:T(8,128)(2,1)S(1)}, bf16[2,256,896]{2,1,0:T(8,128)(2,1)S(1)}, u32[]{:S(2)}, u32[]{:S(2)}) collective-permute-start(bf16[2,256,896]{2,1,0:T(8,128)(2,1)S(1)} %collective-permute-done.18.refs_11_.refs_19_), channel_id=1, source_target_pairs={{0,8},{8,16},{16,24},{24,28},{28,20},{20,12},{12,4},{4,0},{1,9},{9... | collective-permute-start | bytes 2752520 | tf_op jit(solution)/shard_map/ppermute | solution.py:56
  362.8 16.8 %collective-permute-start.21 = (bf16[2,256,896]{2,1,0:T(8,128)(2,1)S(1)}, bf16[2,256,896]{2,1,0:T(8,128)(2,1)S(1)}, u32[]{:S(2)}, u32[]{:S(2)}) collective-permute-start(bf16[2,256,896]{2,1,0:T(8,128)(2,1)S(1)} %collective-permute-done.19.refs_12_.refs_20_), channel_id=1, source_target_pairs={{8,0},{16,8},{24,16},{28,24},{20,28},{12,20},{4,12},{0,4},{9,1},{1... | collective-permute-start | bytes 2752520 | tf_op jit(solution)/shard_map/ppermute | solution.py:57
  369.4 107.0 %collective-permute-start.53 = (bf16[192,3072]{1,0:T(8,128)(2,1)}, bf16[192,3072]{1,0:T(8,128)(2,1)}, u32[]{:S(2)}, u32[]{:S(2)}) collective-permute-start(bf16[192,3072]{1,0:T(8,128)(2,1)} %constant_dynamic-slice_fusion.16), channel_id=1, source_target_pairs={{0,2},{1,3},{2,0},{3,1},{4,6},{5,7},{6,4},{7,5},{8,10},{9,11},{10,... | collective-permute-start | bytes 3538952 | tf_op jit(solution)/shard_map/ppermute | solution.py:91
  379.7 8.5 %collective-permute-start.23 = (bf16[1,256,896]{2,1,0:T(8,128)(2,1)S(1)}, bf16[1,256,896]{2,1,0:T(8,128)(2,1)S(1)}, u32[]{:S(2)}, u32[]{:S(2)}) collective-permute-start(bf16[1,256,896]{2,1,0:T(8,128)(2,1)S(1)} %slice.215), channel_id=1, source_target_pairs={{8,0},{16,8},{24,16},{28,24},{20,28},{12,20},{4,12},{0,4},{9,1},{1... | collective-permute-start | bytes 1376264 | tf_op jit(solution)/shard_map/ppermute | solution.py:61
  385.5 96.8 %collective-permute-start.67 = (bf16[768,768]{1,0:T(8,128)(2,1)}, bf16[768,768]{1,0:T(8,128)(2,1)}, u32[]{:S(2)}, u32[]{:S(2)}) collective-permute-start(bf16[768,768]{1,0:T(8,128)(2,1)} %constant_dynamic-slice_fusion.8), channel_id=1, source_target_pairs={{0,2},{1,3},{2,0},{3,1},{4,6},{5,7},{6,4},{7,5},{8,10},{9,11},{10,... | collective-permute-start | bytes 3538952 | tf_op jit(solution)/shard_map/ppermute | solution.py:91
  429.0 113.4 %collective-permute-start.24 = (bf16[384,2304]{1,0:T(8,128)(2,1)}, bf16[384,2304]{1,0:T(8,128)(2,1)}, u32[]{:S(2)}, u32[]{:S(2)}) collective-permute-start(bf16[384,2304]{1,0:T(8,128)(2,1)} %constant_dynamic-slice_fusion.33), channel_id=1, source_target_pairs={{0,1},{1,0},{2,3},{3,2},{4,5},{5,4},{6,7},{7,6},{8,9},{9,8},{10,11... | collective-permute-start | bytes 5308424 | tf_op jit(solution)/shard_map/ppermute | solution.py:91
  478.2 9.2 %collective-permute-start.60 = (bf16[96,1536]{1,0:T(8,128)(2,1)S(1)}, bf16[96,1536]{1,0:T(8,128)(2,1)S(1)}, u32[]{:S(2)}, u32[]{:S(2)}) collective-permute-start(bf16[96,1536]{1,0:T(8,128)(2,1)S(1)} %constant_dynamic-slice_fusion.12), channel_id=1, source_target_pairs={{0,8},{4,12},{8,0},{12,4},{16,24},{20,28},{24,16},{28,20},{1,9},{5... | collective-permute-start | bytes 884744 | tf_op jit(solution)/shard_map/ppermute | solution.py:91
  479.9 10.7 %collective-permute-start.54 = (bf16[96,1536]{1,0:T(8,128)(2,1)S(1)}, bf16[96,1536]{1,0:T(8,128)(2,1)S(1)}, u32[]{:S(2)}, u32[]{:S(2)}) collective-permute-start(bf16[96,1536]{1,0:T(8,128)(2,1)S(1)} %constant_dynamic-slice_fusion.15), channel_id=1, source_target_pairs={{0,4},{4,0},{8,12},{12,8},{16,20},{20,16},{24,28},{28,24},{1,5},{5... | collective-permute-start | bytes 884744 | tf_op jit(solution)/shard_map/ppermute | solution.py:91
  484.1 10.0 %collective-permute-start.74 = (bf16[384,384]{1,0:T(8,128)(2,1)S(1)}, bf16[384,384]{1,0:T(8,128)(2,1)S(1)}, u32[]{:S(2)}, u32[]{:S(2)}) collective-permute-start(bf16[384,384]{1,0:T(8,128)(2,1)S(1)} %constant_dynamic-slice_fusion.4), channel_id=1, source_target_pairs={{0,8},{4,12},{8,0},{12,4},{16,24},{20,28},{24,16},{28,20},{1,9},{5... | collective-permute-start | bytes 884744 | tf_op jit(solution)/shard_map/ppermute | solution.py:91
  484.5 12.0 %collective-permute-start.68 = (bf16[384,384]{1,0:T(8,128)(2,1)S(1)}, bf16[384,384]{1,0:T(8,128)(2,1)S(1)}, u32[]{:S(2)}, u32[]{:S(2)}) collective-permute-start(bf16[384,384]{1,0:T(8,128)(2,1)S(1)} %constant_dynamic-slice_fusion.7), channel_id=1, source_target_pairs={{0,4},{4,0},{8,12},{12,8},{16,20},{20,16},{24,28},{28,24},{1,5},{5... | collective-permute-start | bytes 884744 | tf_op jit(solution)/shard_map/ppermute | solution.py:91
  487.5 11.8 %collective-permute-start.61 = (bf16[48,1536]{1,0:T(8,128)(2,1)S(1)}, bf16[48,1536]{1,0:T(8,128)(2,1)S(1)}, u32[]{:S(2)}, u32[]{:S(2)}) collective-permute-start(bf16[48,1536]{1,0:T(8,128)(2,1)S(1)} %constant_dynamic-slice_fusion.11), channel_id=1, source_target_pairs={{0,4},{4,0},{8,12},{12,8},{16,20},{20,16},{24,28},{28,24},{1,5},{5... | collective-permute-start | bytes 442376 | tf_op jit(solution)/shard_map/ppermute | solution.py:91
  490.8 9.5 %collective-permute-start.55 = (bf16[48,1536]{1,0:T(8,128)(2,1)S(1)}, bf16[48,1536]{1,0:T(8,128)(2,1)S(1)}, u32[]{:S(2)}, u32[]{:S(2)}) collective-permute-start(bf16[48,1536]{1,0:T(8,128)(2,1)S(1)} %constant_dynamic-slice_fusion.14), channel_id=1, source_target_pairs={{0,8},{4,12},{8,0},{12,4},{16,24},{20,28},{24,16},{28,20},{1,9},{5... | collective-permute-start | bytes 442376 | tf_op jit(solution)/shard_map/ppermute | solution.py:91
  499.3 12.6 %collective-permute-start.62 = (bf16[24,1536]{1,0:T(8,128)(2,1)S(1)}, bf16[24,1536]{1,0:T(8,128)(2,1)S(1)}, u32[]{:S(2)}, u32[]{:S(2)}) collective-permute-start(bf16[24,1536]{1,0:T(8,128)(2,1)S(1)} %constant_dynamic-slice_fusion.10), channel_id=1, source_target_pairs={{0,16},{4,20},{8,24},{12,28},{16,0},{20,4},{24,8},{28,12},{1,17},{... | collective-permute-start | bytes 221192 | tf_op jit(solution)/shard_map/ppermute | solution.py:91
  500.3 13.2 %collective-permute-start.56 = (bf16[24,1536]{1,0:T(8,128)(2,1)S(1)}, bf16[24,1536]{1,0:T(8,128)(2,1)S(1)}, u32[]{:S(2)}, u32[]{:S(2)}) collective-permute-start(bf16[24,1536]{1,0:T(8,128)(2,1)S(1)} %constant_dynamic-slice_fusion.13), channel_id=1, source_target_pairs={{0,16},{4,20},{8,24},{12,28},{16,0},{20,4},{24,8},{28,12},{1,17},{... | collective-permute-start | bytes 221192 | tf_op jit(solution)/shard_map/ppermute | solution.py:91
  502.5 14.1 %collective-permute-start.76 = (bf16[96,384]{1,0:T(8,128)(2,1)S(1)}, bf16[96,384]{1,0:T(8,128)(2,1)S(1)}, u32[]{:S(2)}, u32[]{:S(2)}) collective-permute-start(bf16[96,384]{1,0:T(8,128)(2,1)S(1)} %constant_dynamic-slice_fusion.2), channel_id=1, source_target_pairs={{0,16},{4,20},{8,24},{12,28},{16,0},{20,4},{24,8},{28,12},{1,17},{... | collective-permute-start | bytes 221192 | tf_op jit(solution)/shard_map/ppermute | solution.py:91
  503.6 14.6 %collective-permute-start.70 = (bf16[96,384]{1,0:T(8,128)(2,1)S(1)}, bf16[96,384]{1,0:T(8,128)(2,1)S(1)}, u32[]{:S(2)}, u32[]{:S(2)}) collective-permute-start(bf16[96,384]{1,0:T(8,128)(2,1)S(1)} %constant_dynamic-slice_fusion.5), channel_id=1, source_target_pairs={{0,16},{4,20},{8,24},{12,28},{16,0},{20,4},{24,8},{28,12},{1,17},{... | collective-permute-start | bytes 221192 | tf_op jit(solution)/shard_map/ppermute | solution.py:91
  511.9 8.9 %collective-permute-start.63 = (bf16[24,1536]{1,0:T(8,128)(2,1)S(1)}, bf16[24,1536]{1,0:T(8,128)(2,1)S(1)}, u32[]{:S(2)}, u32[]{:S(2)}) collective-permute-start(bf16[24,1536]{1,0:T(8,128)(2,1)S(1)} %add_convert_fusion.25), channel_id=1, source_target_pairs={{0,16},{4,20},{8,24},{12,28},{16,0},{20,4},{24,8},{28,12},{1,17},{... | collective-permute-start | bytes 221192 | tf_op jit(solution)/shard_map/ppermute | solution.py:98
  513.5 9.6 %collective-permute-start.57 = (bf16[24,1536]{1,0:T(8,128)(2,1)S(1)}, bf16[24,1536]{1,0:T(8,128)(2,1)S(1)}, u32[]{:S(2)}, u32[]{:S(2)}) collective-permute-start(bf16[24,1536]{1,0:T(8,128)(2,1)S(1)} %add_convert_fusion.26), channel_id=1, source_target_pairs={{0,16},{4,20},{8,24},{12,28},{16,0},{20,4},{24,8},{28,12},{1,17},{... | collective-permute-start | bytes 221192 | tf_op jit(solution)/shard_map/ppermute | solution.py:98
  523.2 10.7 %collective-permute-start.58 = (bf16[48,1536]{1,0:T(8,128)(2,1)S(1)}, bf16[48,1536]{1,0:T(8,128)(2,1)S(1)}, u32[]{:S(2)}, u32[]{:S(2)}) collective-permute-start(bf16[48,1536]{1,0:T(8,128)(2,1)S(1)} %pad_maximum_fusion.17), channel_id=1, source_target_pairs={{0,8},{4,12},{8,0},{12,4},{16,24},{20,28},{24,16},{28,20},{1,9},{5... | collective-permute-start | bytes 442376 | tf_op jit(solution)/shard_map/ppermute | solution.py:98
  526.2 16.1 %collective-permute-start.65 = (bf16[96,1536]{1,0:T(8,128)(2,1)S(1)}, bf16[96,1536]{1,0:T(8,128)(2,1)S(1)}, u32[]{:S(2)}, u32[]{:S(2)}) collective-permute-start(bf16[96,1536]{1,0:T(8,128)(2,1)S(1)} %pad_maximum_fusion.12), channel_id=1, source_target_pairs={{0,8},{4,12},{8,0},{12,4},{16,24},{20,28},{24,16},{28,20},{1,9},{5... | collective-permute-start | bytes 884744 | tf_op jit(solution)/shard_map/ppermute | solution.py:98
  529.4 12.7 %collective-permute-start.79 = (bf16[384,384]{1,0:T(8,128)(2,1)S(1)}, bf16[384,384]{1,0:T(8,128)(2,1)S(1)}, u32[]{:S(2)}, u32[]{:S(2)}) collective-permute-start(bf16[384,384]{1,0:T(8,128)(2,1)S(1)} %pad_maximum_fusion.14), channel_id=1, source_target_pairs={{0,8},{4,12},{8,0},{12,4},{16,24},{20,28},{24,16},{28,20},{1,9},{5... | collective-permute-start | bytes 884744 | tf_op jit(solution)/shard_map/ppermute | solution.py:98
  533.3 8.9 %collective-permute-start.73 = (bf16[384,384]{1,0:T(8,128)(2,1)S(1)}, bf16[384,384]{1,0:T(8,128)(2,1)S(1)}, u32[]{:S(2)}, u32[]{:S(2)}) collective-permute-start(bf16[384,384]{1,0:T(8,128)(2,1)S(1)} %pad_maximum_fusion.13), channel_id=1, source_target_pairs={{0,4},{4,0},{8,12},{12,8},{16,20},{20,16},{24,28},{28,24},{1,5},{5... | collective-permute-start | bytes 884744 | tf_op jit(solution)/shard_map/ppermute | solution.py:98
  534.0 13.4 %collective-permute-start.59 = (bf16[96,1536]{1,0:T(8,128)(2,1)S(1)}, bf16[96,1536]{1,0:T(8,128)(2,1)S(1)}, u32[]{:S(2)}, u32[]{:S(2)}) collective-permute-start(bf16[96,1536]{1,0:T(8,128)(2,1)S(1)} %pad_maximum_fusion.11), channel_id=1, source_target_pairs={{0,4},{4,0},{8,12},{12,8},{16,20},{20,16},{24,28},{28,24},{1,5},{5... | collective-permute-start | bytes 884744 | tf_op jit(solution)/shard_map/ppermute | solution.py:98
  544.5 18.1 %collective-permute-start.25 = (bf16[192,2304]{1,0:T(8,128)(2,1)S(1)}, bf16[192,2304]{1,0:T(8,128)(2,1)S(1)}, u32[]{:S(2)}, u32[]{:S(2)}) collective-permute-start(bf16[192,2304]{1,0:T(8,128)(2,1)S(1)} %constant_dynamic-slice_fusion.32), channel_id=1, source_target_pairs={{0,2},{1,3},{2,0},{3,1},{4,6},{5,7},{6,4},{7,5},{8,10},{9,11},{10,... | collective-permute-start | bytes 2654216 | tf_op jit(solution)/shard_map/ppermute | solution.py:91
  (97 other events, 942.8 us)

commit v2 on v1

v2 whole, which is shorter than its diff:
```python
import functools
import math

import jax
import jax.numpy as jnp
from jax import lax
from jax.experimental import pallas as pl
from jax.experimental.pallas import tpu as pltpu
from jax.sharding import PartitionSpec as P

HEAD_DIM = 64
LANES = 128
EPS = 1e-12
SCALE = 0.125
LOG2E = math.log2(math.e)
COEF = SCALE * LOG2E
MASKED = -1e30
SAFE = 60.0
LOWEST = -1e9
MASK_LANE = 127
CORR_LANE = 36
VMEM = 48 * 1024 * 1024

f32 = jnp.float32
b16 = jnp.bfloat16


def together(*values):
    return lax.optimization_barrier(values)


def swap(x, axis, bit):
    count = lax.axis_size(axis)
    return lax.ppermute(x, axis, [(i, i ^ bit) for i in range(count)])


def bits_of(count):
    return [1 << k for k in range(count.bit_length() - 1)]


def ring_order(count):
    half = count // 2
    return [2 * p if p < half else 2 * (count - 1 - p) + 1 for p in range(count)]


def ring_slots(axis):
    count = lax.axis_size(axis)
    order = jnp.asarray(ring_order(count), jnp.int32)
    place = lax.axis_index(axis)
    spot = jnp.where(place % 2 == 0, place // 2, count - 1 - place // 2)
    steps = [0]
    for s in range(1, count // 2):
        steps += [-s, s]
    steps.append(count // 2)
    return order[jnp.mod(spot + jnp.asarray(steps, jnp.int32), count)]


def ring_step(r, l, axis):
    count = lax.axis_size(axis)
    order = ring_order(count)
    right = [(order[p], order[(p + 1) % count]) for p in range(count)]
    left = [(d, s) for s, d in right]
    return lax.ppermute(r, axis, right), lax.ppermute(l, axis, left)


def ring_last(r, l, axis):
    return ring_step(r[:1], l[1:], axis)


def across(w, axis):
    blocks = {0: w}
    for bit in bits_of(lax.axis_size(axis))[1:]:
        blocks |= {k ^ bit: swap(v, axis, bit) for k, v in list(blocks.items())}
    return blocks


def between(blocks, axis):
    keys = list(blocks)
    got = swap(jnp.stack([blocks[k] for k in keys]), axis, 1)
    return blocks | {k ^ 1: got[i] for i, k in enumerate(keys)}


def in_order(blocks, axis):
    i = lax.axis_index(axis)
    count = lax.axis_size(axis)
    now = [blocks[k] for k in range(count)]
    for bit in bits_of(count):
        low = (i // bit) % 2 == 0
        now = [jnp.where(low, now[k], now[k ^ bit]) for k in range(count)]
    return jnp.concatenate(now, 0)


def added(keep, got):
    return (keep.astype(f32) + got.astype(f32)).astype(b16)


def core_parts(g):
    core = lax.axis_index("fsdp") % 2
    pairs = g.reshape((-1, 2) + g.shape[1:])
    send = lax.dynamic_index_in_dim(pairs, 1 - core, 1, keepdims=False)
    keep = lax.dynamic_index_in_dim(pairs, core, 1, keepdims=False)
    return send, keep


def chip_sum(x):
    bits = bits_of(lax.axis_size("fsdp"))[1:]
    for bit in bits[::-1]:
        upper = (lax.axis_index("fsdp") // bit) % 2
        pairs = x.reshape((2, -1) + x.shape[1:])
        send = lax.dynamic_index_in_dim(pairs, 1 - upper, 0, keepdims=False)
        keep = lax.dynamic_index_in_dim(pairs, upper, 0, keepdims=False)
        x = added(keep, swap(send, "fsdp", bit))
    return x[0]


def halve(x, axis, bit):
    upper = (lax.axis_index(axis) // bit) % 2
    half = x.shape[0] // 2
    send = lax.dynamic_slice_in_dim(x, (1 - upper) * half, half, 0)
    keep = lax.dynamic_slice_in_dim(x, upper * half, half, 0)
    return added(keep, swap(send, axis, bit))


def unhalve(x, axis, bit):
    low = (lax.axis_index(axis) // bit) % 2 == 0
    other = swap(x, axis, bit)
    return jnp.concatenate([jnp.where(low, x, other), jnp.where(low, other, x)], 0)


def block_sum_steps(blocks):
    first = bits_of(blocks)
    second = [first[1], first[0]] + first[2:]

    def down(k):
        return lambda ab: (halve(ab[0], "ctx", first[k]), halve(ab[1], "ctx", second[k]))

    def up(k):
        return lambda ab: (unhalve(ab[0], "ctx", first[k]), unhalve(ab[1], "ctx", second[k]))

    count = len(first)
    return [down(k) for k in range(count)] + [up(k) for k in range(count)][::-1]


def columns_to_rows(x, width):
    return jnp.concatenate(
        [x[..., k * width : (k + 1) * width] for k in range(x.shape[-1] // width)], axis=-2
    )


def rows_to_columns(x, count):
    rows = x.shape[0] // count
    return jnp.concatenate([x[k * rows : (k + 1) * rows] for k in range(count)], axis=1)


def row_pad(rows, blocks):
    unit = 8 * blocks
    return -rows % unit


def dot_nt(a, b):
    return lax.dot_general(a, b, (((1,), (1,)), ((), ())), preferred_element_type=f32)


def dot_nn(a, b):
    return lax.dot_general(a, b, (((1,), (0,)), ((), ())), preferred_element_type=f32)


def lane_iota(rows):
    return lax.broadcasted_iota(jnp.int32, (rows, LANES), 1)


def split3(x):
    hi = x.astype(b16)
    rest = x - hi.astype(f32)
    mid = rest.astype(b16)
    low = (rest - mid.astype(f32)).astype(b16)
    return hi, mid, low


def place3(x, lane, at):
    hi, mid, low = (p.astype(f32) for p in split3(x))
    zero = jnp.zeros_like(x)
    return jnp.where(
        lane == at, hi, jnp.where(lane == at + 1, mid, jnp.where(lane == at + 2, low, zero))
    )


def stack_heads(pair):
    rows = pair.shape[0]
    lane = lane_iota(rows)
    zero = jnp.zeros_like(pair)
    return jnp.concatenate(
        [jnp.where(lane < HEAD_DIM, pair, zero), jnp.where(lane >= HEAD_DIM, pair, zero)], 0
    )


def join_heads(x):
    rows = x.shape[0] // 2
    return jnp.where(lane_iota(rows) < HEAD_DIM, x[:rows], x[rows:])


def key_extra(rows, base, length):
    lane = lane_iota(rows)
    dead = base + lax.broadcasted_iota(jnp.int32, (rows, LANES), 0) >= length
    mask = jnp.where(dead, MASKED, 0.0)
    return jnp.where(lane == MASK_LANE, mask, -1.0).astype(b16)


def spread_heads(x):
    rows = x.shape[0]
    lane = lane_iota(rows)
    other = pltpu.roll(x, HEAD_DIM, 1)
    return jnp.concatenate(
        [jnp.where(lane < HEAD_DIM, x, other), jnp.where(lane < HEAD_DIM, other, x)], 0
    )


def pair_columns(pair):
    return pl.ds(pl.multiple_of(pair * LANES, LANES), LANES)


def forward_kernel(slots, begin, final, bases, lengths, safe, q_ref, *refs):
    k_refs, v_refs = refs[:slots], refs[slots : 2 * slots]
    refs = refs[2 * slots :]
    if not begin:
        numer_in, sums_in, level_in = refs[:3]
        refs = refs[3:]
    if final:
        out_ref, extra_ref, level_ref, lanes_ref, meet_ref = refs
    else:
        numer_out, sums_out, level_out, level_ref, lanes_ref, meet_ref = refs
    seq = pl.program_id(0)
    length = lengths[seq]
    rows = q_ref.shape[1]
    block = k_refs[0].shape[1]
    pairs = q_ref.shape[2] // LANES
    lane2 = lane_iota(2 * rows)
    lane = lane_iota(rows)
    onehot = jnp.where(lane2 == MASK_LANE, 1.0, 0.0)
    for s in range(slots):
        meet_ref[s] = key_extra(block, bases[s], length)
    if final:
        extra_ref[0] = jnp.where(lane == MASK_LANE, 1.0, 0.0)

    def one_pair(pair, carry):
        cols = pair_columns(pair)
        stacked = stack_heads(q_ref[0, :, cols])
        level_ref[...] = jnp.zeros_like(level_ref)
        lanes_ref[...] = onehot.astype(b16)

        @pl.when(safe[seq * pairs + pair] == 0)
        def _():
            top = jnp.full((2 * rows, 1), MASKED, f32)
            probe = jnp.concatenate([stacked, onehot.astype(b16)], 1)
            for s in range(slots):
                scores = dot_nt(probe, jnp.concatenate([k_refs[s][0, :, cols], meet_ref[s]], 1))
                top = jnp.maximum(top, jnp.max(scores, axis=1, keepdims=True))
            before = LOWEST if begin else spread_heads(level_in[0, :, cols])
            level = jnp.maximum(before, jnp.ceil(top * COEF))
            lanes_ref[...] = (place3(level / COEF, lane2, 0) + onehot).astype(b16)
            level_ref[...] = join_heads(jnp.broadcast_to(level, (2 * rows, LANES)))

        query = jnp.concatenate([stacked, lanes_ref[...]], 1)
        ones = jnp.ones((block, LANES), b16)
        total = jnp.zeros((2 * rows, 2 * LANES), f32)
        for s in range(slots):
            scores = dot_nt(query, jnp.concatenate([k_refs[s][0, :, cols], meet_ref[s]], 1))
            weights = jnp.exp2(scores * COEF).astype(b16)
            total = total + dot_nn(weights, jnp.concatenate([v_refs[s][0, :, cols], ones], 1))
        numer, sums, now = join_heads(total[:, :LANES]), join_heads(total[:, LANES:]), level_ref[...]
        if not begin:
            factor = jnp.exp2(level_in[0, :, cols] - now)
            numer = numer + numer_in[0, :, cols] * factor
            sums = sums + sums_in[0, :, cols] * factor
        if not final:
            numer_out[0, :, cols] = numer
            sums_out[0, :, cols] = sums
            level_out[0, :, cols] = now
            return carry
        out_ref[0, :, cols] = numer / sums
        whole = spread_heads((now + jnp.log2(sums)) / COEF)
        extra_ref[0] += place3(whole[:rows], lane, 6 * pair) + place3(
            whole[rows:], lane, 6 * pair + 3
        )
        return carry

    lax.fori_loop(0, pairs, one_pair, 0)


def corr_kernel(grad_ref, value_ref, extra_ref, out_ref):
    width = grad_ref.shape[1]
    grad = grad_ref[...]
    feature = lax.broadcasted_iota(jnp.int32, (width, LANES), 0) // HEAD_DIM
    lane = lax.broadcasted_iota(jnp.int32, (width, LANES), 1)
    pick = jnp.where(
        (lane >= CORR_LANE) & (feature == (lane - CORR_LANE) // 3), 1.0, 0.0
    ).astype(b16)
    corr = sum(dot_nn(p, pick) for p in split3(grad * value_ref[...]))
    rows = grad.shape[0]
    lane = lane_iota(rows)
    hi, mid, low = (p.astype(f32) for p in split3(corr))
    part = lax.rem(lane, 3)
    placed = jnp.where(part == 0, hi, jnp.where(part == 1, mid, low))
    inside = (lane >= CORR_LANE) & (lane < CORR_LANE + 3 * (width // HEAD_DIM))
    out_ref[:, :width] = grad.astype(b16)
    out_ref[:, width:] = (extra_ref[...] + jnp.where(inside, placed, 0.0)).astype(b16)


def keep_lanes(x, lane, at):
    return jnp.where((lane >= at) & (lane < at + 3), x, jnp.zeros_like(x))


def query_kernel(slots, bases, lengths, q_ref, grad_ref, extra_ref, *refs):
    k_refs, v_refs = refs[:slots], refs[slots : 2 * slots]
    out_ref, meet_ref = refs[2 * slots :]
    seq = pl.program_id(0)
    length = lengths[seq]
    block = k_refs[0].shape[1]
    rows = q_ref.shape[1]
    lane = lane_iota(rows)
    onehot = jnp.where(lane == MASK_LANE, 1.0, 0.0).astype(b16)
    for s in range(slots):
        meet_ref[s] = key_extra(block, bases[s], length)

    def one_pair(pair, carry):
        cols = pair_columns(pair)
        extra = extra_ref[0]
        levels = [keep_lanes(extra, lane, 6 * pair + 3 * h) + onehot for h in range(2)]
        corrs = [keep_lanes(extra, lane, CORR_LANE + 6 * pair + 3 * h) for h in range(2)]
        query = jnp.concatenate([stack_heads(q_ref[0, :, cols]), jnp.concatenate(levels, 0)], 1)
        grad = jnp.concatenate([stack_heads(grad_ref[0, :, cols]), jnp.concatenate(corrs, 0)], 1)
        total = jnp.zeros((2 * rows, LANES), f32)
        for s in range(slots):
            meet = meet_ref[s]
            keys = k_refs[s][0, :, cols]
            weights = jnp.exp2(dot_nt(query, jnp.concatenate([keys, meet], 1)) * COEF)
            terms = dot_nt(grad, jnp.concatenate([v_refs[s][0, :, cols], meet], 1))
            total = total + dot_nn((weights * terms).astype(b16), keys)
        out_ref[0, :, cols] = (join_heads(total) * SCALE).astype(b16)
        return carry

    lax.fori_loop(0, q_ref.shape[2] // LANES, one_pair, 0)


def key_kernel(slots, begin, final, place, lengths, k_ref, v_ref, *refs):
    q_refs, g_refs, e_refs = refs[:slots], refs[slots : 2 * slots], refs[2 * slots : 3 * slots]
    refs = refs[3 * slots :]
    if not begin:
        dk_in, dv_in = refs[:2]
        refs = refs[2:]
    dk_ref, dv_ref = refs
    length = lengths[pl.program_id(0)]
    rows = k_ref.shape[1]
    lane = lane_iota(rows)
    dead = place[0] * rows + lax.broadcasted_iota(jnp.int32, (rows, LANES), 0) >= length
    mask = jnp.where((lane == MASK_LANE) & dead, MASKED, 0.0)
    minus = jnp.full((rows, LANES), -1.0, f32)

    def one_pair(pair, carry):
        cols = pair_columns(pair)
        levels = [(keep_lanes(minus, lane, 6 * pair + 3 * h) + mask).astype(b16) for h in range(2)]
        corrs = [
            keep_lanes(minus, lane, CORR_LANE + 6 * pair + 3 * h).astype(b16) for h in range(2)
        ]
        keys = jnp.concatenate([stack_heads(k_ref[0, :, cols]), jnp.concatenate(levels, 0)], 1)
        values = jnp.concatenate([stack_heads(v_ref[0, :, cols]), jnp.concatenate(corrs, 0)], 1)
        dkeys = jnp.zeros((2 * rows, LANES), f32)
        dvalues = jnp.zeros((2 * rows, LANES), f32)
        for s in range(slots):
            query, grad, extra = q_refs[s][0, :, cols], g_refs[s][0, :, cols], e_refs[s][0]
            weights = jnp.exp2(dot_nt(keys, jnp.concatenate([query, extra], 1)) * COEF)
            terms = dot_nt(values, jnp.concatenate([grad, extra], 1))
            dvalues = dvalues + dot_nn(weights.astype(b16), grad)
            dkeys = dkeys + dot_nn((weights * terms).astype(b16), query)
        dk, dv = join_heads(dkeys) * SCALE, join_heads(dvalues)
        if not begin:
            dk, dv = dk + dk_in[0, :, cols], dv + dv_in[0, :, cols]
        dk_ref[0, :, cols] = dk.astype(dk_ref.dtype)
        dv_ref[0, :, cols] = dv.astype(dv_ref.dtype)
        return carry

    lax.fori_loop(0, k_ref.shape[2] // LANES, one_pair, 0)


def third(block, width, which, seq_at=0):
    return pl.BlockSpec((1, block, width), lambda seq, *_: (seq_at + seq, 0, which))


def lanes_spec(block, at, seq_at=0):
    return pl.BlockSpec((1, block, LANES), lambda seq, *_: (seq_at + seq, 0, at))


def cost(matmuls, seqs, block, slots, width):
    return pl.CostEstimate(
        flops=8 * matmuls * seqs * block * block * slots * width,
        bytes_accessed=slots * seqs * block * width * 4,
        transcendentals=0,
    )


def attend_forward(own, slots_qkv, bases, lengths, safe, state=(), final=False):
    slots = len(slots_qkv)
    seqs, block, triple = own.shape
    width = triple // 3
    q, k, v = (third(block, width, n) for n in range(3))
    part = jax.ShapeDtypeStruct((seqs, block, width), f32)
    if final:
        shapes = [part, jax.ShapeDtypeStruct((seqs, block, LANES), f32)]
        outs = [q, lanes_spec(block, 0)]
    else:
        shapes, outs = [part] * 3, [q] * 3
    return pl.pallas_call(
        functools.partial(forward_kernel, slots, not state, final),
        grid_spec=pltpu.PrefetchScalarGridSpec(
            num_scalar_prefetch=3,
            grid=(seqs,),
            in_specs=[q] + [k] * slots + [v] * slots + [q] * len(state),
            out_specs=outs,
            scratch_shapes=[
                pltpu.VMEM((block, LANES), f32),
                pltpu.VMEM((2 * block, LANES), b16),
                pltpu.VMEM((slots, block, LANES), b16),
            ],
        ),
        out_shape=shapes,
        compiler_params=pltpu.CompilerParams(vmem_limit_bytes=VMEM),
        cost_estimate=cost(2, seqs, block, slots, width),
    )(bases, lengths, safe, own, *slots_qkv, *slots_qkv, *state)


def attend_query(seq_at, count, slots_qkv, grads, bases, lengths):
    slots = len(slots_qkv)
    block, triple = slots_qkv[0].shape[1:]
    width = triple // 3
    q, k, v = (third(block, width, n, seq_at) for n in range(3))
    return pl.pallas_call(
        functools.partial(query_kernel, slots),
        grid_spec=pltpu.PrefetchScalarGridSpec(
            num_scalar_prefetch=2,
            grid=(count,),
            in_specs=[q, q, lanes_spec(block, width // LANES, seq_at)]
            + [k] * slots
            + [v] * slots,
            out_specs=third(block, width, 0),
            scratch_shapes=[pltpu.VMEM((slots, block, LANES), b16)],
        ),
        out_shape=jax.ShapeDtypeStruct((count, block, width), b16),
        compiler_params=pltpu.CompilerParams(vmem_limit_bytes=VMEM),
        cost_estimate=cost(3, count, block, slots, width),
    )(bases, lengths[seq_at : seq_at + count], slots_qkv[0], grads, grads, *slots_qkv, *slots_qkv)


def attend_keys(own, slots_qkv, slots_grads, place, lengths, state=(), final=False):
    slots = len(slots_qkv)
    seqs, block, triple = own.shape
    width = triple // 3
    q, k, v = (third(block, width, n) for n in range(3))
    shape = jax.ShapeDtypeStruct((seqs, block, width), b16 if final else f32)
    return pl.pallas_call(
        functools.partial(key_kernel, slots, not state, final),
        grid_spec=pltpu.PrefetchScalarGridSpec(
            num_scalar_prefetch=2,
            grid=(seqs,),
            in_specs=[k, v]
            + [q] * (2 * slots)
            + [lanes_spec(block, width // LANES)] * slots
            + [q] * len(state),
            out_specs=[q, q],
        ),
        out_shape=[shape, shape],
        compiler_params=pltpu.CompilerParams(vmem_limit_bytes=VMEM),
        cost_estimate=cost(4, seqs, block, slots, width),
    )(place, lengths, own, own, *slots_qkv, *slots_grads, *slots_grads, *state)


def place_corr(dattended, attended, extra):
    rows, width = dattended.shape
    return pl.pallas_call(
        corr_kernel,
        out_shape=jax.ShapeDtypeStruct((rows, width + LANES), b16),
        compiler_params=pltpu.CompilerParams(vmem_limit_bytes=VMEM),
    )(dattended, attended, extra)


def layer_norm(value, gain, shift):
    mean = jnp.mean(value, axis=-1, keepdims=True)
    centred = value - mean
    spread = jnp.mean(centred * centred, axis=-1, keepdims=True)
    return centred * lax.rsqrt(spread + EPS) * gain + shift


def gelu_exact(value):
    return jax.nn.gelu(value, approximate=False)


def largest_norm(rows3):
    seqs, block, width = rows3.shape
    heads = width // HEAD_DIM
    pick = (jnp.arange(width)[:, None] // HEAD_DIM == jnp.arange(heads)[None]).astype(b16)
    squares = rows3.astype(f32)
    squares = (squares * squares).astype(b16)
    sums = jnp.einsum("sbw,wh->sbh", squares, pick, preferred_element_type=f32)
    return jnp.max(sums, axis=1)


def per_device(
    tokens,
    lengths,
    attend_weight,
    query_bias,
    value_bias,
    mixing_weight,
    mixing_bias,
    first_gain,
    first_shift,
    up_weight,
    up_bias,
    down_weight,
    down_bias,
    second_gain,
    second_shift,
    cotangent,
):
    seqs, block, width = tokens.shape
    rows = seqs * block
    owners = lax.axis_size("fsdp")
    blocks = lax.axis_size("ctx")
    place = lax.axis_index("ctx")
    share = width // owners
    steps = blocks // 2

    flat = tokens.reshape(rows, width)
    flat_low = flat.astype(b16)
    own_tokens = flat_low.reshape(seqs, block, width)

    small = jnp.concatenate(
        [query_bias, value_bias, mixing_bias, first_gain, first_shift, down_bias,
         second_gain, second_shift, up_bias]
    )
    small_rows = -(-small.shape[0] // (16 * width)) * 16
    small = jnp.pad(small, (0, small_rows * width - small.shape[0])).reshape(small_rows, width)
    mixing_more = jnp.concatenate([mixing_weight, small], 0)

    spots = ring_slots("ctx")
    bases = spots * block

    def pick(blocks_at):
        keys = list(blocks_at)
        return keys, [blocks_at[k] for k in keys]

    tr, tl = ring_step(own_tokens, own_tokens, "ctx")
    keys, got = pick(across(attend_weight, "fsdp"))
    tr, tl, mixing_more, up_weight, *got = together(tr, tl, mixing_more, up_weight, *got)
    attend_blocks = dict(zip(keys, got))
    token_slots = [own_tokens, tr, tl]

    def project(t):
        out = jnp.dot(t.reshape(rows, width), attend_full, preferred_element_type=f32) + bias
        return out.astype(b16).reshape(seqs, block, 3 * width)

    attend_blocks = between(attend_blocks, "fsdp")
    tr, tl = ring_step(tr, tl, "ctx")
    _, mixing_got = pick(across(mixing_more, "fsdp"))
    _, up_got = pick(across(up_weight, "fsdp"))
    attend_full = in_order(attend_blocks, "fsdp")
    tr, tl, attend_full, *mixing_got = together(tr, tl, attend_full, *mixing_got)
    token_slots += [tr, tl]

    mixing_blocks = between(dict(zip(keys, mixing_got)), "fsdp")
    mixing_all = in_order(mixing_blocks, "fsdp").reshape(owners, share + small_rows, width)
    mixing_full = mixing_all[:, :share].reshape(width, width)
    small_full = mixing_all[:, share:].reshape(owners, -1).astype(f32)
    vectors = small_full[:, : 8 * share].reshape(owners, 8, share).transpose(1, 0, 2)
    vectors = vectors.reshape(8, width)
    qbias, vbias, mixbias, fgain, fshift, downbias, sgain, sshift = (
        vectors[k : k + 1] for k in range(8)
    )
    upbias = small_full[:, 8 * share : 8 * share + up_bias.shape[0]].reshape(1, -1)
    bias = jnp.concatenate([qbias, jnp.zeros_like(qbias), vbias], 1)

    def flags(query_norm, slots):
        norm = functools.reduce(
            jnp.maximum, [largest_norm(v[..., width : 2 * width]) for v in slots]
        )
        bound = jnp.sqrt(norm * query_norm) * COEF
        return jnp.all(bound.reshape(seqs, -1, 2) < SAFE, axis=-1).reshape(-1)

    slots_qkv = []
    for step in range(3, steps + 1):
        last = step == steps
        nr, nl = ring_last(tr, tl, "ctx") if last else ring_step(tr, tl, "ctx")
        slots_qkv += [project(t) for t in token_slots[len(slots_qkv) : 2 * step - 1]]
        if last:
            _, down_got = pick(across(down_weight, "fsdp"))
            up_blocks = between(dict(zip(keys, up_got)), "fsdp")
            query_norm = largest_norm(slots_qkv[0][..., :width])
            safe = flags(query_norm, slots_qkv)
            state = attend_forward(
                slots_qkv[0], slots_qkv, bases[: len(slots_qkv)], lengths, safe.astype(jnp.int32)
            )
            tr, tl, *state = together(nr, nl, *state)
            token_slots.append(jnp.concatenate([tr, tl], 0))
        else:
            tr, tl, down_weight, *rest = together(nr, nl, down_weight, *up_got, *slots_qkv)
            up_got, slots_qkv = rest[: len(up_got)], rest[len(up_got) :]
            token_slots += [tr, tl]
    done = len(slots_qkv)
    slots_qkv += [project(t) for t in token_slots[done:]]
    safe &= flags(query_norm, slots_qkv[done:])
    attended3, extra = attend_forward(
        slots_qkv[0], slots_qkv[done:], bases[done:], lengths, safe.astype(jnp.int32),
        tuple(state), True,
    )
    up_full = in_order(up_blocks, "fsdp")
    down_full = in_order(between(dict(zip(keys, down_got)), "fsdp"), "fsdp")

    attended = attended3.reshape(rows, width)
    attended_low = attended.astype(b16)
    mixed = jnp.dot(attended_low, mixing_full, preferred_element_type=f32) + mixbias
    hidden = flat + mixed
    first = layer_norm(hidden, fgain, fshift)
    first_low = first.astype(b16)
    pre = jnp.dot(first_low, up_full, preferred_element_type=f32) + upbias
    act, gelu_back = jax.vjp(gelu_exact, pre)
    act_low = act.astype(b16)
    branch = jnp.dot(act_low, down_full, preferred_element_type=f32) + downbias
    summed = first + branch
    result, second_back = jax.vjp(layer_norm, summed, sgain, sshift)
    dsummed, grad_sgain, grad_sshift = second_back(cotangent.reshape(rows, width))
    dbranch = dsummed.astype(b16)
    dact = jnp.einsum("rd,fd->rf", dbranch, down_full, preferred_element_type=f32)
    dpre = gelu_back(dact)[0].astype(b16)
    dfirst = dsummed + jnp.einsum("rf,df->rd", dpre, up_full, preferred_element_type=f32)
    _, first_back = jax.vjp(layer_norm, hidden, fgain, fshift)
    dhidden, grad_fgain, grad_fshift = first_back(dfirst)
    dmixed = dhidden.astype(b16)
    dattended = jnp.einsum("re,de->rd", dmixed, mixing_full, preferred_element_type=f32)

    grads = place_corr(dattended, attended, extra.reshape(rows, LANES))
    grads = grads.reshape(seqs, block, width + LANES)
    grads, act_low, dbranch, first_low, dpre, attended_low, dmixed = together(
        grads, act_low, dbranch, first_low, dpre, attended_low, dmixed
    )

    def summed_rows(x):
        return jnp.sum(x.astype(f32), axis=0)

    def vector_rows(vectors):
        flat_vectors = jnp.concatenate([v.reshape(owners, -1) for v in vectors], 1)
        need = -(-flat_vectors.shape[1] // width)
        need += row_pad(need, blocks)
        pad = need * width - flat_vectors.shape[1]
        return jnp.pad(flat_vectors, ((0, 0), (0, pad))).astype(b16).reshape(owners, need, width)

    steps_ctx = block_sum_steps(blocks)

    def begin_sum(x):
        more = row_pad(x.shape[0], blocks)
        x = jnp.pad(x, ((0, more), (0, 0))) if more else x
        return x[:, : width // 2], x[:, width // 2 :]

    place1 = place.reshape(1)

    gr, gl = ring_step(grads, grads, "ctx")
    grad_down = jnp.einsum("rf,rd->fd", act_low, dbranch, preferred_element_type=f32).astype(b16)
    down_send, down_keep = core_parts(grad_down.reshape(owners, -1, width))
    down_got = swap(down_send, "fsdp", 1)
    grad_mixing = jnp.einsum("rd,re->de", attended_low, dmixed, preferred_element_type=f32)
    early = vector_rows(
        [summed_rows(dmixed), grad_fgain, grad_fshift, summed_rows(dbranch), grad_sgain,
         grad_sshift, summed_rows(dpre)]
    )
    grad_mixing = jnp.concatenate(
        [grad_mixing.astype(b16).reshape(owners, share, width), early], 1
    )
    mixing_send, mixing_keep = core_parts(grad_mixing)
    mixing_got = swap(mixing_send, "fsdp", 1)
    grad_up = jnp.einsum("rd,rf->df", first_low, dpre, preferred_element_type=f32).astype(b16)
    dquery = [attend_query(0, 1, slots_qkv, grads, bases, lengths)]
    gr, gl, down_got, mixing_got, grad_up, grads, dquery[0] = together(
        gr, gl, down_got, mixing_got, grad_up, grads, dquery[0]
    )
    grad_slots = [grads, gr, gl]

    gr, gl = ring_step(gr, gl, "ctx")
    sum_one = jnp.concatenate([added(down_keep, down_got), added(mixing_keep, mixing_got)], 1)
    sum_one = chip_sum(sum_one)
    up_send, up_keep = core_parts(grad_up.reshape(owners, share, -1))
    up_got = swap(up_send, "fsdp", 1)
    dquery.append(attend_query(1, 1, slots_qkv, grads, bases, lengths))
    gr, gl, up_got, dquery[1] = together(gr, gl, up_got, dquery[1])
    grad_slots += [gr, gl]
    dquery = jnp.concatenate(dquery, 0).reshape(rows, width)

    dkv = ()
    done = 0
    for step in range(3, steps + 1):
        last = step == steps
        nr, nl = ring_last(gr, gl, "ctx") if last else ring_step(gr, gl, "ctx")
        if step == 3:
            grad_query = jnp.einsum("rd,re->de", flat_low, dquery, preferred_element_type=f32)
            query_send, query_keep = core_parts(grad_query.astype(b16).reshape(owners, share, width))
            query_got = swap(query_send, "fsdp", 1)
        if last:
            sum_two = jnp.concatenate(
                [columns_to_rows(added(up_keep, up_got), width), added(query_keep, query_got)], 1
            )
            sum_two = chip_sum(sum_two)
            one = steps_ctx[0](begin_sum(sum_one))
        use = slice(done, len(grad_slots))
        dkv = attend_keys(
            slots_qkv[0], slots_qkv[use], grad_slots[use], place1, lengths, tuple(dkv)
        )
        done = len(grad_slots)
        if last:
            gr, gl, *rest = together(nr, nl, *one, *dkv)
            one, dkv = tuple(rest[:2]), rest[2:]
            grad_slots.append(jnp.concatenate([gr, gl], 0))
        else:
            gr, gl, sum_one, query_got, *dkv = together(nr, nl, sum_one, query_got, *dkv)
            grad_slots += [gr, gl]

    use = slice(done, len(grad_slots))
    one = steps_ctx[1](one)
    dkeys, dvalues = attend_keys(
        slots_qkv[0], slots_qkv[use], grad_slots[use], place1, lengths, tuple(dkv), True
    )
    dkeys, dvalues, one0, one1, sum_two = together(dkeys, dvalues, *one, sum_two)
    one = (one0, one1)
    dkeys, dvalues = dkeys.reshape(rows, width), dvalues.reshape(rows, width)
    dlate = jnp.concatenate([dkeys, dvalues], 1)
    grad_late = jnp.einsum("rd,re->de", flat_low, dlate, preferred_element_type=f32).astype(b16)
    grad_late = columns_to_rows(grad_late.reshape(owners, share, -1), width)
    late = vector_rows([summed_rows(dquery), summed_rows(dvalues)])
    late_send, late_keep = core_parts(jnp.concatenate([grad_late, late], 1))
    late_got = swap(late_send, "fsdp", 1)
    one = steps_ctx[2](one)
    dprojected = jnp.concatenate([dquery, dlate], 1)
    tokens_grad = dhidden + jnp.einsum(
        "re,de->rd", dprojected, attend_full, preferred_element_type=f32
    )
    late_got, sum_two, *one = together(late_got, sum_two, *one)

    two = begin_sum(sum_two)
    sum_late = chip_sum(added(late_keep, late_got))
    one = steps_ctx[3](one)
    two = steps_ctx[0](two)
    sum_late, *both = together(sum_late, *one, *two)
    chains = [(tuple(both[:2]), 4), (tuple(both[2:]), 1), (begin_sum(sum_late), 0)]
    while any(at < len(steps_ctx) for _, at in chains):
        chains = [
            (steps_ctx[at](pair), at + 1) if at < len(steps_ctx) else (pair, at)
            for pair, at in chains
        ]
        flat_chains = together(*(v for pair, _ in chains for v in pair))
        chains = [
            ((flat_chains[2 * k], flat_chains[2 * k + 1]), at)
            for k, (_, at) in enumerate(chains)
        ]
    one, two, three = (jnp.concatenate(pair, 1).astype(f32) for pair, _ in chains)

    at = down_weight.shape[0]
    own_down = one[:at]
    own_mixing = one[at : at + share]
    early = one[at + share : at + share + early.shape[1]].reshape(-1)
    parts = up_weight.shape[1] // width
    own_up = rows_to_columns(two[: parts * share], parts)
    own_query = two[parts * share : (parts + 1) * share]
    own_attend = jnp.concatenate([own_query, rows_to_columns(three[: 2 * share], 2)], 1)
    late = three[2 * share : 2 * share + late.shape[1]].reshape(-1)
    own_qbias, own_vbias = (late[k * share : (k + 1) * share] for k in range(2))
    own_mixbias, own_fgain, own_fshift, own_downbias, own_sgain, own_sshift = (
        early[k * share : (k + 1) * share] for k in range(6)
    )
    own_upbias = early[6 * share : 6 * share + up_bias.shape[0]]
    return (
        result.reshape(seqs, block, width),
        tokens_grad.reshape(seqs, block, width),
        own_attend,
        own_qbias,
        own_vbias,
        own_mixing,
        own_mixbias,
        own_fgain,
        own_fshift,
        own_up,
        own_upbias,
        own_down,
        own_downbias,
        own_sgain,
        own_sshift,
    )


def solution(mesh):
    rows = P("fsdp", "ctx", None)
    matrix = P("fsdp", None)
    vector = P("fsdp")
    return jax.shard_map(
        per_device,
        mesh=mesh,
        in_specs=(
            rows, vector, matrix, vector, vector, matrix, vector, vector, vector,
            matrix, vector, matrix, vector, vector, vector, rows,
        ),
        out_specs=(
            rows, rows, matrix, vector, vector, matrix, vector, vector, vector,
            matrix, vector, matrix, vector, vector, vector,
        ),
        check_vma=False,
    )
```

time: 605 us -> 526 us (0.87)
  blocking collectives: 83.6 us -> 0 us
  waiting for transfers between devices: 153 us -> 123 us
  other arithmetic: 45.2 us -> 65.8 us
  matrix products: 76.4 us -> 90.8 us
  Pallas kernels: 95.5 us -> 108 us
  starting transfers between devices: 94.4 us -> 83.7 us
    all_gather x1 -> x0, blocking collectives: 44.5 us -> none  [per_device(): small_full = lax.all_gather(jnp.concatenate(small), 'fsdp', axis=0)]
    psum x1 -> x0, blocking collectives: 39.1 us -> none  [per_device(): lax.psum(jnp.concatenate([v.reshape(owners, -1) for v in late], 1), ('fsd...]
    ppermute x80 -> x68, waiting for transfers between devices: 153 us -> 123 us  [the longest x52 95.2 us: swap(): return lax.ppermute(x, axis, [(i, i ^ bit) for i in range(count)])]
    dot_general x9 -> x10, matrix products: 21.6 us -> 33.6 us  [the longest x8 30.2 us: project(): jnp.dot(t.reshape(rows, width), attend_full, preferred_element_type=f32)]
    ppermute x80 -> x68, starting transfers between devices: 94.4 us -> 83.7 us  [the longest x52 66.3 us: swap(): return lax.ppermute(x, axis, [(i, i ^ bit) for i in range(count)])]
    slice x10 -> x21, local copies, waits for them, and re-layouts: 1.77 us -> 12.2 us  [the longest x4 3.94 us: ring_last(): return ring_step(r[:1], l[1:], axis)]
    convert_element_type x10 -> x2, local copies, waits for them, and re-layouts: 10.3 us -> 0.16 us  [per_device(): safe.astype(jnp.int32)]
    dynamic_slice x32 -> x18, local copies, waits for them, and re-layouts: 9.29 us -> 0.38 us  [halve(): send = lax.dynamic_slice_in_dim(x, (1 - upper) * half, half, 0)]
  transfers between devices with their start and end apart: 80 -> 68, of which waited for: 47 -> 28; matrix products, arithmetic and copies ran while one was open for 18% -> 22% of each run, Pallas kernels for 16% -> 20%
where the time goes in v2:
time: 526 us; the launch traced here: 522 us
  waiting for transfers between devices  123 us (23%)
  Pallas kernels  108 us (21%)
  matrix products  90.8 us (17%)
  starting transfers between devices  83.7 us (16%)
  other arithmetic  65.8 us (13%)
  local copies, waits for them, and re-layouts  47.4 us (9%)
    ppermute x52, waiting for transfers between devices, swap(): return lax.ppermute(x, axis, [(i, i ^ bit) for i in range(count)])  95.2 us
    ppermute x52, starting transfers between devices, swap(): return lax.ppermute(x, axis, [(i, i ^ bit) for i in range(count)])  66.3 us
    pallas_call x3, Pallas kernels, attend_keys(): pl.pallas_call(functools.partial(key_kernel, slots, not state, final), gr...  42.2 us
    pallas_call x2, Pallas kernels, attend_query(): pl.pallas_call(functools.partial(query_kernel, slots), grid_spec=pltpu.Pr...  33.4 us
    pallas_call x2, Pallas kernels, attend_forward(): pl.pallas_call(functools.partial(forward_kernel, slots, not state, final)...  31.4 us
    dot_general x8, matrix products, project(): jnp.dot(t.reshape(rows, width), attend_full, preferred_element_type=f32)  30.2 us
    ppermute x16, waiting for transfers between devices, ring_step(): return (lax.ppermute(r, axis, right), lax.ppermute(l, axis, left))  28.2 us
    unnamed x155, local copies, waits for them, and re-layouts  22.4 us
  transfers between devices with their start and end apart: 68, of which 28 were waited for; matrix products, arithmetic and copies ran while one was open for 22% of the time, Pallas kernels for 20%

profile of v2, /device:TPU:0, one launch (start us, length us, event | category | flops | bytes accessed | tf_op | source)
XLA Modules:
  0.0 521.9 jit_solution(5623193328563317581)
XLA Ops:
  0.8 3.0 collective-permute-start.2
  3.8 2.9 bitcast_convert_fusion.1
  9.0 16.8 %collective-permute-done = bf16[2,256,768]{2,1,0:T(8,128)(2,1)} collective-permute-done((bf16[2,256,768]{2,1,0:T(8,128)(2,1)S(1)}, bf16[2,256,768]{2,1,0:T(8,128)(2,1)}, u32[]{:S(2)}, u32[]{:S(2)}) %collective-permute-start) | collective-permute-done | bytes 786464 | tf_op jit(solution)/shard_map/ppermute | solution.py:63
  36.2 3.7 collective-permute-done.6
  39.9 8.7 %collective-permute-done.3 = bf16[2,256,768]{2,1,0:T(8,128)(2,1)S(1)} collective-permute-done((bf16[2,256,768]{2,1,0:T(8,128)(2,1)}, bf16[2,256,768]{2,1,0:T(8,128)(2,1)S(1)}, u32[]{:S(2)}, u32[]{:S(2)}) %collective-permute-start.3) | collective-permute-done | bytes 786464 | tf_op jit(solution)/shard_map/ppermute | solution.py:63
  56.7 4.4 fusion.15
  61.1 5.1 fusion.8
  66.3 4.6 fusion.9
  70.9 3.4 fusion.10
  75.9 4.4 fusion.11
  82.9 3.1 fusion.13
  88.6 3.1 fusion.12
  99.8 3.2 pad_maximum_fusion.4
  104.5 21.2 %shard_map.289 = (f32[2,256,768]{2,1,0:T(8,128)S(1)}, f32[2,256,768]{2,1,0:T(8,128)S(1)}, f32[2,256,768]{2,1,0:T(8,128)S(1)}) custom-call(s32[7]{0:T(128)S(1)} %bitcast.314, s32[2]{0:T(128)S(1)} %copy-done.6, s32[12]{0:T(128)S(1)} %reshape.384.safe, bf16[2,256,2304]{2,1,0:T(8,128)(2,1)} %bitcast.277, bf16[2,256,2304]{2,1,0:T(8,128)(2,1)} %bitcast.278, ...), custom_call_target="tpu_custom_call" | custom-call | flops 11274289152 | bytes 11010048 | tf_op jit(solution)/shard_map/pallas_call | solution.py:412
  131.7 10.2 %shard_map.290 = (f32[2,256,768]{2,1,0:T(8,128)S(1)}, f32[2,256,128]{2,1,0:T(8,128)S(1)}) custom-call(s32[1]{0:T(128)} %slice.227.bases, s32[2]{0:T(128)S(1)} %copy-done.6, s32[12]{0:T(128)S(1)} %reshape.385.safe, bf16[2,256,2304]{2,1,0:T(8,128)(2,1)} %bitcast.280, bf16[2,256,2304]{2,1,0:T(8,128)(2,1)} %bitcast.318, bf16[2,256,2304]{2,1,0:T(8,128)(2,1)} %bitcast.319, ...), custom_call_target="tpu_custom_call" | custom-call | flops 1610612736 | bytes 1572864 | tf_op jit(solution)/shard_map/pallas_call | solution.py:412
  147.9 2.7 broadcast_select_fusion.15
  150.6 18.4 %multiply_convert_fusion = (bf16[512,3072]{1,0:T(8,128)(2,1)S(1)}, f32[512,3072]{1,0:T(8,128)}, f32[512,3072]{1,0:T(8,128)}) fusion(f32[3072]{0:T(1024)S(1)} %add.468, bf16[512,768]{1,0:T(8,128)(2,1)S(1)} %fusion.34, bf16[192,3072]{1,0:T(8,128)(2,1)S(1)} %get-tuple-element.275, bf16[192,3072]{1,0:T(8,128)(2,1)S(1)} %get-tuple-element.274, ...), kind=kOutput, calls=%fused_computation.4 | convolution fusion | flops 2538602496 | bytes 21245952 | tf_op jit(solution)/shard_map/dot_general | solution.py:623
  169.1 3.1 broadcast_select_fusion.7
  173.6 2.7 fusion.105
  180.3 10.7 %add_convert_fusion = bf16[512,3072]{1,0:T(8,128)(2,1)S(1)} fusion(f32[512,3072]{1,0:T(8,128)} %get-tuple-element.267, f32[512,3072]{1,0:T(8,128)} %get-tuple-element.356, f32[3072]{0:T(1024)S(1)} %add.468, bf16[512,768]{1,0:T(8,128)(2,1)S(1)} %add_convert_fusion.4, bf16[768,768]{1,0:T(8,128)(2,1)} %copy-done.43, bf16[768,768]{1,0:T(8,128)(2,1)} %copy-done.42, ...), kind=kOutput, calls=%fused_computation.3 | convolution fusion | flops 2458386432 | bytes 21245952 | tf_op jit(solution)/shard_map/rd,fd->rf/dot_general | solution.py:631
  191.0 5.2 multiply_reduce_fusion
  201.4 2.9 convolution_convert_fusion.1
  220.1 3.1 convolution_convert_fusion
  223.2 16.9 %shard_map.292 = bf16[1,256,768]{2,1,0:T(8,128)(2,1)S(1)} custom-call(s32[8]{0:T(128)S(1)} %broadcast_multiply_fusion.2.bases, s32[1]{0:T(128)} %get-tuple-element.353.lengths, bf16[2,256,2304]{2,1,0:T(8,128)(2,1)S(1)} %bitcast.288, bf16[2,256,896]{2,1,0:T(8,128)(2,1)S(1)} %bitcast.304, bf16[2,256,896]{2,1,0:T(8,128)(2,1)S(1)} %bitcast.305, ...), custom_call_target="tpu_custom_call" | custom-call | flops 9663676416 | bytes 6291456 | tf_op jit(solution)/shard_map/pallas_call | solution.py:436
  243.6 2.6 fusion.7
  248.1 14.3 %collective-permute-start.25 = (bf16[1,1024,768]{2,1,0:T(8,128)(2,1)}, bf16[1,1024,768]{2,1,0:T(8,128)(2,1)}, u32[]{:S(2)}, u32[]{:S(2)}) collective-permute-start(bf16[1,1024,768]{2,1,0:T(8,128)(2,1)} %fusion.24), channel_id=1, source_target_pairs={{0,2},{1,3},{2,0},{3,1},{4,6},{5,7},{6,4},{7,5},{8,10},{9,11},{10,... | collective-permute-start | bytes 4718600 | tf_op jit(solution)/shard_map/ppermute | solution.py:34
  267.2 16.5 %shard_map.293 = bf16[1,256,768]{2,1,0:T(8,128)(2,1)S(1)} custom-call(s32[8]{0:T(128)S(1)} %broadcast_multiply_fusion.2.bases, s32[1]{0:T(128)} %get-tuple-element.352.lengths, bf16[2,256,2304]{2,1,0:T(8,128)(2,1)S(1)} %bitcast.291, bf16[2,256,896]{2,1,0:T(8,128)(2,1)S(1)} %bitcast.306, bf16[2,256,896]{2,1,0:T(8,128)(2,1)S(1)} %bitcast.307, ...), custom_call_target="tpu_custom_call" | custom-call | flops 9663676416 | bytes 6291456 | tf_op jit(solution)/shard_map/pallas_call | solution.py:436
  283.7 14.0 %collective-permute-done.25 = bf16[1,1024,768]{2,1,0:T(8,128)(2,1)} collective-permute-done((bf16[1,1024,768]{2,1,0:T(8,128)(2,1)}, bf16[1,1024,768]{2,1,0:T(8,128)(2,1)}, u32[]{:S(2)}, u32[]{:S(2)}) %collective-permute-start.25) | collective-permute-done | bytes 1572896 | tf_op jit(solution)/shard_map/ppermute | solution.py:34
  297.7 3.1 fusion.23
  305.0 22.8 %shard_map.294 = (f32[2,256,768]{2,1,0:T(8,128)S(1)}, f32[2,256,768]{2,1,0:T(8,128)}) custom-call(s32[1]{0:T(128)} %bitcast.50.place, s32[2]{0:T(128)S(1)} %copy-done.6, bf16[2,256,2304]{2,1,0:T(8,128)(2,1)} %bitcast.281, bf16[2,256,2304]{2,1,0:T(8,128)(2,1)} %bitcast.282, bf16[2,256,2304]{2,1,0:T(8,128)(2,1)} %bitcast.283, bf16[2,256,2304]{2,1,0:T(8,128)(2,1)} %bitcast.297, ...), custom_call_target="tpu_custom_call" | custom-call | flops 16106127360 | bytes 7864320 | tf_op jit(solution)/shard_map/pallas_call | solution.py:459
  327.9 4.5 fusion.6
  351.0 11.6 %shard_map.295 = (f32[2,256,768]{2,1,0:T(8,128)S(1)}, f32[2,256,768]{2,1,0:T(8,128)S(1)}) custom-call(s32[1]{0:T(128)} %bitcast.50.place, s32[2]{0:T(128)S(1)} %copy-done.6, bf16[2,256,2304]{2,1,0:T(8,128)(2,1)} %bitcast.284, bf16[2,256,2304]{2,1,0:T(8,128)(2,1)} %bitcast.285, bf16[2,256,2304]{2,1,0:T(8,128)(2,1)} %bitcast.340, ...), custom_call_target="tpu_custom_call" | custom-call | flops 6442450944 | bytes 3145728 | tf_op jit(solution)/shard_map/pallas_call | solution.py:459
  366.0 7.7 %shard_map.296 = (bf16[2,256,768]{2,1,0:T(8,128)(2,1)S(1)}, bf16[2,256,768]{2,1,0:T(8,128)(2,1)S(1)}) custom-call(s32[1]{0:T(128)} %bitcast.50.place, s32[2]{0:T(128)S(1)} %copy-done.6, bf16[2,256,2304]{2,1,0:T(8,128)(2,1)} %bitcast.286, bf16[2,256,2304]{2,1,0:T(8,128)(2,1)} %bitcast.287, bf16[2,256,2304]{2,1,0:T(8,128)(2,1)} %bitcast.324, ...), custom_call_target="tpu_custom_call" | custom-call | flops 3221225472 | bytes 1572864 | tf_op jit(solution)/shard_map/pallas_call | solution.py:459
  373.9 9.1 %collective-permute-done.33 = bf16[1,960,768]{2,1,0:T(8,128)(2,1)S(1)} collective-permute-done((bf16[1,960,768]{2,1,0:T(8,128)(2,1)S(1)}, bf16[1,960,768]{2,1,0:T(8,128)(2,1)S(1)}, u32[]{:S(2)}, u32[]{:S(2)}) %collective-permute-start.33) | collective-permute-done | bytes 1474592 | tf_op jit(solution)/shard_map/ppermute | solution.py:34
  395.3 7.6 %collective-permute-done.35 = bf16[128,384]{1,0:T(8,128)(2,1)S(1)} collective-permute-done((bf16[128,384]{1,0:T(8,128)(2,1)S(1)}, bf16[128,384]{1,0:T(8,128)(2,1)S(1)}, u32[]{:S(2)}, u32[]{:S(2)}) %collective-permute-start.35) | collective-permute-done | bytes 98336 | tf_op jit(solution)/shard_map/ppermute | solution.py:34
  408.7 2.9 collective-permute-start.39
  413.7 4.4 collective-permute-done.38
  421.6 5.4 %collective-permute-done.41 = bf16[480,384]{1,0:T(8,128)(2,1)S(1)} collective-permute-done((bf16[480,384]{1,0:T(8,128)(2,1)S(1)}, bf16[480,384]{1,0:T(8,128)(2,1)S(1)}, u32[]{:S(2)}, u32[]{:S(2)}) %collective-permute-start.41) | collective-permute-done | bytes 368672 | tf_op jit(solution)/shard_map/ppermute | solution.py:34
  432.3 6.6 %collective-permute-done.46 = bf16[224,384]{1,0:T(8,128)(2,1)S(1)} collective-permute-done((bf16[224,384]{1,0:T(8,128)(2,1)S(1)}, bf16[224,384]{1,0:T(8,128)(2,1)S(1)}, u32[]{:S(2)}, u32[]{:S(2)}) %collective-permute-start.46) | collective-permute-done | bytes 172064 | tf_op jit(solution)/shard_map/ppermute | solution.py:34
  440.8 5.6 %collective-permute-done.47 = bf16[224,384]{1,0:T(8,128)(2,1)S(1)} collective-permute-done((bf16[224,384]{1,0:T(8,128)(2,1)S(1)}, bf16[224,384]{1,0:T(8,128)(2,1)S(1)}, u32[]{:S(2)}, u32[]{:S(2)}) %collective-permute-start.47) | collective-permute-done | bytes 172064 | tf_op jit(solution)/shard_map/ppermute | solution.py:34
  448.7 2.8 collective-permute-start.51
  452.2 6.4 %collective-permute-done.52 = bf16[112,384]{1,0:T(8,128)(2,1)S(1)} collective-permute-done((bf16[112,384]{1,0:T(8,128)(2,1)S(1)}, bf16[112,384]{1,0:T(8,128)(2,1)S(1)}, u32[]{:S(2)}, u32[]{:S(2)}) %collective-permute-start.52) | collective-permute-done | bytes 86048 | tf_op jit(solution)/shard_map/ppermute | solution.py:34
  459.7 3.4 collective-permute-done.53
  469.5 6.0 %collective-permute-done.56 = bf16[56,384]{1,0:T(8,128)(2,1)S(1)} collective-permute-done((bf16[56,384]{1,0:T(8,128)(2,1)S(1)}, bf16[56,384]{1,0:T(8,128)(2,1)S(1)}, u32[]{:S(2)}, u32[]{:S(2)}) %collective-permute-start.56) | collective-permute-done | bytes 43040 | tf_op jit(solution)/shard_map/ppermute | solution.py:34
  481.3 3.4 collective-permute-done.61
  490.1 6.2 %collective-permute-done.65 = bf16[112,384]{1,0:T(8,128)(2,1)S(1)} collective-permute-done((bf16[112,384]{1,0:T(8,128)(2,1)S(1)}, bf16[112,384]{1,0:T(8,128)(2,1)S(1)}, u32[]{:S(2)}, u32[]{:S(2)}) %collective-permute-start.65) | collective-permute-done | bytes 86048 | tf_op jit(solution)/shard_map/ppermute | solution.py:34
  499.7 3.2 add_add_fusion.3
  504.4 4.0 collective-permute-done.67
  (482 shorter events, 180.9 us)
Async XLA Ops:
  0.8 26.3 %collective-permute-start.2 = (bf16[192,2304]{1,0:T(8,128)(2,1)}, bf16[192,2304]{1,0:T(8,128)(2,1)S(1)}, u32[]{:S(2)}, u32[]{:S(2)}) collective-permute-start(bf16[192,2304]{1,0:T(8,128)(2,1)} %param.20), channel_id=1, source_target_pairs={{0,2},{1,3},{2,0},{3,1},{4,6},{5,7},{6,4},{7,5},{8,10},{9,11},{10,... | collective-permute-start | bytes 2654216 | tf_op jit(solution)/shard_map/ppermute | solution.py:34
  6.7 19.1 %collective-permute-start = (bf16[2,256,768]{2,1,0:T(8,128)(2,1)S(1)}, bf16[2,256,768]{2,1,0:T(8,128)(2,1)}, u32[]{:S(2)}, u32[]{:S(2)}) collective-permute-start(bf16[2,256,768]{2,1,0:T(8,128)(2,1)S(1)} %get-tuple-element.293), channel_id=1, source_target_pairs={{0,8},{8,16},{16,24},{24,28},{28,20},{20,12},{12,4},{4,0},{1,9},{9... | collective-permute-start | bytes 2359304 | tf_op jit(solution)/shard_map/ppermute | solution.py:63
  8.3 18.8 %collective-permute-start.1 = (bf16[2,256,768]{2,1,0:T(8,128)(2,1)S(1)}, bf16[2,256,768]{2,1,0:T(8,128)(2,1)}, u32[]{:S(2)}, u32[]{:S(2)}) collective-permute-start(bf16[2,256,768]{2,1,0:T(8,128)(2,1)S(1)} %get-tuple-element.293), channel_id=1, source_target_pairs={{8,0},{16,8},{24,16},{28,24},{20,28},{12,20},{4,12},{0,4},{9,1},{1... | collective-permute-start | bytes 2359304 | tf_op jit(solution)/shard_map/ppermute | solution.py:63
  28.5 20.2 %collective-permute-start.3 = (bf16[2,256,768]{2,1,0:T(8,128)(2,1)}, bf16[2,256,768]{2,1,0:T(8,128)(2,1)S(1)}, u32[]{:S(2)}, u32[]{:S(2)}) collective-permute-start(bf16[2,256,768]{2,1,0:T(8,128)(2,1)} %collective-permute-done), channel_id=1, source_target_pairs={{0,8},{8,16},{16,24},{24,28},{28,20},{20,12},{12,4},{4,0},{1,9},{9... | collective-permute-start | bytes 2359304 | tf_op jit(solution)/shard_map/ppermute | solution.py:63
  30.0 19.9 %collective-permute-start.4 = (bf16[2,256,768]{2,1,0:T(8,128)(2,1)}, bf16[2,256,768]{2,1,0:T(8,128)(2,1)S(1)}, u32[]{:S(2)}, u32[]{:S(2)}) collective-permute-start(bf16[2,256,768]{2,1,0:T(8,128)(2,1)} %collective-permute-done.1), channel_id=1, source_target_pairs={{8,0},{16,8},{24,16},{28,24},{20,28},{12,20},{4,12},{0,4},{9,1},{1... | collective-permute-start | bytes 2359304 | tf_op jit(solution)/shard_map/ppermute | solution.py:63
  52.1 28.2 %collective-permute-start.9 = (bf16[192,3072]{1,0:T(8,128)(2,1)}, bf16[192,3072]{1,0:T(8,128)(2,1)}, u32[]{:S(2)}, u32[]{:S(2)}) collective-permute-start(bf16[192,3072]{1,0:T(8,128)(2,1)} %param.27), channel_id=1, source_target_pairs={{0,2},{1,3},{2,0},{3,1},{4,6},{5,7},{6,4},{7,5},{8,10},{9,11},{10,... | collective-permute-start | bytes 3538952 | tf_op jit(solution)/shard_map/ppermute | solution.py:34
  52.7 27.6 %collective-permute-start.7 = (bf16[2,256,768]{2,1,0:T(8,128)(2,1)}, bf16[2,256,768]{2,1,0:T(8,128)(2,1)}, u32[]{:S(2)}, u32[]{:S(2)}) collective-permute-start(bf16[2,256,768]{2,1,0:T(8,128)(2,1)} %copy-done.64), channel_id=1, source_target_pairs={{0,8},{8,16},{16,24},{24,28},{28,20},{20,12},{12,4},{4,0},{1,9},{9... | collective-permute-start | bytes 2359304 | tf_op jit(solution)/shard_map/ppermute | solution.py:63
  54.2 26.1 %collective-permute-start.8 = (bf16[2,256,768]{2,1,0:T(8,128)(2,1)}, bf16[2,256,768]{2,1,0:T(8,128)(2,1)}, u32[]{:S(2)}, u32[]{:S(2)}) collective-permute-start(bf16[2,256,768]{2,1,0:T(8,128)(2,1)} %copy-done.66), channel_id=1, source_target_pairs={{8,0},{16,8},{24,16},{28,24},{20,28},{12,20},{4,12},{0,4},{9,1},{1... | collective-permute-start | bytes 2359304 | tf_op jit(solution)/shard_map/ppermute | solution.py:63
  97.5 28.2 %collective-permute-start.11 = (bf16[1,256,768]{2,1,0:T(8,128)(2,1)}, bf16[1,256,768]{2,1,0:T(8,128)(2,1)}, u32[]{:S(2)}, u32[]{:S(2)}) collective-permute-start(bf16[1,256,768]{2,1,0:T(8,128)(2,1)} %slice.246), channel_id=1, source_target_pairs={{0,8},{8,16},{16,24},{24,28},{28,20},{20,12},{12,4},{4,0},{1,9},{9... | collective-permute-start | bytes 1179656 | tf_op jit(solution)/shard_map/ppermute | solution.py:63
  99.1 26.6 %collective-permute-start.12 = (bf16[1,256,768]{2,1,0:T(8,128)(2,1)}, bf16[1,256,768]{2,1,0:T(8,128)(2,1)}, u32[]{:S(2)}, u32[]{:S(2)}) collective-permute-start(bf16[1,256,768]{2,1,0:T(8,128)(2,1)} %slice.247), channel_id=1, source_target_pairs={{8,0},{16,8},{24,16},{28,24},{20,28},{12,20},{4,12},{0,4},{9,1},{1... | collective-permute-start | bytes 1179656 | tf_op jit(solution)/shard_map/ppermute | solution.py:63
  103.0 44.8 %collective-permute-start.13 = (bf16[2,192,3072]{2,1,0:T(8,128)(2,1)}, bf16[2,192,3072]{2,1,0:T(8,128)(2,1)}, u32[]{:S(2)}, u32[]{:S(2)}) collective-permute-start(bf16[2,192,3072]{2,1,0:T(8,128)(2,1)} %pad_maximum_fusion.4), channel_id=1, source_target_pairs={{0,1},{1,0},{2,3},{3,2},{4,5},{5,4},{6,7},{7,6},{8,9},{9,8},{10,11... | collective-permute-start | bytes 7077896 | tf_op jit(solution)/shard_map/ppermute | solution.py:34
  103.0 42.4 %collective-permute-start.14 = (bf16[768,768]{1,0:T(8,128)(2,1)}, bf16[768,768]{1,0:T(8,128)(2,1)}, u32[]{:S(2)}, u32[]{:S(2)}) collective-permute-start(bf16[768,768]{1,0:T(8,128)(2,1)} %param.29), channel_id=1, source_target_pairs={{0,2},{1,3},{2,0},{3,1},{4,6},{5,7},{6,4},{7,5},{8,10},{9,11},{10,... | collective-permute-start | bytes 3538952 | tf_op jit(solution)/shard_map/ppermute | solution.py:34
  147.6 21.5 %collective-permute-start.15 = (bf16[2,768,768]{2,1,0:T(8,128)(2,1)S(1)}, bf16[2,768,768]{2,1,0:T(8,128)(2,1)S(1)}, u32[]{:S(2)}, u32[]{:S(2)}) collective-permute-start(bf16[2,768,768]{2,1,0:T(8,128)(2,1)S(1)} %pad_maximum_fusion.5), channel_id=1, source_target_pairs={{0,1},{1,0},{2,3},{3,2},{4,5},{5,4},{6,7},{7,6},{8,9},{9,8},{10,11... | collective-permute-start | bytes 7077896 | tf_op jit(solution)/shard_map/ppermute | solution.py:34
  207.2 32.9 %collective-permute-start.18 = (bf16[2,768,768]{2,1,0:T(8,128)(2,1)}, bf16[2,768,768]{2,1,0:T(8,128)(2,1)}, u32[]{:S(2)}, u32[]{:S(2)}) collective-permute-start(bf16[2,768,768]{2,1,0:T(8,128)(2,1)} %dynamic-slice_bitcast_fusion.1), channel_id=1, source_target_pairs={{0,1},{1,0},{2,3},{3,2},{4,5},{5,4},{6,7},{7,6},{8,9},{9,8},{10,11... | collective-permute-start | bytes 7077896 | tf_op jit(solution)/shard_map/ppermute | solution.py:34
  208.4 31.8 %collective-permute-start.16 = (bf16[2,256,896]{2,1,0:T(8,128)(2,1)S(1)}, bf16[2,256,896]{2,1,0:T(8,128)(2,1)}, u32[]{:S(2)}, u32[]{:S(2)}) collective-permute-start(bf16[2,256,896]{2,1,0:T(8,128)(2,1)S(1)} %bitcast.302), channel_id=1, source_target_pairs={{0,8},{8,16},{16,24},{24,28},{28,20},{20,12},{12,4},{4,0},{1,9},{9... | collective-permute-start | bytes 2752520 | tf_op jit(solution)/shard_map/ppermute | solution.py:63
  209.9 30.2 %collective-permute-start.17 = (bf16[2,256,896]{2,1,0:T(8,128)(2,1)S(1)}, bf16[2,256,896]{2,1,0:T(8,128)(2,1)}, u32[]{:S(2)}, u32[]{:S(2)}) collective-permute-start(bf16[2,256,896]{2,1,0:T(8,128)(2,1)S(1)} %bitcast.303), channel_id=1, source_target_pairs={{8,0},{16,8},{24,16},{28,24},{20,28},{12,20},{4,12},{0,4},{9,1},{1... | collective-permute-start | bytes 2752520 | tf_op jit(solution)/shard_map/ppermute | solution.py:63
  219.8 20.3 %collective-permute-start.19 = (bf16[2,256,768]{2,1,0:T(8,128)(2,1)}, bf16[2,256,768]{2,1,0:T(8,128)(2,1)}, u32[]{:S(2)}, u32[]{:S(2)}) collective-permute-start(bf16[2,256,768]{2,1,0:T(8,128)(2,1)} %fusion.42), channel_id=1, source_target_pairs={{0,1},{1,0},{2,3},{3,2},{4,5},{5,4},{6,7},{7,6},{8,9},{9,8},{10,11... | collective-permute-start | bytes 2359304 | tf_op jit(solution)/shard_map/ppermute | solution.py:34
  241.8 59.0 %collective-permute-start.22 = (bf16[2,192,3072]{2,1,0:T(8,128)(2,1)}, bf16[2,192,3072]{2,1,0:T(8,128)(2,1)}, u32[]{:S(2)}, u32[]{:S(2)}) collective-permute-start(bf16[2,192,3072]{2,1,0:T(8,128)(2,1)} %dynamic-slice_bitcast_fusion), channel_id=1, source_target_pairs={{0,1},{1,0},{2,3},{3,2},{4,5},{5,4},{6,7},{7,6},{8,9},{9,8},{10,11... | collective-permute-start | bytes 7077896 | tf_op jit(solution)/shard_map/ppermute | solution.py:34
  248.1 49.6 %collective-permute-start.25 = (bf16[1,1024,768]{2,1,0:T(8,128)(2,1)}, bf16[1,1024,768]{2,1,0:T(8,128)(2,1)}, u32[]{:S(2)}, u32[]{:S(2)}) collective-permute-start(bf16[1,1024,768]{2,1,0:T(8,128)(2,1)} %fusion.24), channel_id=1, source_target_pairs={{0,2},{1,3},{2,0},{3,1},{4,6},{5,7},{6,4},{7,5},{8,10},{9,11},{10,... | collective-permute-start | bytes 4718600 | tf_op jit(solution)/shard_map/ppermute | solution.py:34
  262.4 38.4 %collective-permute-start.20 = (bf16[2,256,896]{2,1,0:T(8,128)(2,1)}, bf16[2,256,896]{2,1,0:T(8,128)(2,1)}, u32[]{:S(2)}, u32[]{:S(2)}) collective-permute-start(bf16[2,256,896]{2,1,0:T(8,128)(2,1)} %collective-permute-done.16.refs_6_.refs_11_), channel_id=1, source_target_pairs={{0,8},{8,16},{16,24},{24,28},{28,20},{20,12},{12,4},{4,0},{1,9},{9... | collective-permute-start | bytes 2752520 | tf_op jit(solution)/shard_map/ppermute | solution.py:63
  263.6 37.2 %collective-permute-start.21 = (bf16[2,256,896]{2,1,0:T(8,128)(2,1)}, bf16[2,256,896]{2,1,0:T(8,128)(2,1)}, u32[]{:S(2)}, u32[]{:S(2)}) collective-permute-start(bf16[2,256,896]{2,1,0:T(8,128)(2,1)} %collective-permute-done.17.refs_7_.refs_12_), channel_id=1, source_target_pairs={{8,0},{16,8},{24,16},{28,24},{20,28},{12,20},{4,12},{0,4},{9,1},{1... | collective-permute-start | bytes 2752520 | tf_op jit(solution)/shard_map/ppermute | solution.py:63
  300.8 39.5 %collective-permute-start.23 = (bf16[2,256,896]{2,1,0:T(8,128)(2,1)}, bf16[2,256,896]{2,1,0:T(8,128)(2,1)S(1)}, u32[]{:S(2)}, u32[]{:S(2)}) collective-permute-start(bf16[2,256,896]{2,1,0:T(8,128)(2,1)} %collective-permute-done.20.refs_8_.refs_13_), channel_id=1, source_target_pairs={{0,8},{8,16},{16,24},{24,28},{28,20},{20,12},{12,4},{4,0},{1,9},{9... | collective-permute-start | bytes 2752520 | tf_op jit(solution)/shard_map/ppermute | solution.py:63
  301.9 38.3 %collective-permute-start.24 = (bf16[2,256,896]{2,1,0:T(8,128)(2,1)}, bf16[2,256,896]{2,1,0:T(8,128)(2,1)S(1)}, u32[]{:S(2)}, u32[]{:S(2)}) collective-permute-start(bf16[2,256,896]{2,1,0:T(8,128)(2,1)} %collective-permute-done.21.refs_9_.refs_14_), channel_id=1, source_target_pairs={{8,0},{16,8},{24,16},{28,24},{20,28},{12,20},{4,12},{0,4},{9,1},{1... | collective-permute-start | bytes 2752520 | tf_op jit(solution)/shard_map/ppermute | solution.py:63
  304.7 35.5 %collective-permute-start.26 = (bf16[2,192,768]{2,1,0:T(8,128)(2,1)}, bf16[2,192,768]{2,1,0:T(8,128)(2,1)}, u32[]{:S(2)}, u32[]{:S(2)}) collective-permute-start(bf16[2,192,768]{2,1,0:T(8,128)(2,1)} %dynamic-slice_bitcast_fusion.3), channel_id=1, source_target_pairs={{0,1},{1,0},{2,3},{3,2},{4,5},{5,4},{6,7},{7,6},{8,9},{9,8},{10,11... | collective-permute-start | bytes 1769480 | tf_op jit(solution)/shard_map/ppermute | solution.py:34
  340.3 22.6 %collective-permute-start.27 = (bf16[1,256,896]{2,1,0:T(8,128)(2,1)S(1)}, bf16[1,256,896]{2,1,0:T(8,128)(2,1)S(1)}, u32[]{:S(2)}, u32[]{:S(2)}) collective-permute-start(bf16[1,256,896]{2,1,0:T(8,128)(2,1)S(1)} %slice.264), channel_id=1, source_target_pairs={{0,8},{8,16},{16,24},{24,28},{28,20},{20,12},{12,4},{4,0},{1,9},{9... | collective-permute-start | bytes 1376264 | tf_op jit(solution)/shard_map/ppermute | solution.py:63
  341.7 21.2 %collective-permute-start.28 = (bf16[1,256,896]{2,1,0:T(8,128)(2,1)S(1)}, bf16[1,256,896]{2,1,0:T(8,128)(2,1)S(1)}, u32[]{:S(2)}, u32[]{:S(2)}) collective-permute-start(bf16[1,256,896]{2,1,0:T(8,128)(2,1)S(1)} %slice.265), channel_id=1, source_target_pairs={{8,0},{16,8},{24,16},{28,24},{20,28},{12,20},{4,12},{0,4},{9,1},{1... | collective-permute-start | bytes 1376264 | tf_op jit(solution)/shard_map/ppermute | solution.py:63
  344.3 18.3 %collective-permute-start.29 = (bf16[512,384]{1,0:T(8,128)(2,1)S(1)}, bf16[512,384]{1,0:T(8,128)(2,1)S(1)}, u32[]{:S(2)}, u32[]{:S(2)}) collective-permute-start(bf16[512,384]{1,0:T(8,128)(2,1)S(1)} %constant_dynamic-slice_fusion.19), channel_id=1, source_target_pairs={{0,4},{4,0},{8,12},{12,8},{16,20},{20,16},{24,28},{28,24},{1,5},{5... | collective-permute-start | bytes 1179656 | tf_op jit(solution)/shard_map/ppermute | solution.py:34
  344.8 17.9 %collective-permute-start.30 = (bf16[512,384]{1,0:T(8,128)(2,1)S(1)}, bf16[512,384]{1,0:T(8,128)(2,1)S(1)}, u32[]{:S(2)}, u32[]{:S(2)}) collective-permute-start(bf16[512,384]{1,0:T(8,128)(2,1)S(1)} %constant_dynamic-slice_fusion.18), channel_id=1, source_target_pairs={{0,8},{4,12},{8,0},{12,4},{16,24},{20,28},{24,16},{28,20},{1,9},{5... | collective-permute-start | bytes 1179656 | tf_op jit(solution)/shard_map/ppermute | solution.py:34
  349.2 33.9 %collective-permute-start.33 = (bf16[1,960,768]{2,1,0:T(8,128)(2,1)S(1)}, bf16[1,960,768]{2,1,0:T(8,128)(2,1)S(1)}, u32[]{:S(2)}, u32[]{:S(2)}) collective-permute-start(bf16[1,960,768]{2,1,0:T(8,128)(2,1)S(1)} %constant_dynamic-slice_fusion.15), channel_id=1, source_target_pairs={{0,2},{1,3},{2,0},{3,1},{4,6},{5,7},{6,4},{7,5},{8,10},{9,11},{10,... | collective-permute-start | bytes 4423688 | tf_op jit(solution)/shard_map/ppermute | solution.py:34
  362.9 10.8 %collective-permute-start.31 = (bf16[256,384]{1,0:T(8,128)(2,1)S(1)}, bf16[256,384]{1,0:T(8,128)(2,1)S(1)}, u32[]{:S(2)}, u32[]{:S(2)}) collective-permute-start(bf16[256,384]{1,0:T(8,128)(2,1)S(1)} %constant_dynamic-slice_fusion.17), channel_id=1, source_target_pairs={{0,8},{4,12},{8,0},{12,4},{16,24},{20,28},{24,16},{28,20},{1,9},{5... | collective-permute-start | bytes 589832 | tf_op jit(solution)/shard_map/ppermute | solution.py:34
  364.3 9.5 %collective-permute-start.32 = (bf16[256,384]{1,0:T(8,128)(2,1)S(1)}, bf16[256,384]{1,0:T(8,128)(2,1)S(1)}, u32[]{:S(2)}, u32[]{:S(2)}) collective-permute-start(bf16[256,384]{1,0:T(8,128)(2,1)S(1)} %constant_dynamic-slice_fusion.16), channel_id=1, source_target_pairs={{0,4},{4,0},{8,12},{12,8},{16,20},{20,16},{24,28},{28,24},{1,5},{5... | collective-permute-start | bytes 589832 | tf_op jit(solution)/shard_map/ppermute | solution.py:34
  392.2 12.5 %collective-permute-start.34 = (bf16[2,448,768]{2,1,0:T(8,128)(2,1)}, bf16[2,448,768]{2,1,0:T(8,128)(2,1)}, u32[]{:S(2)}, u32[]{:S(2)}) collective-permute-start(bf16[2,448,768]{2,1,0:T(8,128)(2,1)} %dynamic-slice_bitcast_fusion.2), channel_id=1, source_target_pairs={{0,1},{1,0},{2,3},{3,2},{4,5},{5,4},{6,7},{7,6},{8,9},{9,8},{10,11... | collective-permute-start | bytes 4128776 | tf_op jit(solution)/shard_map/ppermute | solution.py:34
  392.2 10.7 %collective-permute-start.35 = (bf16[128,384]{1,0:T(8,128)(2,1)S(1)}, bf16[128,384]{1,0:T(8,128)(2,1)S(1)}, u32[]{:S(2)}, u32[]{:S(2)}) collective-permute-start(bf16[128,384]{1,0:T(8,128)(2,1)S(1)} %constant_dynamic-slice_fusion.14), channel_id=1, source_target_pairs={{0,16},{4,20},{8,24},{12,28},{16,0},{20,4},{24,8},{28,12},{1,17},{... | collective-permute-start | bytes 294920 | tf_op jit(solution)/shard_map/ppermute | solution.py:34
  394.1 10.7 %collective-permute-start.36 = (bf16[128,384]{1,0:T(8,128)(2,1)S(1)}, bf16[128,384]{1,0:T(8,128)(2,1)S(1)}, u32[]{:S(2)}, u32[]{:S(2)}) collective-permute-start(bf16[128,384]{1,0:T(8,128)(2,1)S(1)} %constant_dynamic-slice_fusion.13), channel_id=1, source_target_pairs={{0,16},{4,20},{8,24},{12,28},{16,0},{20,4},{24,8},{28,12},{1,17},{... | collective-permute-start | bytes 294920 | tf_op jit(solution)/shard_map/ppermute | solution.py:34
  406.9 20.2 %collective-permute-start.37 = (bf16[1,448,768]{2,1,0:T(8,128)(2,1)S(1)}, bf16[1,448,768]{2,1,0:T(8,128)(2,1)S(1)}, u32[]{:S(2)}, u32[]{:S(2)}) collective-permute-start(bf16[1,448,768]{2,1,0:T(8,128)(2,1)S(1)} %constant_dynamic-slice_fusion.12), channel_id=1, source_target_pairs={{0,2},{1,3},{2,0},{3,1},{4,6},{5,7},{6,4},{7,5},{8,10},{9,11},{10,... | collective-permute-start | bytes 2064392 | tf_op jit(solution)/shard_map/ppermute | solution.py:34
  408.7 11.5 %collective-permute-start.39 = (bf16[128,384]{1,0:T(8,128)(2,1)S(1)}, bf16[128,384]{1,0:T(8,128)(2,1)S(1)}, u32[]{:S(2)}, u32[]{:S(2)}) collective-permute-start(bf16[128,384]{1,0:T(8,128)(2,1)S(1)} %add_convert_fusion.16), channel_id=1, source_target_pairs={{0,16},{4,20},{8,24},{12,28},{16,0},{20,4},{24,8},{28,12},{1,17},{... | collective-permute-start | bytes 294920 | tf_op jit(solution)/shard_map/ppermute | solution.py:34
  411.8 9.7 %collective-permute-start.40 = (bf16[480,384]{1,0:T(8,128)(2,1)S(1)}, bf16[480,384]{1,0:T(8,128)(2,1)S(1)}, u32[]{:S(2)}, u32[]{:S(2)}) collective-permute-start(bf16[480,384]{1,0:T(8,128)(2,1)S(1)} %constant_dynamic-slice_fusion.11), channel_id=1, source_target_pairs={{0,4},{4,0},{8,12},{12,8},{16,20},{20,16},{24,28},{28,24},{1,5},{5... | collective-permute-start | bytes 1105928 | tf_op jit(solution)/shard_map/ppermute | solution.py:34
  413.7 13.3 %collective-permute-start.41 = (bf16[480,384]{1,0:T(8,128)(2,1)S(1)}, bf16[480,384]{1,0:T(8,128)(2,1)S(1)}, u32[]{:S(2)}, u32[]{:S(2)}) collective-permute-start(bf16[480,384]{1,0:T(8,128)(2,1)S(1)} %constant_dynamic-slice_fusion.10), channel_id=1, source_target_pairs={{0,8},{4,12},{8,0},{12,4},{16,24},{20,28},{24,16},{28,20},{1,9},{5... | collective-permute-start | bytes 1105928 | tf_op jit(solution)/shard_map/ppermute | solution.py:34
  427.3 19.3 %collective-permute-start.42 = (bf16[256,384]{1,0:T(8,128)(2,1)S(1)}, bf16[256,384]{1,0:T(8,128)(2,1)S(1)}, u32[]{:S(2)}, u32[]{:S(2)}) collective-permute-start(bf16[256,384]{1,0:T(8,128)(2,1)S(1)} %get-tuple-element.208), channel_id=1, source_target_pairs={{0,8},{4,12},{8,0},{12,4},{16,24},{20,28},{24,16},{28,20},{1,9},{5... | collective-permute-start | bytes 589832 | tf_op jit(solution)/shard_map/ppermute | solution.py:34
  427.4 19.4 %collective-permute-start.43 = (bf16[256,384]{1,0:T(8,128)(2,1)S(1)}, bf16[256,384]{1,0:T(8,128)(2,1)S(1)}, u32[]{:S(2)}, u32[]{:S(2)}) collective-permute-start(bf16[256,384]{1,0:T(8,128)(2,1)S(1)} %get-tuple-element.209), channel_id=1, source_target_pairs={{0,4},{4,0},{8,12},{12,8},{16,20},{20,16},{24,28},{28,24},{1,5},{5... | collective-permute-start | bytes 589832 | tf_op jit(solution)/shard_map/ppermute | solution.py:34
  428.0 18.5 %collective-permute-start.44 = (bf16[240,384]{1,0:T(8,128)(2,1)S(1)}, bf16[240,384]{1,0:T(8,128)(2,1)S(1)}, u32[]{:S(2)}, u32[]{:S(2)}) collective-permute-start(bf16[240,384]{1,0:T(8,128)(2,1)S(1)} %constant_dynamic-slice_fusion.9), channel_id=1, source_target_pairs={{0,8},{4,12},{8,0},{12,4},{16,24},{20,28},{24,16},{28,20},{1,9},{5... | collective-permute-start | bytes 552968 | tf_op jit(solution)/shard_map/ppermute | solution.py:34
  431.7 14.9 %collective-permute-start.45 = (bf16[240,384]{1,0:T(8,128)(2,1)S(1)}, bf16[240,384]{1,0:T(8,128)(2,1)S(1)}, u32[]{:S(2)}, u32[]{:S(2)}) collective-permute-start(bf16[240,384]{1,0:T(8,128)(2,1)S(1)} %constant_dynamic-slice_fusion.8), channel_id=1, source_target_pairs={{0,4},{4,0},{8,12},{12,8},{16,20},{20,16},{24,28},{28,24},{1,5},{5... | collective-permute-start | bytes 552968 | tf_op jit(solution)/shard_map/ppermute | solution.py:34
  446.9 16.4 %collective-permute-start.48 = (bf16[512,384]{1,0:T(8,128)(2,1)S(1)}, bf16[512,384]{1,0:T(8,128)(2,1)S(1)}, u32[]{:S(2)}, u32[]{:S(2)}) collective-permute-start(bf16[512,384]{1,0:T(8,128)(2,1)S(1)} %pad_maximum_fusion.24), channel_id=1, source_target_pairs={{0,4},{4,0},{8,12},{12,8},{16,20},{20,16},{24,28},{28,24},{1,5},{5... | collective-permute-start | bytes 1179656 | tf_op jit(solution)/shard_map/ppermute | solution.py:34
  446.9 16.5 %collective-permute-start.49 = (bf16[512,384]{1,0:T(8,128)(2,1)S(1)}, bf16[512,384]{1,0:T(8,128)(2,1)S(1)}, u32[]{:S(2)}, u32[]{:S(2)}) collective-permute-start(bf16[512,384]{1,0:T(8,128)(2,1)S(1)} %pad_maximum_fusion.25), channel_id=1, source_target_pairs={{0,8},{4,12},{8,0},{12,4},{16,24},{20,28},{24,16},{28,20},{1,9},{5... | collective-permute-start | bytes 1179656 | tf_op jit(solution)/shard_map/ppermute | solution.py:34
  448.4 14.7 %collective-permute-start.50 = (bf16[120,384]{1,0:T(8,128)(2,1)S(1)}, bf16[120,384]{1,0:T(8,128)(2,1)S(1)}, u32[]{:S(2)}, u32[]{:S(2)}) collective-permute-start(bf16[120,384]{1,0:T(8,128)(2,1)S(1)} %constant_dynamic-slice_fusion.5), channel_id=1, source_target_pairs={{0,16},{4,20},{8,24},{12,28},{16,0},{20,4},{24,8},{28,12},{1,17},{... | collective-permute-start | bytes 276488 | tf_op jit(solution)/shard_map/ppermute | solution.py:34
  448.7 14.5 %collective-permute-start.51 = (bf16[120,384]{1,0:T(8,128)(2,1)S(1)}, bf16[120,384]{1,0:T(8,128)(2,1)S(1)}, u32[]{:S(2)}, u32[]{:S(2)}) collective-permute-start(bf16[120,384]{1,0:T(8,128)(2,1)S(1)} %constant_dynamic-slice_fusion.4), channel_id=1, source_target_pairs={{0,16},{4,20},{8,24},{12,28},{16,0},{20,4},{24,8},{28,12},{1,17},{... | collective-permute-start | bytes 276488 | tf_op jit(solution)/shard_map/ppermute | solution.py:34
  463.6 12.4 %collective-permute-start.54 = (bf16[120,384]{1,0:T(8,128)(2,1)S(1)}, bf16[120,384]{1,0:T(8,128)(2,1)S(1)}, u32[]{:S(2)}, u32[]{:S(2)}) collective-permute-start(bf16[120,384]{1,0:T(8,128)(2,1)S(1)} %add_convert_fusion.19), channel_id=1, source_target_pairs={{0,16},{4,20},{8,24},{12,28},{16,0},{20,4},{24,8},{28,12},{1,17},{... | collective-permute-start | bytes 276488 | tf_op jit(solution)/shard_map/ppermute | solution.py:34
  465.9 10.2 %collective-permute-start.55 = (bf16[120,384]{1,0:T(8,128)(2,1)S(1)}, bf16[120,384]{1,0:T(8,128)(2,1)S(1)}, u32[]{:S(2)}, u32[]{:S(2)}) collective-permute-start(bf16[120,384]{1,0:T(8,128)(2,1)S(1)} %add_convert_fusion.18), channel_id=1, source_target_pairs={{0,16},{4,20},{8,24},{12,28},{16,0},{20,4},{24,8},{28,12},{1,17},{... | collective-permute-start | bytes 276488 | tf_op jit(solution)/shard_map/ppermute | solution.py:34
  (94 other events, 751.3 us)
